TPU v7x, 256 devices: a whole 4x4x8 slice. The times are simulated.
256 devices in a mesh: seq: 64 (over x, z, y_hi), tp: 4 (over y_lo, core).
Axes of the slice: x: 4, y: 4 (y_hi: 2, y_lo: 2; y = y_hi * 2 + y_lo), z: 8, core: 2. Of those that a mesh axis runs over, the one named last changes fastest.
Arguments:
- video: bfloat16 [128, 256, 1408], P('seq'), may hold values from -16 to 16
- spatial_norm_gain: float32 [1408], replicated, may hold values from 0.5 to 1.5
- spatial_query_key_value: bfloat16 [1408, 3, 1408], P(None, None, 'tp'), may hold values from -1.5 to 1.5
- spatial_output_weight: bfloat16 [1408, 1408], P('tp'), may hold values from -0.15625 to 0.15625
- temporal_norm_gain: float32 [1408], replicated, may hold values from 0.1 to 1.9
- temporal_query_key_value: bfloat16 [1408, 3, 1408], P(None, None, 'tp'), may hold values from -1.5 to 1.5
- temporal_output_weight: bfloat16 [1408, 1408], P('tp'), may hold values from -0.15625 to 0.15625
- closing_norm_gain: float32 [1408], replicated, may hold values from 0.5 to 1.5
- scoring_hidden_weight: bfloat16 [1408, 1408], P(None, 'tp'), may hold values from -0.15625 to 0.15625
- adapter_down_weight: bfloat16 [8, 1408, 16], replicated, may hold values from -0.15625 to 0.15625
- adapter_up_weight: bfloat16 [8, 16, 1408], P(None, None, 'tp'), may hold values from -1.5 to 1.5
- scoring_vector: bfloat16 [1408], P('tp'), may hold values from -0.15625 to 0.15625
- policy: int32 [1], replicated, may hold values from 0 to 7
- valid_frame_count: int32 [1], replicated, may hold values from 64 to 128
Outputs:
- blended: bfloat16 [128, 256, 1408], P('seq')
- reward: float32 [128], P('seq')
All inputs are finite; a program needn't handle non-finite values.
Results may differ from a plain program's by a relative error of at most 0.035.
Values may be sent and summed in bfloat16 or wider, within the bound.
No kernel may reach another device: no remote copies, remote signals or barrier semaphores. Data moves between devices by JAX's collectives and lax.ppermute only.
A program may use at most 64 MiB of HBM per device.

v0:
```python
import jax
import jax.numpy as jnp
from jax import lax
from jax.sharding import PartitionSpec as P

HEAD_DIM = 88


adapter_scale = 2.0


def normalize(values, gain):
    values = values.astype(jnp.float32)
    average = jnp.mean(values, axis=-1, keepdims=True)
    centered = values - average
    spread = jnp.mean(centered * centered, axis=-1, keepdims=True)
    return centered * lax.rsqrt(spread + 1e-05) * gain


def attend(queries, keys, values, visible, score_form, mix_form):
    scores = jnp.einsum(
        score_form, queries, keys, preferred_element_type=jnp.float32
    ) * queries.shape[-1] ** (-0.5)
    scores = jnp.where(visible, scores, -jnp.inf)
    highest = jnp.max(scores, axis=-1, keepdims=True)
    weights = jnp.exp(scores - highest)
    weights = (weights / jnp.sum(weights, axis=-1, keepdims=True)).astype(jnp.bfloat16)
    return jnp.einsum(mix_form, weights, values, preferred_element_type=jnp.float32).astype(
        jnp.bfloat16
    )


def shards(
    video,
    spatial_norm_gain,
    spatial_query_key_value,
    spatial_output_weight,
    temporal_norm_gain,
    temporal_query_key_value,
    temporal_output_weight,
    closing_norm_gain,
    scoring_hidden_weight,
    adapter_down_weight,
    adapter_up_weight,
    scoring_vector,
    policy,
    valid_frame_count,
):
    frames_here, patches, width = video.shape
    local_width = spatial_output_weight.shape[0]
    heads_here = local_width // HEAD_DIM
    rows = frames_here * patches
    tokens_flat = video.reshape(rows, width)
    normed = normalize(tokens_flat, spatial_norm_gain).astype(jnp.bfloat16)
    packed = jnp.dot(
        normed,
        spatial_query_key_value.reshape(width, 3 * local_width),
        preferred_element_type=jnp.float32,
    ).astype(jnp.bfloat16)
    packed = packed.reshape(frames_here, patches, 3, heads_here, HEAD_DIM)
    everywhere = jnp.ones((patches,), jnp.bool_)
    spatial = attend(
        packed[:, :, 0],
        packed[:, :, 1],
        packed[:, :, 2],
        everywhere,
        "blhe,bmhe->bhlm",
        "bhlm,bmhe->blhe",
    )
    space_partial = jnp.dot(
        spatial.reshape(rows, local_width),
        spatial_output_weight,
        preferred_element_type=jnp.float32,
    )
    frame_total = frames_here * lax.axis_size("seq")
    visible = jnp.arange(frame_total) < valid_frame_count[0]
    space_total = lax.psum(space_partial.astype(jnp.bfloat16), "tp").astype(jnp.float32)
    stream = (
        (tokens_flat.astype(jnp.float32) + space_total)
        .astype(jnp.bfloat16)
        .reshape(frames_here, patches, width)
    )
    moved = lax.all_to_all(stream, "seq", split_axis=1, concat_axis=0, tiled=True)
    moved_flat = moved.reshape(moved.shape[0] * moved.shape[1], width)
    frames_in = moved.shape[0]
    positions = moved.shape[1]
    normed_time = normalize(moved_flat, temporal_norm_gain).astype(jnp.bfloat16)
    packed_time = jnp.dot(
        normed_time,
        temporal_query_key_value.reshape(width, 3 * local_width),
        preferred_element_type=jnp.float32,
    ).astype(jnp.bfloat16)
    packed_time = packed_time.reshape(frames_in, positions, 3, heads_here, HEAD_DIM)
    mixed = attend(
        packed_time[:, :, 0],
        packed_time[:, :, 1],
        packed_time[:, :, 2],
        visible,
        "lbhe,mbhe->bhlm",
        "bhlm,mbhe->lbhe",
    )
    time_partial = jnp.dot(
        mixed.reshape(frames_in * positions, local_width),
        temporal_output_weight,
        preferred_element_type=jnp.float32,
    )
    time_total = lax.psum(time_partial.astype(jnp.bfloat16), "tp").astype(jnp.float32)
    updated = (
        (moved_flat.astype(jnp.float32) + time_total).astype(jnp.bfloat16).reshape(moved.shape)
    )
    blended = lax.all_to_all(updated, "seq", split_axis=0, concat_axis=1, tiled=True)
    pooled_features = jnp.mean(normalize(blended, closing_norm_gain), axis=1).astype(jnp.bfloat16)
    selected_policy = policy[0]
    selected_down_map = lax.dynamic_index_in_dim(
        adapter_down_weight, selected_policy, 0, keepdims=False
    )
    selected_up_map = lax.dynamic_index_in_dim(
        adapter_up_weight, selected_policy, 0, keepdims=False
    )
    adapter_correction = jnp.dot(
        pooled_features, selected_down_map, preferred_element_type=jnp.float32
    ).astype(jnp.bfloat16)
    hidden_features = jnp.dot(
        pooled_features, scoring_hidden_weight, preferred_element_type=jnp.float32
    ) + adapter_scale * jnp.dot(
        adapter_correction, selected_up_map, preferred_element_type=jnp.float32
    )
    activated = jax.nn.gelu(hidden_features, approximate=True)
    partial_score = jnp.sum(activated * scoring_vector.astype(jnp.float32), axis=-1)
    score = lax.psum(partial_score, "tp")
    frame_index = lax.axis_index("seq") * frames_here + jnp.arange(frames_here)
    reward = jnp.where(frame_index < valid_frame_count[0], score, jnp.float32(0.0))
    return (blended, reward)


def solution(mesh):
    in_specs = (
        P("seq", None, None),
        P(),
        P(None, None, "tp"),
        P("tp", None),
        P(),
        P(None, None, "tp"),
        P("tp", None),
        P(),
        P(None, "tp"),
        P(),
        P(None, None, "tp"),
        P("tp"),
        P(),
        P(),
    )
    out_specs = (P("seq", None, None), P("seq"))
    return jax.shard_map(shards, mesh=mesh, in_specs=in_specs, out_specs=out_specs, check_vma=False)
```

profile of v0, /device:TPU:1, one launch (start us, length us, event | category | flops | bytes accessed | tf_op | source)
XLA Modules:
  0.0 317.7 jit_solution(4080617696681233609)
XLA Ops:
  10.2 2.9 convolution_convert_fusion.3
  13.1 3.4 %reshape.150 = bf16[2,256,3,4,88]{1,0,4,3,2:T(2,128)(2,1)} reshape(bf16[512,1056]{0,1:T(8,128)(2,1)} %convolution_convert_fusion.3) | data formatting | bytes 2162688 | tf_op jit(solution)/shard_map/reshape | solution.py:60
  16.5 2.8 fusion.50
  19.3 3.3 %fusion.51 = (f32[2,4,256]{2,1,0:T(4,128)S(1)}, f32[2,4,256,256]{2,3,1,0:T(8,128)}) fusion(bf16[2,256,1,4,88]{1,0,4,3,2:T(2,128)(2,1)} %get-tuple-element.7, bf16[2,256,1,4,88]{1,0,4,3,2:T(2,128)(2,1)} %get-tuple-element.6), kind=kOutput, calls=%fused_computation.81 | convolution fusion | flops 93847808 | bytes 2826240 | tf_op jit(solution)/shard_map/sub | solution.py:26
  27.2 56.2 %all-reduce.3.cloned.1.call-done = bf16[512,1408]{1,0:T(8,128)(2,1)} async-done(((bf16[512,1408]{1,0:T(8,128)(2,1)}), bf16[512,1408]{1,0:T(8,128)(2,1)}) %all-reduce.3.cloned.1.call-update) | async-done | bytes 1441808 | tf_op jit(solution)/shard_map/psum | solution.py:77
  83.4 2.1 fusion.7
  85.5 2.6 copy.44
  88.1 12.5 %all-to-all-start = ((bf16[2,256,1408]{2,0,1:T(2,128)(2,1)}), bf16[2,256,1408]{2,0,1:T(2,128)(2,1)}, u32[]{:S(2)}, u32[]{:S(2)}) async-start(bf16[2,256,1408]{2,0,1:T(2,128)(2,1)} %copy.44), calls=%async_computation | async-start | bytes 2883584 | tf_op jit(solution)/shard_map/all_to_all | solution.py:83
  101.5 36.2 %all-to-all-done = bf16[2,256,1408]{2,0,1:T(2,128)(2,1)} async-done(((bf16[2,256,1408]{2,0,1:T(2,128)(2,1)}), bf16[2,256,1408]{2,0,1:T(2,128)(2,1)}, u32[]{:S(2)}, u32[]{:S(2)}) %all-to-all-start) | async-done | bytes 1441824 | tf_op jit(solution)/shard_map/all_to_all | solution.py:83
  137.7 2.4 bitcast_convert_fusion
  143.9 3.5 %convert_element_type.119 = bf16[512,1408]{1,0:T(8,128)(2,1)} reshape(bf16[64,2,4,1408]{3,2,1,0:T(4,128)(2,1)} %multiply_convert_fusion) | data formatting | bytes 2883584 | tf_op jit(solution)/shard_map/convert_element_type | solution.py:87
  147.4 5.1 %convolution_convert_fusion.1 = bf16[512,1056]{0,1:T(8,128)(2,1)} fusion(bf16[512,1408]{1,0:T(8,128)(2,1)} %convert_element_type.119, bf16[1408,1056]{0,1:T(8,128)(2,1)} %bitcast.114), kind=kOutput, calls=%fused_computation.7 | convolution fusion | flops 1523073024 | bytes 5496832 | tf_op jit(solution)/shard_map/dot_general | solution.py:88
  152.5 2.4 copy.46
  154.9 4.5 %reshape.154 = bf16[128,4,3,4,88]{4,3,2,1,0:T(4,128)(2,1)} reshape(bf16[512,1056]{1,0:T(8,128)(2,1)} %copy.46) | data formatting | bytes 2162688 | tf_op jit(solution)/shard_map/reshape | solution.py:93
  159.3 2.9 fusion.49
  162.2 2.2 copy.59
  164.4 2.2 copy.60
  166.6 2.4 fusion.11
  171.8 2.9 fusion.12
  177.2 3.4 %convolution_convert_fusion = bf16[512,1408]{1,0:T(8,128)(2,1)} fusion(bf16[512,352]{1,0:T(8,128)(2,1)} %reshape.155, bf16[352,1408]{1,0:T(8,128)(2,1)} %param.20), kind=kOutput, calls=%fused_computation.6 | convolution fusion | flops 508231680 | bytes 2793472 | tf_op jit(solution)/shard_map/dot_general | solution.py:102
  180.6 4.2 %copy.98 = f32[2,64,4,1408]{3,2,0,1:T(4,128)} copy(f32[2,64,4,1408]{3,0,2,1:T(2,128)} %copy-done.1) | data formatting | bytes 5767168 | tf_op jit(solution)/shard_map/convert_element_type | solution.py:109
  184.8 4.4 %reshape.158 = f32[512,1408]{1,0:T(8,128)} reshape(f32[64,2,4,1408]{3,2,1,0:T(4,128)} %bitcast.109) | data formatting | bytes 5767168 | tf_op jit(solution)/shard_map/convert_element_type | solution.py:109
  189.2 40.1 %all-reduce.5.cloned.1.call-done = bf16[512,1408]{1,0:T(8,128)(2,1)} async-done(((bf16[512,1408]{1,0:T(8,128)(2,1)}), bf16[512,1408]{1,0:T(8,128)(2,1)}) %all-reduce.5.cloned.1.call-update) | async-done | bytes 1441808 | tf_op jit(solution)/shard_map/psum | solution.py:107
  229.4 3.6 %add_convert_fusion = bf16[512,1408]{1,0:T(8,128)(2,1)} fusion(f32[512,1408]{1,0:T(8,128)} %reshape.158, bf16[512,1408]{1,0:T(8,128)(2,1)} %all-reduce.5.cloned.1.call-done), kind=kLoop, calls=%fused_computation.16 | loop fusion | flops 2162688 | bytes 5767168 | tf_op jit(solution)/shard_map/convert_element_type | solution.py:109
  232.9 3.7 %reshape.156 = bf16[128,4,1408]{2,1,0:T(4,128)(2,1)} reshape(bf16[512,1408]{1,0:T(8,128)(2,1)} %add_convert_fusion) | data formatting | bytes 2883584 | tf_op jit(solution)/shard_map/reshape | solution.py:109
  236.6 12.9 %all-to-all-start.1 = ((bf16[128,4,1408]{2,1,0:T(4,128)(2,1)}), bf16[128,4,1408]{2,1,0:T(4,128)(2,1)}, u32[]{:S(2)}, u32[]{:S(2)}) async-start(bf16[128,4,1408]{2,1,0:T(4,128)(2,1)} %reshape.156), calls=%async_computation.1 | async-start | bytes 2883584 | tf_op jit(solution)/shard_map/all_to_all | solution.py:111
  250.2 36.1 %all-to-all-done.1 = bf16[128,4,1408]{2,1,0:T(4,128)(2,1)} async-done(((bf16[128,4,1408]{2,1,0:T(4,128)(2,1)}), bf16[128,4,1408]{2,1,0:T(4,128)(2,1)}, u32[]{:S(2)}, u32[]{:S(2)}) %all-to-all-start.1) | async-done | bytes 1441824 | tf_op jit(solution)/shard_map/all_to_all | solution.py:111
  288.3 2.5 fusion.4
  290.8 2.4 fusion.6
  296.0 7.9 %psum.23 = f32[2]{0:T(128)S(1)} all-reduce(f32[2]{0:T(128)S(1)} %fusion.38), channel_id=1, replica_groups=mesh['seq'=64,'tp'=4] {'tp'}, use_global_device_ids=true, to_apply=%region_14.15 | all-reduce | flops 2 | bytes 16 | tf_op jit(solution)/shard_map/psum | solution.py:130
  303.9 3.0 copy_bitcast_fusion.1
  306.8 3.5 %all_to_all.24 = bf16[2,256,1408]{2,1,0:T(8,128)(2,1)} reshape(bf16[2,64,4,1408]{3,2,1,0:T(4,128)(2,1)} %copy_bitcast_fusion.1) | data formatting | bytes 2883584 | tf_op jit(solution)/shard_map/all_to_all | solution.py:111
  (46 shorter events, 22.2 us)
Async XLA Ops:
  7.2 3.1 copy-start
  7.2 76.2 %all-reduce.3.cloned.1.call-start = ((), (), s32[]{:S(2)}) async-start(), calls=%async_computation.2 | async-start | bytes 2883584 | tf_op jit(solution)/shard_map/psum | solution.py:77
  7.2 1.9 copy-start.2
  7.2 2.5 copy-start.4
  22.6 2.5 copy-start.3
  88.1 49.6 %all-to-all-start = ((bf16[2,256,1408]{2,0,1:T(2,128)(2,1)}), bf16[2,256,1408]{2,0,1:T(2,128)(2,1)}, u32[]{:S(2)}, u32[]{:S(2)}) async-start(bf16[2,256,1408]{2,0,1:T(2,128)(2,1)} %copy.44), calls=%async_computation | async-start | bytes 2883584 | tf_op jit(solution)/shard_map/all_to_all | solution.py:83
  100.7 128.7 %all-reduce.5.cloned.1.call-start = ((), (), s32[]{:S(2)}) async-start(), calls=%async_computation.3 | async-start | bytes 2883584 | tf_op jit(solution)/shard_map/psum | solution.py:107
  140.1 1.8 copy-start.1
  140.8 1.1 copy-start.5
  236.6 13.6 %copy-start.7 = (bf16[352]{0:T(512)(128)(2,1)S(1)}, bf16[352]{0:T(512)(128)(2,1)}, u32[]{:S(2)}) copy-start(bf16[352]{0:T(512)(128)(2,1)} %param.25) | copy-start | bytes 2116
  236.6 49.7 %all-to-all-start.1 = ((bf16[128,4,1408]{2,1,0:T(4,128)(2,1)}), bf16[128,4,1408]{2,1,0:T(4,128)(2,1)}, u32[]{:S(2)}, u32[]{:S(2)}) async-start(bf16[128,4,1408]{2,1,0:T(4,128)(2,1)} %reshape.156), calls=%async_computation.1 | async-start | bytes 2883584 | tf_op jit(solution)/shard_map/all_to_all | solution.py:111
  249.5 41.3 %copy-start.6 = (f32[1408]{0:T(1024)S(1)}, f32[1408]{0:T(1024)}, u32[]{:S(2)}) copy-start(f32[1408]{0:T(1024)} %param.21) | copy-start | bytes 16900
Sparse Core Ops, SparseCore 0:
  27.3 56.0 all-reduce.2
  180.7 48.5 all-reduce.4
where the time goes:
time: 319 us; the launch traced here: 318 us
  waiting for transfers between devices  169 us (53%)
  local copies, waits for them, and re-layouts  49.5 us (16%)
  matrix products  28.4 us (9%)
  starting transfers between devices  25.7 us (8%)
  other arithmetic  22 us (7%)
  between operations  15.6 us (5%)
  blocking collectives  7.86 us (2%)
    psum x1, waiting for transfers between devices, shards(): lax.psum(space_partial.astype(jnp.bfloat16), 'tp').astype(jnp.float32)  56.2 us
    psum x1, waiting for transfers between devices, shards(): lax.psum(time_partial.astype(jnp.bfloat16), 'tp').astype(jnp.float32)  40.1 us
    all_to_all x1, waiting for transfers between devices, shards(): lax.all_to_all(stream, 'seq', split_axis=1, concat_axis=0, tiled=True)  36.2 us
    all_to_all x1, waiting for transfers between devices, shards(): lax.all_to_all(updated, 'seq', split_axis=0, concat_axis=1, tiled=True)  36.1 us
    all_to_all x1, starting transfers between devices, shards(): lax.all_to_all(updated, 'seq', split_axis=0, concat_axis=1, tiled=True)  12.9 us
    all_to_all x1, starting transfers between devices, shards(): lax.all_to_all(stream, 'seq', split_axis=1, concat_axis=0, tiled=True)  12.5 us
    convert_element_type x2, local copies, waits for them, and re-layouts, shards(): moved_flat.astype(jnp.float32) + time_total  8.6 us
    psum x1, blocking collectives, shards(): score = lax.psum(partial_score, 'tp')  7.86 us
  transfers between devices with their start and end apart: 4, of which 4 were waited for; matrix products, arithmetic and copies ran while one was open for 3% of the time, Pallas kernels for 0%

commit v1 on v0

v1 whole, which is shorter than its diff:
```python
import jax
import jax.numpy as jnp
from jax import lax
from jax.experimental import pallas as pl
from jax.experimental.pallas import tpu as pltpu
from jax.sharding import PartitionSpec as P

HEAD_DIM = 88
SCALE = HEAD_DIM ** (-0.5)
LANES = 128
ADAPTER_SCALE = 2.0
F32 = jnp.float32
BF16 = jnp.bfloat16
VMEM_LIMIT = 48 * 1024 * 1024


def dot_nn(a, b):
    return lax.dot_general(a, b, (((1,), (0,)), ((), ())), preferred_element_type=F32)


def dot_nt(a, b):
    return lax.dot_general(a, b, (((1,), (1,)), ((), ())), preferred_element_type=F32)


def normalize(values, gain):
    average = jnp.mean(values, axis=-1, keepdims=True)
    centered = values - average
    spread = jnp.mean(centered * centered, axis=-1, keepdims=True)
    return centered * lax.rsqrt(spread + 1e-05) * gain


def project_qkv(normed, w_ref, width):
    queries_t = dot_nt(w_ref[0:width], normed)
    keys = dot_nt(normed, w_ref[width : 2 * width]).astype(BF16)
    values_t = dot_nt(w_ref[2 * width : 3 * width], normed)
    return queries_t, keys, values_t


def attend_t(queries_t, keys, values_t, hidden_keys):
    width = queries_t.shape[0]
    outs = []
    for h in range(width // HEAD_DIM):
        first, last = h * HEAD_DIM, (h + 1) * HEAD_DIM
        low = first // LANES * LANES
        high = min(width, -(-last // LANES) * LANES)
        window = queries_t[low:high]
        row = lax.broadcasted_iota(jnp.int32, window.shape, 0) + low
        window = jnp.where((row >= first) & (row < last), window, 0.0).astype(BF16)
        scores = dot_nn(keys[:, low:high], window) * SCALE
        if hidden_keys is not None:
            scores = jnp.where(hidden_keys, -jnp.inf, scores)
        highest = jnp.max(scores, axis=0, keepdims=True)
        weights = jnp.exp(scores - highest)
        total = jnp.sum(weights, axis=0, keepdims=True)
        mixed = dot_nn(values_t[first:last].astype(BF16), weights.astype(BF16))
        outs.append(mixed * (1.0 / total))
    return jnp.transpose(jnp.concatenate(outs, axis=0))


def spatial_kernel(me_ref, x_ref, gain_ref, w_ref, *refs):
    outs, mixed = refs[:4], refs[4]
    frames, patches, model = x_ref.shape
    width = w_ref.shape[0] // 3
    share = patches // 4
    for f in range(frames):
        normed = normalize(x_ref[f].astype(F32), gain_ref[...]).astype(BF16)
        queries_t, keys, values_t = project_qkv(normed, w_ref, width)
        mixed[f] = attend_t(queries_t, keys, values_t, None).astype(BF16)
    me = me_ref[0]
    for d in range(4):
        group = jnp.bitwise_xor(me, d)
        start = pl.multiple_of(group * share, share)
        for f in range(frames):
            outs[d][f * share : (f + 1) * share] = mixed[f, pl.ds(start, share)]


def spatial_call(me, video, gain, weight_t):
    frames, patches, model = video.shape
    width = weight_t.shape[0] // 3
    rows = frames * patches // 4
    return pl.pallas_call(
        spatial_kernel,
        out_shape=[jax.ShapeDtypeStruct((rows, width), BF16)] * 4,
        in_specs=[pl.BlockSpec(memory_space=pltpu.SMEM)]
        + [pl.BlockSpec(memory_space=pltpu.VMEM)] * 3,
        out_specs=[pl.BlockSpec(memory_space=pltpu.VMEM)] * 4,
        scratch_shapes=[pltpu.VMEM((frames, patches, width), BF16)],
        compiler_params=pltpu.CompilerParams(vmem_limit_bytes=VMEM_LIMIT),
        name="spatial_attention",
    )(me, video, gain, weight_t)


def one_hot_rows(rows, source):
    i = lax.broadcasted_iota(jnp.int32, (rows, rows), 0)
    j = lax.broadcasted_iota(jnp.int32, (rows, rows), 1)
    return jnp.where(source(i) == j, 1.0, 0.0).astype(BF16)


def project_out(parts, weights):
    total = None
    for part, weight in zip(parts, weights):
        low = 0
        for w in weight:
            high = low + w.shape[0]
            term = dot_nn(part[:, low:high] if len(weight) > 1 else part[...], w[...])
            total = term if total is None else total + term
            low = high
    return total


def spatial_out_kernel(me_ref, *refs):
    parts = refs[:4]
    w0, w1, w2, w3, video, out = refs[4:]
    share = video.shape[1]
    rows = out.shape[0]
    frames = rows // share
    total = project_out(parts, [(w0,), (w1,), (w2,), (w3,)])
    stream = (video[...].reshape(rows, -1).astype(F32) + total).astype(BF16)
    order = one_hot_rows(rows, lambda i: (i % frames) * share + i // frames)
    out[...] = dot_nn(order, stream).astype(BF16)


def whole(array):
    zeros = (0,) * array.ndim
    return pl.BlockSpec(array.shape, lambda i, s: zeros)


def spatial_out_call(me, parts, weights, video):
    frames, patches, model = video.shape
    share = patches // 4
    rows = frames * share
    arrays = [*parts, *weights]
    return pl.pallas_call(
        spatial_out_kernel,
        out_shape=jax.ShapeDtypeStruct((rows, model), BF16),
        grid_spec=pltpu.PrefetchScalarGridSpec(
            num_scalar_prefetch=1,
            grid=(1,),
            in_specs=[whole(a) for a in arrays]
            + [pl.BlockSpec((frames, share, model), lambda i, s: (0, s[0], 0))],
            out_specs=pl.BlockSpec((rows, model), lambda i, s: (0, 0)),
        ),
        compiler_params=pltpu.CompilerParams(vmem_limit_bytes=VMEM_LIMIT),
        name="spatial_output",
    )(me, *arrays, video)


def temporal_kernel(valid_ref, *refs):
    inputs, (gain_ref, w_ref), outs = refs[:4], refs[4:6], refs[6:]
    width = w_ref.shape[0] // 3
    frames = inputs[0].shape[0]
    hidden = lax.broadcasted_iota(jnp.int32, (frames, frames), 0) >= valid_ref[0]
    for d in range(4):
        normed = normalize(inputs[d][...].astype(F32), gain_ref[...]).astype(BF16)
        queries_t, keys, values_t = project_qkv(normed, w_ref, width)
        outs[d][...] = attend_t(queries_t, keys, values_t, hidden).astype(BF16)


def temporal_call(valid, quarters, gain, weight_t):
    frames = quarters[0].shape[0]
    width = weight_t.shape[0] // 3
    return pl.pallas_call(
        temporal_kernel,
        out_shape=[jax.ShapeDtypeStruct((frames, width), BF16)] * 4,
        in_specs=[pl.BlockSpec(memory_space=pltpu.SMEM)]
        + [pl.BlockSpec(memory_space=pltpu.VMEM)] * 6,
        out_specs=[pl.BlockSpec(memory_space=pltpu.VMEM)] * 4,
        compiler_params=pltpu.CompilerParams(vmem_limit_bytes=VMEM_LIMIT),
        name="temporal_attention",
    )(valid, *quarters, gain, weight_t)


def temporal_out_kernel(*refs):
    parts = refs[:4]
    w0, w1, w2, w3, residual, out = refs[4:]
    total = project_out(parts, [(w0,), (w1,), (w2,), (w3,)])
    out[...] = (residual[...].astype(F32) + total).astype(BF16)


def temporal_out_call(parts, weights, residual):
    return pl.pallas_call(
        temporal_out_kernel,
        out_shape=jax.ShapeDtypeStruct(residual.shape, BF16),
        compiler_params=pltpu.CompilerParams(vmem_limit_bytes=VMEM_LIMIT),
        name="temporal_output",
    )(*parts, *weights, residual)


def pool_kernel(x_ref, gain_ref, out, sums):
    frames, share, _ = out.shape
    rows = frames * share
    order = one_hot_rows(rows, lambda i: (i % share) * frames + i // share)
    ordered = dot_nn(order, x_ref[...])
    out[...] = ordered.astype(BF16).reshape(out.shape)
    closing = normalize(ordered, gain_ref[...])
    for f in range(frames):
        sums[f : f + 1] = jnp.sum(closing[f * share : (f + 1) * share], axis=0, keepdims=True)


def pool_call(mixed, gain, frames):
    rows, model = mixed.shape
    return pl.pallas_call(
        pool_kernel,
        out_shape=[
            jax.ShapeDtypeStruct((frames, rows // frames, model), BF16),
            jax.ShapeDtypeStruct((frames, model), F32),
        ],
        compiler_params=pltpu.CompilerParams(vmem_limit_bytes=VMEM_LIMIT),
        name="closing_pool",
    )(mixed, gain)


def head_kernel(policy_ref, s0, s1, s2, s3, w_ref, down, up, vector, out, *, patches):
    pooled = ((s0[...] + s1[...] + s2[...] + s3[...]) * (1.0 / patches)).astype(BF16)
    lowrank = dot_nt(pooled, down[0]).astype(BF16)
    hidden = dot_nt(pooled, w_ref[...]) + ADAPTER_SCALE * dot_nn(lowrank, up[0])
    activated = jax.nn.gelu(hidden, approximate=True)
    score = jnp.sum(activated * vector[...].astype(F32), axis=-1, keepdims=True)
    out[...] = jnp.broadcast_to(score, out.shape)


def head_call(policy, sums, weight_t, down_t, up, vector, patches):
    frames, model = sums[0].shape
    rank, width = up.shape[1:]

    def kernel(*refs):
        head_kernel(*refs, patches=patches)

    return pl.pallas_call(
        kernel,
        out_shape=jax.ShapeDtypeStruct((frames, LANES), F32),
        grid_spec=pltpu.PrefetchScalarGridSpec(
            num_scalar_prefetch=1,
            grid=(1,),
            in_specs=[whole(s) for s in sums]
            + [
                whole(weight_t),
                pl.BlockSpec((1, rank, model), lambda i, s: (s[0], 0, 0)),
                pl.BlockSpec((1, rank, width), lambda i, s: (s[0], 0, 0)),
                whole(vector),
            ],
            out_specs=pl.BlockSpec((frames, LANES), lambda i, s: (0, 0)),
        ),
        compiler_params=pltpu.CompilerParams(vmem_limit_bytes=VMEM_LIMIT),
        name="scoring_head",
    )(policy, *sums, weight_t, down_t, up, vector)


def assemble_kernel(me_ref, p0, p1, p2, p3, out, sems):
    share = p0.shape[1]
    copies = []
    for d, piece in enumerate((p0, p1, p2, p3)):
        start = pl.multiple_of(jnp.bitwise_xor(me_ref[0], d) * share, share)
        copies.append(pltpu.make_async_copy(piece, out.at[:, pl.ds(start, share), :], sems.at[d]))
    for copy in copies:
        copy.start()
    for copy in copies:
        copy.wait()


def assemble_call(me, pieces):
    frames, share, model = pieces[0].shape
    return pl.pallas_call(
        assemble_kernel,
        out_shape=jax.ShapeDtypeStruct((frames, 4 * share, model), BF16),
        in_specs=[pl.BlockSpec(memory_space=pltpu.SMEM)] + [pl.BlockSpec(memory_space=pl.ANY)] * 4,
        out_specs=pl.BlockSpec(memory_space=pl.ANY),
        scratch_shapes=[pltpu.SemaphoreType.DMA((4,))],
        name="assemble_output",
    )(me, *pieces)


def peer(x, d):
    return lax.ppermute(x, "tp", [(i, i ^ d) for i in range(4)])


def gather_four(x):
    other = peer(x, 2)
    return [x, peer(x, 1), other, peer(other, 1)]


def exchange_four(parts):
    return [parts[0], *(peer(parts[d], d) for d in (1, 2, 3))]


def across(x):
    pairs = [
        (s * 4 + t, (s ^ 1) * 4 + (t ^ 2)) for s in range(lax.axis_size("seq")) for t in range(4)
    ]
    return lax.ppermute(x, ("seq", "tp"), pairs)


def gather_weight(weight):
    half = weight.shape[0] // 2
    other = jnp.concatenate([across(weight[:half]), peer(weight[half:], 2)], axis=0)
    return [weight, peer(weight, 1), other, peer(other, 1)]


def shards(
    video,
    spatial_norm_gain,
    spatial_query_key_value,
    spatial_output_weight,
    temporal_norm_gain,
    temporal_query_key_value,
    temporal_output_weight,
    closing_norm_gain,
    scoring_hidden_weight,
    adapter_down_weight,
    adapter_up_weight,
    scoring_vector,
    policy,
    valid_frame_count,
):
    frames_here, patches, model = video.shape
    width = spatial_output_weight.shape[0]
    seq = lax.axis_size("seq")
    me = lax.axis_index("tp").astype(jnp.int32).reshape(1)

    def turned(weight):
        return jnp.transpose(weight, (1, 2, 0)).reshape(3 * width, model)

    def over_seq(x):
        rows = x.shape[0]
        blocks = x.reshape(seq, rows // seq, model)
        return lax.all_to_all(blocks, "seq", 0, 0, tiled=True).reshape(rows, model)

    spatial_out_weights = gather_weight(spatial_output_weight)
    parts = spatial_call(
        me, video, spatial_norm_gain.reshape(1, model), turned(spatial_query_key_value)
    )
    parts = exchange_four(parts)
    stream = spatial_out_call(me, parts, spatial_out_weights, video)
    temporal_weight, _ = lax.optimization_barrier((temporal_output_weight, parts[0]))
    temporal_out_weights = gather_weight(temporal_weight)
    moved = over_seq(stream)
    quarters = gather_four(moved)
    mixed = temporal_call(
        valid_frame_count,
        quarters,
        temporal_norm_gain.reshape(1, model),
        turned(temporal_query_key_value),
    )
    mixed = exchange_four(mixed)
    updated = temporal_out_call(mixed, temporal_out_weights, moved)
    returned = over_seq(updated)
    piece, sums = pool_call(returned, closing_norm_gain.reshape(1, model), frames_here)
    all_sums = exchange_four([sums] * 4)
    pieces = gather_four(piece)
    blended = assemble_call(me, pieces)
    scores = head_call(
        policy,
        all_sums,
        jnp.transpose(scoring_hidden_weight),
        jnp.transpose(adapter_down_weight, (0, 2, 1)),
        adapter_up_weight,
        scoring_vector.reshape(1, width),
        patches,
    )
    score = sum(exchange_four([scores] * 4))[:, 0]
    frame_index = lax.axis_index("seq") * frames_here + jnp.arange(frames_here)
    reward = jnp.where(frame_index < valid_frame_count[0], score, jnp.float32(0.0))
    return (blended, reward)


def solution(mesh):
    in_specs = (
        P("seq", None, None),
        P(),
        P(None, None, "tp"),
        P("tp", None),
        P(),
        P(None, None, "tp"),
        P("tp", None),
        P(),
        P(None, "tp"),
        P(),
        P(None, None, "tp"),
        P("tp"),
        P(),
        P(),
    )
    out_specs = (P("seq", None, None), P("seq"))
    return jax.shard_map(shards, mesh=mesh, in_specs=in_specs, out_specs=out_specs, check_vma=False)
```

time: 319 us -> 200 us (0.63)
  waiting for transfers between devices: 169 us -> 69.8 us
  Pallas kernels: 0 us -> 62.8 us
  local copies, waits for them, and re-layouts: 49.5 us -> 16.8 us
  matrix products: 28.4 us -> 0 us
  starting transfers between devices: 25.7 us -> 47.4 us
  other arithmetic: 22 us -> 0.52 us
  between operations: 15.6 us -> 2.37 us
  blocking collectives: 7.86 us -> 0 us
    psum x2 -> x0, waiting for transfers between devices: 96.3 us -> none  [the longest x1 56.2 us: shards(): lax.psum(space_partial.astype(jnp.bfloat16), 'tp').astype(jnp.float32)]
    pallas_call x0 -> x7, Pallas kernels: none -> 62.8 us  [the longest x1 44.8 us: assemble_call(): pl.pallas_call(assemble_kernel, out_shape=jax.ShapeDtypeStruct((frames, 4...]
    all_to_all x2, waiting for transfers between devices: 72.3 us -> 25.2 us  [over_seq(): return lax.all_to_all(blocks, 'seq', 0, 0, tiled=True).reshape(rows, model)]
    ppermute x0 -> x26, waiting for transfers between devices: none -> 44.6 us  [the longest x24 35.7 us: peer(): return lax.ppermute(x, 'tp', [(i, i ^ d) for i in range(4)])]
    ppermute x0 -> x26, starting transfers between devices: none -> 27.3 us  [the longest x24 22.4 us: peer(): return lax.ppermute(x, 'tp', [(i, i ^ d) for i in range(4)])]
    dot_general x9 -> x0, matrix products: 23.5 us -> none  [the longest x1 5.13 us: shards(): jnp.dot(normed_time, temporal_query_key_value.reshape(width, 3 * local_wi...]
    convert_element_type x6 -> x0, local copies, waits for them, and re-layouts: 16.3 us -> none  [the longest x2 8.6 us: shards(): moved_flat.astype(jnp.float32) + time_total]
    reshape x5 -> x8, local copies, waits for them, and re-layouts: 15.2 us -> 4.02 us  [the longest x2 2.74 us: over_seq(): blocks = x.reshape(seq, rows // seq, model)]
  transfers between devices with their start and end apart: 4 -> 28, of which waited for: 4 -> 15; matrix products, arithmetic and copies ran while one was open for 3% -> 3% of each run, Pallas kernels for 0% -> 8%
where the time goes in v1:
time: 200 us
  waiting for transfers between devices  69.8 us (35%)
  Pallas kernels  62.8 us (31%)
  starting transfers between devices  47.4 us (24%)
  local copies, waits for them, and re-layouts  16.8 us (8%)
  between operations  2.37 us (1%)
    pallas_call x1, Pallas kernels, assemble_call(): pl.pallas_call(assemble_kernel, out_shape=jax.ShapeDtypeStruct((frames, 4...  44.8 us
    ppermute x24, waiting for transfers between devices, peer(): return lax.ppermute(x, 'tp', [(i, i ^ d) for i in range(4)])  35.7 us
    all_to_all x2, waiting for transfers between devices, over_seq(): return lax.all_to_all(blocks, 'seq', 0, 0, tiled=True).reshape(rows, model)  25.2 us
    ppermute x24, starting transfers between devices, peer(): return lax.ppermute(x, 'tp', [(i, i ^ d) for i in range(4)])  22.4 us
    all_to_all x2, starting transfers between devices, over_seq(): return lax.all_to_all(blocks, 'seq', 0, 0, tiled=True).reshape(rows, model)  20.1 us
    unnamed x40, local copies, waits for them, and re-layouts  9.15 us
    ppermute x2, waiting for transfers between devices, across(): return lax.ppermute(x, ('seq', 'tp'), pairs)  8.88 us
    pallas_call x1, Pallas kernels, temporal_call(): pl.pallas_call(temporal_kernel, out_shape=[jax.ShapeDtypeStruct((frames,...  6.96 us
  transfers between devices with their start and end apart: 28, of which 15 were waited for; matrix products, arithmetic and copies ran while one was open for 3% of the time, Pallas kernels for 8%

profile of v1, /device:TPU:1, one launch (start us, length us, event | category | flops | bytes accessed | tf_op | source)
XLA Modules:
  0.0 199.7 jit_solution(4126705577918777196)
XLA Ops:
  0.6 1.4 fusion.1
  2.0 3.7 %collective-permute-start.4 = (bf16[176,1408]{1,0:T(8,128)(2,1)S(1)}, bf16[176,1408]{1,0:T(8,128)(2,1)S(1)}, u32[]{:S(2)}, u32[]{:S(2)}) collective-permute-start(bf16[176,1408]{1,0:T(8,128)(2,1)S(1)} %get-tuple-element.27), channel_id=1, source_target_pairs={{0,6},{1,7},{2,4},{3,5},{4,2},{5,3},{6,0},{7,1},{8,14},{9,15},{10,... | collective-permute-start | bytes 1486856 | tf_op jit(solution)/shard_map/ppermute | solution.py:290
  6.8 8.9 %collective-permute-done.4 = bf16[176,1408]{1,0:T(8,128)(2,1)S(1)} collective-permute-done((bf16[176,1408]{1,0:T(8,128)(2,1)S(1)}, bf16[176,1408]{1,0:T(8,128)(2,1)S(1)}, u32[]{:S(2)}, u32[]{:S(2)}) %collective-permute-start.4) | collective-permute-done | bytes 495648 | tf_op jit(solution)/shard_map/ppermute | solution.py:290
  15.7 1.8 collective-permute-done.5
  17.6 2.0 collective-permute-start.6
  19.6 1.8 copy-done.3
  21.4 5.0 %spatial_attention.1 = (bf16[128,352]{1,0:T(8,128)(2,1)S(1)}, bf16[128,352]{1,0:T(8,128)(2,1)S(1)}, bf16[128,352]{1,0:T(8,128)(2,1)S(1)}, bf16[128,352]{1,0:T(8,128)(2,1)S(1)}) custom-call(s32[1]{0:T(128)} %bitcast.me_ref, bf16[2,256,1408]{2,1,0:T(8,128)(2,1)S(1)} %copy-done, f32[1,1408]{1,0:T(1,128)S(1)} %reshape.38.gain_ref, bf16[1056,1408]{1,0:T(8,128)(2,1)S(1)} %bitcast.11), custom_call_target="tpu_custom_call" | custom-call | tf_op jit(solution)/shard_map/spatial_attention/pallas_call | solution.py:81
  27.5 1.3 collective-permute-start.14
  30.5 13.6 %collective-permute-done.1.refs_2_ = bf16[128,352]{1,0:T(8,128)(2,1)S(1)} collective-permute-done((bf16[128,352]{1,0:T(8,128)(2,1)S(1)}, bf16[128,352]{1,0:T(8,128)(2,1)S(1)}, u32[]{:S(2)}, u32[]{:S(2)}) %collective-permute-start.1) | collective-permute-done | bytes 90144 | tf_op jit(solution)/shard_map/ppermute | solution.py:274
  45.0 4.2 %collective-permute-done.2.refs_3_ = bf16[128,352]{1,0:T(8,128)(2,1)S(1)} collective-permute-done((bf16[128,352]{1,0:T(8,128)(2,1)S(1)}, bf16[128,352]{1,0:T(8,128)(2,1)S(1)}, u32[]{:S(2)}, u32[]{:S(2)}) %collective-permute-start.2) | collective-permute-done | bytes 90144 | tf_op jit(solution)/shard_map/ppermute | solution.py:274
  49.2 2.7 %spatial_output.1 = bf16[128,1408]{1,0:T(8,128)(2,1)S(1)} custom-call(s32[1]{0:T(128)} %bitcast.me_ref, bf16[128,352]{1,0:T(8,128)(2,1)S(1)} %get-tuple-element.13.refs_0_, bf16[128,352]{1,0:T(8,128)(2,1)S(1)} %collective-permute-done.refs_1_, bf16[128,352]{1,0:T(8,128)(2,1)S(1)} %collective-permute-done.1.refs_2_, ...), custom_call_target="tpu_custom_call" | custom-call | tf_op jit(solution)/shard_map/spatial_output/pallas_call | solution.py:133
  52.6 1.9 reshape.40
  54.5 13.0 %all-to-all-start = ((bf16[64,2,1408]{2,1,0:T(2,128)(2,1)}), bf16[64,2,1408]{2,1,0:T(2,128)(2,1)}, u32[]{:S(2)}, u32[]{:S(2)}) async-start(bf16[64,2,1408]{2,1,0:T(2,128)(2,1)} %reshape.40), calls=%async_computation | async-start | bytes 720896 | tf_op jit(solution)/shard_map/all_to_all | solution.py:326
  70.7 10.8 %all-to-all-done = bf16[64,2,1408]{2,1,0:T(2,128)(2,1)} async-done(((bf16[64,2,1408]{2,1,0:T(2,128)(2,1)}), bf16[64,2,1408]{2,1,0:T(2,128)(2,1)}, u32[]{:S(2)}, u32[]{:S(2)}) %all-to-all-start) | async-done | bytes 360480 | tf_op jit(solution)/shard_map/all_to_all | solution.py:326
  83.2 3.0 %collective-permute-start.7 = (bf16[128,1408]{1,0:T(8,128)(2,1)S(1)}, bf16[128,1408]{1,0:T(8,128)(2,1)S(1)}, u32[]{:S(2)}, u32[]{:S(2)}) collective-permute-start(bf16[128,1408]{1,0:T(8,128)(2,1)S(1)} %reshape.41.refs_0_.refs_8_), channel_id=1, source_target_pairs={{0,1},{1,0},{2,3},{3,2},{4,5},{5,4},{6,7},{7,6},{8,9},{9,8},{10,11... | collective-permute-start | bytes 1081352 | tf_op jit(solution)/shard_map/ppermute | solution.py:274
  86.2 3.9 %collective-permute-done.8.refs_2_ = bf16[128,1408]{1,0:T(8,128)(2,1)S(1)} collective-permute-done((bf16[128,1408]{1,0:T(8,128)(2,1)S(1)}, bf16[128,1408]{1,0:T(8,128)(2,1)S(1)}, u32[]{:S(2)}, u32[]{:S(2)}) %collective-permute-start.8) | collective-permute-done | bytes 360480 | tf_op jit(solution)/shard_map/ppermute | solution.py:274
  90.1 3.5 %collective-permute-start.9 = (bf16[128,1408]{1,0:T(8,128)(2,1)S(1)}, bf16[128,1408]{1,0:T(8,128)(2,1)S(1)}, u32[]{:S(2)}, u32[]{:S(2)}) collective-permute-start(bf16[128,1408]{1,0:T(8,128)(2,1)S(1)} %collective-permute-done.8.refs_2_), channel_id=1, source_target_pairs={{0,1},{1,0},{2,3},{3,2},{4,5},{5,4},{6,7},{7,6},{8,9},{9,8},{10,11... | collective-permute-start | bytes 1081352 | tf_op jit(solution)/shard_map/ppermute | solution.py:274
  94.9 1.8 copy-done.4
  96.7 7.0 %temporal_attention.1 = (bf16[128,352]{1,0:T(8,128)(2,1)S(1)}, bf16[128,352]{1,0:T(8,128)(2,1)S(1)}, bf16[128,352]{1,0:T(8,128)(2,1)S(1)}, bf16[128,352]{1,0:T(8,128)(2,1)S(1)}) custom-call(s32[1]{0:T(128)} %copy.19.valid_ref, bf16[128,1408]{1,0:T(8,128)(2,1)S(1)} %reshape.41.refs_0_.refs_8_, bf16[128,1408]{1,0:T(8,128)(2,1)S(1)} %collective-permute-done.7.refs_1_, ...), custom_call_target="tpu_custom_call" | custom-call | tf_op jit(solution)/shard_map/temporal_attention/pallas_call | solution.py:162
  104.6 1.4 collective-permute-start.12
  106.9 1.5 collective-permute-done.11.refs_2_
  108.4 2.4 %collective-permute-done.12.refs_3_ = bf16[128,352]{1,0:T(8,128)(2,1)S(1)} collective-permute-done((bf16[128,352]{1,0:T(8,128)(2,1)S(1)}, bf16[128,352]{1,0:T(8,128)(2,1)S(1)}, u32[]{:S(2)}, u32[]{:S(2)}) %collective-permute-start.12) | collective-permute-done | bytes 90144 | tf_op jit(solution)/shard_map/ppermute | solution.py:274
  110.8 1.2 copy-done.7
  112.0 2.2 %temporal_output.1 = bf16[128,1408]{1,0:T(8,128)(2,1)S(1)} custom-call(bf16[128,352]{1,0:T(8,128)(2,1)S(1)} %get-tuple-element.17.refs_0_, bf16[128,352]{1,0:T(8,128)(2,1)S(1)} %collective-permute-done.10.refs_1_, bf16[128,352]{1,0:T(8,128)(2,1)S(1)} %collective-permute-done.11.refs_2_, bf16[128,352]{1,0:T(8,128)(2,1)S(1)} %collective-permute-done.12.refs_3_, ...), custom_call_target="tpu_custom_call" | custom-call | tf_op jit(solution)/shard_map/temporal_output/pallas_call | solution.py:181
  115.1 7.1 %all-to-all-start.1 = ((bf16[64,2,1408]{2,1,0:T(2,128)(2,1)}), bf16[64,2,1408]{2,1,0:T(2,128)(2,1)S(1)}, u32[]{:S(2)}, u32[]{:S(2)}) async-start(bf16[64,2,1408]{2,1,0:T(2,128)(2,1)} %reshape.44), calls=%async_computation.1 | async-start | bytes 720896 | tf_op jit(solution)/shard_map/all_to_all | solution.py:326
  122.2 14.4 %all-to-all-done.1 = bf16[64,2,1408]{2,1,0:T(2,128)(2,1)S(1)} async-done(((bf16[64,2,1408]{2,1,0:T(2,128)(2,1)}), bf16[64,2,1408]{2,1,0:T(2,128)(2,1)S(1)}, u32[]{:S(2)}, u32[]{:S(2)}) %all-to-all-start.1) | async-done | bytes 360480 | tf_op jit(solution)/shard_map/all_to_all | solution.py:326
  137.7 2.6 %collective-permute-start.20 = (f32[2,1408]{1,0:T(2,128)S(1)}, f32[2,1408]{1,0:T(2,128)S(1)}, u32[]{:S(2)}, u32[]{:S(2)}) collective-permute-start(f32[2,1408]{1,0:T(2,128)S(1)} %get-tuple-element.23.refs_1_), channel_id=1, source_target_pairs={{0,1},{1,0},{2,3},{3,2},{4,5},{5,4},{6,7},{7,6},{8,9},{9,8},{10,11... | collective-permute-start | bytes 33800 | tf_op jit(solution)/shard_map/ppermute | solution.py:274
  140.2 1.2 collective-permute-start.21
  142.5 2.7 %collective-permute-done.21.refs_3_ = f32[2,1408]{1,0:T(2,128)S(1)} collective-permute-done((f32[2,1408]{1,0:T(2,128)S(1)}, f32[2,1408]{1,0:T(2,128)S(1)}, u32[]{:S(2)}, u32[]{:S(2)}) %collective-permute-start.21) | collective-permute-done | bytes 11296 | tf_op jit(solution)/shard_map/ppermute | solution.py:274
  145.2 2.9 %collective-permute-done.22.refs_4_ = f32[2,1408]{1,0:T(2,128)S(1)} collective-permute-done((f32[2,1408]{1,0:T(2,128)S(1)}, f32[2,1408]{1,0:T(2,128)S(1)}, u32[]{:S(2)}, u32[]{:S(2)}) %collective-permute-start.22) | collective-permute-done | bytes 11296 | tf_op jit(solution)/shard_map/ppermute | solution.py:274
  149.6 1.4 collective-permute-start.25
  154.7 44.8 %assemble_output.1 = bf16[2,256,1408]{2,1,0:T(8,128)(2,1)} custom-call(s32[1]{0:T(128)} %bitcast.me_ref, bf16[2,64,1408]{2,1,0:T(8,128)(2,1)} %copy-done.9, bf16[2,64,1408]{2,1,0:T(8,128)(2,1)} %copy-done.13, bf16[2,64,1408]{2,1,0:T(8,128)(2,1)} %copy-done.12, bf16[2,64,1408]{2,1,0:T(8,128)(2,1)} %copy-done.14), custom_call_target="tpu_custom_call" | custom-call | tf_op jit(solution)/shard_map/assemble_output/pallas_call | solution.py:263
  (86 shorter events, 20.4 us)
Async XLA Ops:
  2.0 13.6 %collective-permute-start.4 = (bf16[176,1408]{1,0:T(8,128)(2,1)S(1)}, bf16[176,1408]{1,0:T(8,128)(2,1)S(1)}, u32[]{:S(2)}, u32[]{:S(2)}) collective-permute-start(bf16[176,1408]{1,0:T(8,128)(2,1)S(1)} %get-tuple-element.27), channel_id=1, source_target_pairs={{0,6},{1,7},{2,4},{3,5},{4,2},{5,3},{6,0},{7,1},{8,14},{9,15},{10,... | collective-permute-start | bytes 1486856 | tf_op jit(solution)/shard_map/ppermute | solution.py:290
  5.7 11.9 %collective-permute-start.5 = (bf16[176,1408]{1,0:T(8,128)(2,1)S(1)}, bf16[176,1408]{1,0:T(8,128)(2,1)S(1)}, u32[]{:S(2)}, u32[]{:S(2)}) collective-permute-start(bf16[176,1408]{1,0:T(8,128)(2,1)S(1)} %get-tuple-element.26), channel_id=1, source_target_pairs={{0,2},{1,3},{2,0},{3,1},{4,6},{5,7},{6,4},{7,5},{8,10},{9,11},{10,... | collective-permute-start | bytes 1486856 | tf_op jit(solution)/shard_map/ppermute | solution.py:274
  5.7 43.5 %collective-permute-start.3 = (bf16[352,1408]{1,0:T(8,128)(2,1)}, bf16[352,1408]{1,0:T(8,128)(2,1)}, u32[]{:S(2)}, u32[]{:S(2)}) collective-permute-start(bf16[352,1408]{1,0:T(8,128)(2,1)} %refs_4_.1), channel_id=1, source_target_pairs={{0,1},{1,0},{2,3},{3,2},{4,5},{5,4},{6,7},{7,6},{8,9},{9,8},{10,11... | collective-permute-start | bytes 2973704 | tf_op jit(solution)/shard_map/ppermute | solution.py:274
  17.6 31.6 %collective-permute-start.6 = (bf16[352,1408]{1,0:T(8,128)(2,1)S(1)}, bf16[352,1408]{1,0:T(8,128)(2,1)}, u32[]{:S(2)}, u32[]{:S(2)}) collective-permute-start(bf16[352,1408]{1,0:T(8,128)(2,1)S(1)} %constant_dynamic-update-slice_fusion.refs_6_), channel_id=1, source_target_pairs={{0,1},{1,0},{2,3},{3,2},{4,5},{5,4},{6,7},{7,6},{8,9},{9,8},{10,11... | collective-permute-start | bytes 2973704 | tf_op jit(solution)/shard_map/ppermute | solution.py:274
  27.5 40.8 %collective-permute-start.14 = (bf16[176,1408]{1,0:T(8,128)(2,1)}, bf16[176,1408]{1,0:T(8,128)(2,1)}, u32[]{:S(2)}, u32[]{:S(2)}) collective-permute-start(bf16[176,1408]{1,0:T(8,128)(2,1)} %get-tuple-element.25), channel_id=1, source_target_pairs={{0,6},{1,7},{2,4},{3,5},{4,2},{5,3},{6,0},{7,1},{8,14},{9,15},{10,... | collective-permute-start | bytes 1486856 | tf_op jit(solution)/shard_map/ppermute | solution.py:290
  28.7 1.3 collective-permute-start
  29.0 40.3 %collective-permute-start.15 = (bf16[176,1408]{1,0:T(8,128)(2,1)}, bf16[176,1408]{1,0:T(8,128)(2,1)}, u32[]{:S(2)}, u32[]{:S(2)}) collective-permute-start(bf16[176,1408]{1,0:T(8,128)(2,1)} %get-tuple-element.24), channel_id=1, source_target_pairs={{0,2},{1,3},{2,0},{3,1},{4,6},{5,7},{6,4},{7,5},{8,10},{9,11},{10,... | collective-permute-start | bytes 1486856 | tf_op jit(solution)/shard_map/ppermute | solution.py:274
  30.0 14.1 %collective-permute-start.1 = (bf16[128,352]{1,0:T(8,128)(2,1)S(1)}, bf16[128,352]{1,0:T(8,128)(2,1)S(1)}, u32[]{:S(2)}, u32[]{:S(2)}) collective-permute-start(bf16[128,352]{1,0:T(8,128)(2,1)S(1)} %get-tuple-element.15), channel_id=1, source_target_pairs={{0,2},{1,3},{2,0},{3,1},{4,6},{5,7},{6,4},{7,5},{8,10},{9,11},{10,... | collective-permute-start | bytes 270344 | tf_op jit(solution)/shard_map/ppermute | solution.py:274
  44.1 5.1 %collective-permute-start.2 = (bf16[128,352]{1,0:T(8,128)(2,1)S(1)}, bf16[128,352]{1,0:T(8,128)(2,1)S(1)}, u32[]{:S(2)}, u32[]{:S(2)}) collective-permute-start(bf16[128,352]{1,0:T(8,128)(2,1)S(1)} %get-tuple-element.16), channel_id=1, source_target_pairs={{0,3},{1,2},{2,1},{3,0},{4,7},{5,6},{6,5},{7,4},{8,11},{9,10},{10,... | collective-permute-start | bytes 270344 | tf_op jit(solution)/shard_map/ppermute | solution.py:274
  52.6 41.7 %copy-start.16 = (f32[1408]{0:T(1024)S(1)}, f32[1408]{0:T(1024)}, u32[]{:S(2)}) copy-start(f32[1408]{0:T(1024)} %param.18) | copy-start | bytes 16900
  54.5 27.1 %all-to-all-start = ((bf16[64,2,1408]{2,1,0:T(2,128)(2,1)}), bf16[64,2,1408]{2,1,0:T(2,128)(2,1)}, u32[]{:S(2)}, u32[]{:S(2)}) async-start(bf16[64,2,1408]{2,1,0:T(2,128)(2,1)} %reshape.40), calls=%async_computation | async-start | bytes 720896 | tf_op jit(solution)/shard_map/all_to_all | solution.py:326
  67.5 38.4 %collective-permute-start.13 = (bf16[352,1408]{1,0:T(8,128)(2,1)S(1)}, bf16[352,1408]{1,0:T(8,128)(2,1)S(1)}, u32[]{:S(2)}, u32[]{:S(2)}) collective-permute-start(bf16[352,1408]{1,0:T(8,128)(2,1)S(1)} %copy-done.2), channel_id=1, source_target_pairs={{0,1},{1,0},{2,3},{3,2},{4,5},{5,4},{6,7},{7,6},{8,9},{9,8},{10,11... | collective-permute-start | bytes 2973704 | tf_op jit(solution)/shard_map/ppermute | solution.py:274
  70.4 36.5 %collective-permute-start.16 = (bf16[352,1408]{1,0:T(8,128)(2,1)S(1)}, bf16[352,1408]{1,0:T(8,128)(2,1)}, u32[]{:S(2)}, u32[]{:S(2)}) collective-permute-start(bf16[352,1408]{1,0:T(8,128)(2,1)S(1)} %constant_dynamic-update-slice_fusion.2.refs_6_), channel_id=1, source_target_pairs={{0,1},{1,0},{2,3},{3,2},{4,5},{5,4},{6,7},{7,6},{8,9},{9,8},{10,11... | collective-permute-start | bytes 2973704 | tf_op jit(solution)/shard_map/ppermute | solution.py:274
  82.7 7.4 %collective-permute-start.8 = (bf16[128,1408]{1,0:T(8,128)(2,1)S(1)}, bf16[128,1408]{1,0:T(8,128)(2,1)S(1)}, u32[]{:S(2)}, u32[]{:S(2)}) collective-permute-start(bf16[128,1408]{1,0:T(8,128)(2,1)S(1)} %reshape.41.refs_0_.refs_8_), channel_id=1, source_target_pairs={{0,2},{1,3},{2,0},{3,1},{4,6},{5,7},{6,4},{7,5},{8,10},{9,11},{10,... | collective-permute-start | bytes 1081352 | tf_op jit(solution)/shard_map/ppermute | solution.py:274
  83.2 11.1 %collective-permute-start.7 = (bf16[128,1408]{1,0:T(8,128)(2,1)S(1)}, bf16[128,1408]{1,0:T(8,128)(2,1)S(1)}, u32[]{:S(2)}, u32[]{:S(2)}) collective-permute-start(bf16[128,1408]{1,0:T(8,128)(2,1)S(1)} %reshape.41.refs_0_.refs_8_), channel_id=1, source_target_pairs={{0,1},{1,0},{2,3},{3,2},{4,5},{5,4},{6,7},{7,6},{8,9},{9,8},{10,11... | collective-permute-start | bytes 1081352 | tf_op jit(solution)/shard_map/ppermute | solution.py:274
  90.1 4.8 %collective-permute-start.9 = (bf16[128,1408]{1,0:T(8,128)(2,1)S(1)}, bf16[128,1408]{1,0:T(8,128)(2,1)S(1)}, u32[]{:S(2)}, u32[]{:S(2)}) collective-permute-start(bf16[128,1408]{1,0:T(8,128)(2,1)S(1)} %collective-permute-done.8.refs_2_), channel_id=1, source_target_pairs={{0,1},{1,0},{2,3},{3,2},{4,5},{5,4},{6,7},{7,6},{8,9},{9,8},{10,11... | collective-permute-start | bytes 1081352 | tf_op jit(solution)/shard_map/ppermute | solution.py:274
  103.7 3.2 %collective-permute-start.10 = (bf16[128,352]{1,0:T(8,128)(2,1)S(1)}, bf16[128,352]{1,0:T(8,128)(2,1)S(1)}, u32[]{:S(2)}, u32[]{:S(2)}) collective-permute-start(bf16[128,352]{1,0:T(8,128)(2,1)S(1)} %get-tuple-element.18), channel_id=1, source_target_pairs={{0,1},{1,0},{2,3},{3,2},{4,5},{5,4},{6,7},{7,6},{8,9},{9,8},{10,11... | collective-permute-start | bytes 270344 | tf_op jit(solution)/shard_map/ppermute | solution.py:274
  104.2 4.3 %collective-permute-start.11 = (bf16[128,352]{1,0:T(8,128)(2,1)S(1)}, bf16[128,352]{1,0:T(8,128)(2,1)S(1)}, u32[]{:S(2)}, u32[]{:S(2)}) collective-permute-start(bf16[128,352]{1,0:T(8,128)(2,1)S(1)} %get-tuple-element.19), channel_id=1, source_target_pairs={{0,2},{1,3},{2,0},{3,1},{4,6},{5,7},{6,4},{7,5},{8,10},{9,11},{10,... | collective-permute-start | bytes 270344 | tf_op jit(solution)/shard_map/ppermute | solution.py:274
  104.6 6.2 %collective-permute-start.12 = (bf16[128,352]{1,0:T(8,128)(2,1)S(1)}, bf16[128,352]{1,0:T(8,128)(2,1)S(1)}, u32[]{:S(2)}, u32[]{:S(2)}) collective-permute-start(bf16[128,352]{1,0:T(8,128)(2,1)S(1)} %get-tuple-element.20), channel_id=1, source_target_pairs={{0,3},{1,2},{2,1},{3,0},{4,7},{5,6},{6,5},{7,4},{8,11},{9,10},{10,... | collective-permute-start | bytes 270344 | tf_op jit(solution)/shard_map/ppermute | solution.py:274
  112.0 36.2 %copy-start.10 = (bf16[8,1408,16]{1,2,0:T(8,128)(2,1)S(1)}, bf16[8,1408,16]{1,2,0:T(8,128)(2,1)}, u32[]{:S(2)}) copy-start(bf16[8,1408,16]{1,2,0:T(8,128)(2,1)} %param.23) | copy-start | bytes 1081348
  112.0 36.2 %copy-start.11 = (bf16[8,16,352]{2,1,0:T(8,128)(2,1)S(1)}, bf16[8,16,352]{2,1,0:T(8,128)(2,1)}, u32[]{:S(2)}) copy-start(bf16[8,16,352]{2,1,0:T(8,128)(2,1)} %refs_7_.1) | copy-start | bytes 270340
  114.2 33.9 %copy-start.8 = (bf16[1408,352]{0,1:T(8,128)(2,1)S(1)}, bf16[1408,352]{0,1:T(8,128)(2,1)}, u32[]{:S(2)}) copy-start(bf16[1408,352]{0,1:T(8,128)(2,1)} %param.22) | copy-start | bytes 2973700
  115.1 21.5 %all-to-all-start.1 = ((bf16[64,2,1408]{2,1,0:T(2,128)(2,1)}), bf16[64,2,1408]{2,1,0:T(2,128)(2,1)S(1)}, u32[]{:S(2)}, u32[]{:S(2)}) async-start(bf16[64,2,1408]{2,1,0:T(2,128)(2,1)} %reshape.44), calls=%async_computation.1 | async-start | bytes 720896 | tf_op jit(solution)/shard_map/all_to_all | solution.py:326
  137.3 13.8 %collective-permute-start.18 = (bf16[2,64,1408]{2,1,0:T(8,128)(2,1)S(1)}, bf16[2,64,1408]{2,1,0:T(8,128)(2,1)S(1)}, u32[]{:S(2)}, u32[]{:S(2)}) collective-permute-start(bf16[2,64,1408]{2,1,0:T(8,128)(2,1)S(1)} %get-tuple-element.22.p0), channel_id=1, source_target_pairs={{0,2},{1,3},{2,0},{3,1},{4,6},{5,7},{6,4},{7,5},{8,10},{9,11},{10,... | collective-permute-start | bytes 1081352 | tf_op jit(solution)/shard_map/ppermute | solution.py:274
  137.7 4.9 %collective-permute-start.20 = (f32[2,1408]{1,0:T(2,128)S(1)}, f32[2,1408]{1,0:T(2,128)S(1)}, u32[]{:S(2)}, u32[]{:S(2)}) collective-permute-start(f32[2,1408]{1,0:T(2,128)S(1)} %get-tuple-element.23.refs_1_), channel_id=1, source_target_pairs={{0,1},{1,0},{2,3},{3,2},{4,5},{5,4},{6,7},{7,6},{8,9},{9,8},{10,11... | collective-permute-start | bytes 33800 | tf_op jit(solution)/shard_map/ppermute | solution.py:274
  140.2 5.0 %collective-permute-start.21 = (f32[2,1408]{1,0:T(2,128)S(1)}, f32[2,1408]{1,0:T(2,128)S(1)}, u32[]{:S(2)}, u32[]{:S(2)}) collective-permute-start(f32[2,1408]{1,0:T(2,128)S(1)} %get-tuple-element.23.refs_1_), channel_id=1, source_target_pairs={{0,2},{1,3},{2,0},{3,1},{4,6},{5,7},{6,4},{7,5},{8,10},{9,11},{10,... | collective-permute-start | bytes 33800 | tf_op jit(solution)/shard_map/ppermute | solution.py:274
  141.4 6.8 %collective-permute-start.22 = (f32[2,1408]{1,0:T(2,128)S(1)}, f32[2,1408]{1,0:T(2,128)S(1)}, u32[]{:S(2)}, u32[]{:S(2)}) collective-permute-start(f32[2,1408]{1,0:T(2,128)S(1)} %get-tuple-element.23.refs_1_), channel_id=1, source_target_pairs={{0,3},{1,2},{2,1},{3,0},{4,7},{5,6},{6,5},{7,4},{8,11},{9,10},{10,... | collective-permute-start | bytes 33800 | tf_op jit(solution)/shard_map/ppermute | solution.py:274
  148.8 2.7 %collective-permute-start.23 = (f32[2,128]{1,0:T(2,128)S(1)}, f32[2,128]{1,0:T(2,128)S(1)}, u32[]{:S(2)}, u32[]{:S(2)}) collective-permute-start(f32[2,128]{1,0:T(2,128)S(1)} %scoring_head.1), channel_id=1, source_target_pairs={{0,1},{1,0},{2,3},{3,2},{4,5},{5,4},{6,7},{7,6},{8,9},{9,8},{10,11... | collective-permute-start | bytes 3080 | tf_op jit(solution)/shard_map/ppermute | solution.py:274
  149.2 2.4 %collective-permute-start.24 = (f32[2,128]{1,0:T(2,128)S(1)}, f32[2,128]{1,0:T(2,128)S(1)}, u32[]{:S(2)}, u32[]{:S(2)}) collective-permute-start(f32[2,128]{1,0:T(2,128)S(1)} %scoring_head.1), channel_id=1, source_target_pairs={{0,2},{1,3},{2,0},{3,1},{4,6},{5,7},{6,4},{7,5},{8,10},{9,11},{10,... | collective-permute-start | bytes 3080 | tf_op jit(solution)/shard_map/ppermute | solution.py:274
  149.6 3.0 %collective-permute-start.25 = (f32[2,128]{1,0:T(2,128)S(1)}, f32[2,128]{1,0:T(2,128)S(1)}, u32[]{:S(2)}, u32[]{:S(2)}) collective-permute-start(f32[2,128]{1,0:T(2,128)S(1)} %scoring_head.1), channel_id=1, source_target_pairs={{0,3},{1,2},{2,1},{3,0},{4,7},{5,6},{6,5},{7,4},{8,11},{9,10},{10,... | collective-permute-start | bytes 3080 | tf_op jit(solution)/shard_map/ppermute | solution.py:274
  151.0 2.2 %collective-permute-start.17 = (bf16[2,64,1408]{2,1,0:T(8,128)(2,1)S(1)}, bf16[2,64,1408]{2,1,0:T(8,128)(2,1)S(1)}, u32[]{:S(2)}, u32[]{:S(2)}) collective-permute-start(bf16[2,64,1408]{2,1,0:T(8,128)(2,1)S(1)} %get-tuple-element.22.p0), channel_id=1, source_target_pairs={{0,1},{1,0},{2,3},{3,2},{4,5},{5,4},{6,7},{7,6},{8,9},{9,8},{10,11... | collective-permute-start | bytes 1081352 | tf_op jit(solution)/shard_map/ppermute | solution.py:274
  151.1 2.1 %collective-permute-start.19 = (bf16[2,64,1408]{2,1,0:T(8,128)(2,1)S(1)}, bf16[2,64,1408]{2,1,0:T(8,128)(2,1)S(1)}, u32[]{:S(2)}, u32[]{:S(2)}) collective-permute-start(bf16[2,64,1408]{2,1,0:T(8,128)(2,1)S(1)} %collective-permute-done.18.p2), channel_id=1, source_target_pairs={{0,1},{1,0},{2,3},{3,2},{4,5},{5,4},{6,7},{7,6},{8,9},{9,8},{10,11... | collective-permute-start | bytes 1081352 | tf_op jit(solution)/shard_map/ppermute | solution.py:274
  (15 other events, 152.5 us)

commit v2 on v1

v2 whole, which is shorter than its diff:
```python
import jax
import jax.numpy as jnp
from jax import lax
from jax.experimental import pallas as pl
from jax.experimental.pallas import tpu as pltpu
from jax.sharding import PartitionSpec as P

HEAD_DIM = 88
SCALE = HEAD_DIM ** (-0.5)
LANES = 128
ADAPTER_SCALE = 2.0
F32 = jnp.float32
BF16 = jnp.bfloat16
ANY = pl.BlockSpec(memory_space=pl.ANY)
VMEM = pl.BlockSpec(memory_space=pltpu.VMEM)
SMEM = pl.BlockSpec(memory_space=pltpu.SMEM)
VMEM_LIMIT = 24 * 1024 * 1024


def dot_nn(a, b):
    return lax.dot_general(a, b, (((1,), (0,)), ((), ())), preferred_element_type=F32)


def dot_nt(a, b):
    return lax.dot_general(a, b, (((1,), (1,)), ((), ())), preferred_element_type=F32)


def normalize(values, gain):
    average = jnp.mean(values, axis=-1, keepdims=True)
    centered = values - average
    spread = jnp.mean(centered * centered, axis=-1, keepdims=True)
    return centered * lax.rsqrt(spread + 1e-05) * gain.reshape(1, -1)


def in_hbm(x):
    return pltpu.with_memory_space_constraint(x, pltpu.HBM)


def in_vmem(x):
    return pltpu.with_memory_space_constraint(x, pltpu.VMEM)


def project_qkv(normed, w_ref, arrived=lambda i: None):
    arrived(0)
    queries_t = dot_nt(w_ref[0], normed)
    arrived(1)
    keys = dot_nt(normed, w_ref[1]).astype(BF16)
    arrived(2)
    values_t = dot_nt(w_ref[2], normed)
    return queries_t, keys, values_t


def attend_t(queries_t, keys, values_t, hidden_keys):
    width = queries_t.shape[0]
    outs = []
    for h in range(width // HEAD_DIM):
        first, last = h * HEAD_DIM, (h + 1) * HEAD_DIM
        low = first // LANES * LANES
        high = min(width, -(-last // LANES) * LANES)
        window = queries_t[low:high]
        row = lax.broadcasted_iota(jnp.int32, window.shape, 0) + low
        window = jnp.where((row >= first) & (row < last), window, 0.0).astype(BF16)
        scores = dot_nn(keys[:, low:high], window) * SCALE
        if hidden_keys is not None:
            scores = jnp.where(hidden_keys, -jnp.inf, scores)
        highest = jnp.max(scores, axis=0, keepdims=True)
        weights = jnp.exp(scores - highest)
        total = jnp.sum(weights, axis=0, keepdims=True)
        mixed = dot_nn(values_t[first:last].astype(BF16), weights.astype(BF16))
        outs.append(mixed * (1.0 / total))
    return jnp.transpose(jnp.concatenate(outs, axis=0))


def spatial_kernel(*refs):
    x_hbm, gain_hbm, w_hbm, out_w_hbm, own, far, send = refs[:7]
    gain_ref, w_ref, out_w_ref, x_ref, mixed, sems = refs[7:]
    frames, patches, _ = x_ref.shape
    share = own.shape[1]
    pairs = [(gain_hbm, gain_ref)]
    pairs += [(x_hbm.at[f], x_ref.at[f]) for f in range(frames)]
    pairs += [(w_hbm.at[i], w_ref.at[i]) for i in range(3)] + [(out_w_hbm, out_w_ref)]
    copies = [pltpu.make_async_copy(s, t, sems.at[i]) for i, (s, t) in enumerate(pairs)]
    first, weights, last = copies[: 1 + frames], copies[1 + frames : 4 + frames], copies[-1]
    first[0].start()
    first[1].start()
    weights[0].start()
    first[0].wait()
    normed = []
    for f in range(frames):
        first[1 + f].wait()
        if f + 1 < frames:
            first[2 + f].start()
        else:
            weights[1].start()
        normed.append(normalize(x_ref[f].astype(F32), gain_ref[...]).astype(BF16))
    normed = jnp.concatenate(normed, axis=0)

    def arrived(i):
        weights[i].wait()
        if i == 0:
            weights[2].start()
        elif i == 1:
            last.start()

    queries_t, keys, values_t = project_qkv(normed, w_ref, arrived)
    for f in range(frames):
        rows = slice(f * patches, (f + 1) * patches)
        mixed[f] = attend_t(queries_t[:, rows], keys[rows], values_t[:, rows], None).astype(BF16)
    last.wait()
    me = lax.axis_index("tp")

    def rows_of(d):
        return pl.ds(pl.multiple_of(jnp.bitwise_xor(me, d) * share, share), share)

    for f in range(frames):
        for d, out in ((1, send.at[0]), (3, send.at[1]), (2, far), (0, own)):
            term = dot_nn(mixed[f, rows_of(d)], out_w_ref[...])
            if d == 0:
                term = x_ref[f, rows_of(0)].astype(F32) + term
            out[f] = term.astype(out.dtype)


def spatial_call(video, gain, weight_t, out_weight):
    frames, patches, model = video.shape
    width = out_weight.shape[0]
    share = patches // 4
    return pl.pallas_call(
        spatial_kernel,
        out_shape=[
            jax.ShapeDtypeStruct((frames, share, model), F32),
            jax.ShapeDtypeStruct((frames, share, model), BF16),
            jax.ShapeDtypeStruct((2, frames, share, model), BF16),
        ],
        in_specs=[ANY] * 4,
        out_specs=[VMEM] * 3,
        scratch_shapes=[
            pltpu.VMEM(gain.shape, F32),
            pltpu.VMEM(weight_t.shape, BF16),
            pltpu.VMEM(out_weight.shape, BF16),
            pltpu.VMEM(video.shape, BF16),
            pltpu.VMEM((frames, patches, width), BF16),
            pltpu.SemaphoreType.DMA((5 + frames,)),
        ],
        compiler_params=pltpu.CompilerParams(vmem_limit_bytes=VMEM_LIMIT),
        name="spatial_attention",
    )(*(in_hbm(x) for x in (video, gain, weight_t, out_weight)))


def one_hot_rows(rows, source):
    i = lax.broadcasted_iota(jnp.int32, (rows, rows), 0)
    j = lax.broadcasted_iota(jnp.int32, (rows, rows), 1)
    return jnp.where(source(i) == j, 1.0, 0.0).astype(BF16)


def stream_kernel(own, recv, other, out):
    frames, share, model = own.shape
    stream = own[...] + recv[0].astype(F32) + other[...].astype(F32)
    stream = stream.astype(BF16).reshape(frames * share, model)
    order = one_hot_rows(frames * share, lambda i: (i % frames) * share + i // frames)
    out[...] = dot_nn(order, stream).astype(BF16)


def stream_call(own, recv, other):
    frames, share, model = own.shape
    return pl.pallas_call(
        stream_kernel,
        out_shape=jax.ShapeDtypeStruct((frames * share, model), BF16),
        in_specs=[VMEM] * 3,
        out_specs=VMEM,
        compiler_params=pltpu.CompilerParams(vmem_limit_bytes=VMEM_LIMIT),
        name="stream",
    )(own, recv, other)


def temporal_kernel(valid_ref, *refs):
    count = len(refs) // 2 - 1
    inputs, (gain_ref, w_ref), outs = refs[:count], refs[count : count + 2], refs[count + 2 :]
    frames = inputs[0].shape[0]
    hidden = lax.broadcasted_iota(jnp.int32, (frames, frames), 0) >= valid_ref[0]
    x = jnp.concatenate([ref[...].astype(F32) for ref in inputs], axis=0)
    normed = normalize(x, gain_ref[...]).astype(BF16)
    queries_t, keys, values_t = project_qkv(normed, w_ref)
    for d in range(count):
        rows = slice(d * frames, (d + 1) * frames)
        outs[d][...] = attend_t(
            queries_t[:, rows], keys[rows], values_t[:, rows], hidden
        ).astype(BF16)


def temporal_call(valid, quarters, gain, weight_t):
    frames = quarters[0].shape[0]
    width = weight_t.shape[1]
    return pl.pallas_call(
        temporal_kernel,
        out_shape=[jax.ShapeDtypeStruct((frames, width), BF16)] * len(quarters),
        in_specs=[SMEM] + [VMEM] * (len(quarters) + 2),
        out_specs=[VMEM] * len(quarters),
        compiler_params=pltpu.CompilerParams(vmem_limit_bytes=VMEM_LIMIT),
        name="temporal_attention",
    )(valid, *quarters, gain, weight_t)


def near_out_call(base, parts, weights, later_weights):
    count = len(parts)

    def kernel(*refs):
        base_ref, part_refs, refs = refs[0], refs[1 : 1 + count], refs[1 + count :]
        weight_refs, later, (out, *later_out) = refs[:count], refs[count : 2 * count], refs[2 * count : -1]
        copies = [
            pltpu.make_async_copy(x, y, refs[-1].at[i])
            for i, (x, y) in enumerate(zip(later, later_out))
        ]
        for copy in copies:
            copy.start()
        total = base_ref[...].astype(F32)
        for part, weight in zip(part_refs, weight_refs):
            total = total + dot_nn(part[...], weight[...])
        out[...] = total
        for copy in copies:
            copy.wait()

    return pl.pallas_call(
        kernel,
        out_shape=[jax.ShapeDtypeStruct(base.shape, F32)]
        + [jax.ShapeDtypeStruct(w.shape, BF16) for w in later_weights],
        in_specs=[VMEM] * (1 + 2 * count) + [ANY] * count,
        out_specs=[VMEM] * (1 + count),
        scratch_shapes=[pltpu.SemaphoreType.DMA((count,))],
        compiler_params=pltpu.CompilerParams(vmem_limit_bytes=VMEM_LIMIT),
        name="temporal_output_near",
    )(base, *parts, *weights, *later_weights)


def far_out_call(base, parts, weights):
    count = len(parts)

    def kernel(*refs):
        total = refs[0][...]
        for part, weight in zip(refs[1 : 1 + count], refs[1 + count : -1]):
            total = total + dot_nn(part[...], weight[...])
        refs[-1][...] = total.astype(BF16)

    return pl.pallas_call(
        kernel,
        out_shape=jax.ShapeDtypeStruct(base.shape, BF16),
        in_specs=[VMEM] * (1 + 2 * count),
        out_specs=VMEM,
        compiler_params=pltpu.CompilerParams(vmem_limit_bytes=VMEM_LIMIT),
        name="temporal_output_far",
    )(base, *parts, *weights)


def after(x, token):
    def kernel(x_ref, token_ref, out_ref):
        del token_ref
        out_ref[...] = x_ref[...]

    return pl.pallas_call(
        kernel,
        out_shape=jax.ShapeDtypeStruct(x.shape, x.dtype),
        in_specs=[VMEM, ANY],
        out_specs=VMEM,
        compiler_params=pltpu.CompilerParams(vmem_limit_bytes=VMEM_LIMIT // 8),
        name="after",
    )(x, token)


def ordered_rows(x_ref, frames, share):
    order = one_hot_rows(frames * share, lambda i: (i % share) * frames + i // share)
    return dot_nn(order, x_ref[...])


def order_call(mixed, gain, frames):
    rows, model = mixed.shape
    share = rows // frames

    def kernel(x_ref, gain_ref, piece, sums):
        ordered = ordered_rows(x_ref, frames, share)
        closing = normalize(ordered, gain_ref[...])
        for f in range(frames):
            part = slice(f * share, (f + 1) * share)
            piece[f] = ordered[part].astype(BF16)
            sums[f : f + 1] = jnp.sum(closing[part], axis=0, keepdims=True)

    return pl.pallas_call(
        kernel,
        out_shape=[
            jax.ShapeDtypeStruct((frames, share, model), BF16),
            jax.ShapeDtypeStruct((frames, model), F32),
        ],
        in_specs=[VMEM] * 2,
        out_specs=[VMEM] * 2,
        compiler_params=pltpu.CompilerParams(vmem_limit_bytes=VMEM_LIMIT),
        name="closing_order",
    )(mixed, gain)


def head_call(policy, sums, weight_t, down_t, up, vector, patches, token):
    frames = sums[0].shape[0]

    def kernel(policy_ref, s0, s1, s2, s3, w_ref, down, up, vector, token_ref, out):
        del token_ref
        pooled = ((s0[...] + s1[...] + s2[...] + s3[...]) * (1.0 / patches)).astype(BF16)
        lowrank = dot_nt(pooled, down[policy_ref[0]]).astype(BF16)
        hidden = dot_nt(pooled, w_ref[...]) + ADAPTER_SCALE * dot_nn(lowrank, up[policy_ref[0]])
        activated = jax.nn.gelu(hidden, approximate=True)
        score = jnp.sum(activated * vector[...].astype(F32), axis=-1, keepdims=True)
        out[...] = jnp.broadcast_to(score, out.shape)

    return pl.pallas_call(
        kernel,
        out_shape=jax.ShapeDtypeStruct((frames, LANES), F32),
        in_specs=[SMEM] + [VMEM] * 8 + [ANY],
        out_specs=VMEM,
        compiler_params=pltpu.CompilerParams(vmem_limit_bytes=VMEM_LIMIT),
        name="scoring_head",
    )(policy, *sums, weight_t, down_t, up, vector, token)


def assemble_call(pieces):
    frames, share, model = pieces[0].shape

    def kernel(*refs):
        me = lax.axis_index("tp")
        for d, piece in enumerate(refs[:-1]):
            start = pl.multiple_of(jnp.bitwise_xor(me, d) * share, share)
            refs[-1][:, pl.ds(start, share), :] = piece[...]

    return pl.pallas_call(
        kernel,
        out_shape=jax.ShapeDtypeStruct((frames, len(pieces) * share, model), BF16),
        in_specs=[VMEM] * len(pieces),
        out_specs=VMEM,
        compiler_params=pltpu.CompilerParams(vmem_limit_bytes=VMEM_LIMIT),
        name="assemble",
    )(*pieces)


def peer(x, d):
    return lax.ppermute(x, "tp", [(i, i ^ d) for i in range(4)])


def exchange_four(parts):
    return [parts[0], *(peer(parts[d], d) for d in (1, 2, 3))]


def across(x):
    pairs = [
        (s * 4 + t, (s ^ 1) * 4 + (t ^ 2)) for s in range(lax.axis_size("seq")) for t in range(4)
    ]
    return lax.ppermute(x, ("seq", "tp"), pairs)


def shards(
    video,
    spatial_norm_gain,
    spatial_query_key_value,
    spatial_output_weight,
    temporal_norm_gain,
    temporal_query_key_value,
    temporal_output_weight,
    closing_norm_gain,
    scoring_hidden_weight,
    adapter_down_weight,
    adapter_up_weight,
    scoring_vector,
    policy,
    valid_frame_count,
):
    frames_here, patches, model = video.shape
    width = spatial_output_weight.shape[0]
    seq = lax.axis_size("seq")

    def turned(weight):
        return jnp.transpose(weight, (1, 2, 0))

    def over_seq(x):
        rows = x.shape[0]
        blocks = x.reshape(seq, rows // seq, model)
        return lax.all_to_all(blocks, "seq", 0, 0, tiled=True).reshape(rows, model)

    own, far, send = spatial_call(
        video, spatial_norm_gain, turned(spatial_query_key_value), spatial_output_weight
    )
    recv = peer(send, 1)
    pair_term = (far.astype(F32) + recv[1].astype(F32)).astype(BF16)
    stream = stream_call(own, recv, peer(pair_term, 2))
    other_weight = across(temporal_output_weight)
    temporal_weights = [
        temporal_output_weight,
        peer(temporal_output_weight, 1),
        other_weight,
        peer(other_weight, 1),
    ]
    moved = over_seq(stream)
    core, chip = peer(moved, 1), peer(moved, 2)
    temporal_qkv = turned(temporal_query_key_value)

    def temporal(quarters):
        return temporal_call(valid_frame_count, quarters, temporal_norm_gain, temporal_qkv)

    near = temporal([moved, core])
    chip = after(chip, near[0])
    last = peer(chip, 1)
    mixed = exchange_four([*near, *temporal([chip]), *temporal([last])])
    updated, *far_weights = near_out_call(
        moved, mixed[:2], temporal_weights[:2], temporal_weights[2:]
    )
    updated = far_out_call(updated, mixed[2:], far_weights)
    returned = over_seq(updated)
    own, sums = order_call(returned, closing_norm_gain, frames_here)
    sums = exchange_four([sums] * 4)
    core, chip = peer(own, 1), peer(own, 2)
    blended = assemble_call([own, core, chip, peer(chip, 1)])
    scores = head_call(
        policy,
        sums,
        jnp.transpose(scoring_hidden_weight),
        jnp.transpose(adapter_down_weight, (0, 2, 1)),
        adapter_up_weight,
        scoring_vector.reshape(1, width),
        patches,
        chip,
    )
    score = sum(exchange_four([scores] * 4))[:, 0]
    frame_index = lax.axis_index("seq") * frames_here + jnp.arange(frames_here)
    reward = jnp.where(frame_index < valid_frame_count[0], score, jnp.float32(0.0))
    return (blended, reward)


def solution(mesh):
    in_specs = (
        P("seq", None, None),
        P(),
        P(None, None, "tp"),
        P("tp", None),
        P(),
        P(None, None, "tp"),
        P("tp", None),
        P(),
        P(None, "tp"),
        P(),
        P(None, None, "tp"),
        P("tp"),
        P(),
        P(),
    )
    out_specs = (P("seq", None, None), P("seq"))
    return jax.shard_map(shards, mesh=mesh, in_specs=in_specs, out_specs=out_specs, check_vma=False)
```

time: 200 us -> 117 us (0.58)
  Pallas kernels: 62.8 us -> 22.6 us
  waiting for transfers between devices: 69.8 us -> 34.7 us
  blocking collectives: 0 us -> 20.1 us
  local copies, waits for them, and re-layouts: 16.8 us -> 2.43 us
  starting transfers between devices: 47.4 us -> 33.9 us
    pallas_call x5 -> x7, Pallas kernels: 55.2 us -> 14.5 us  [the longest x1 8.91 us: spatial_call(): pl.pallas_call(spatial_kernel, out_shape=[jax.ShapeDtypeStruct((frames, s...]
    all_to_all x0 -> x1, blocking collectives: none -> 20.1 us  [over_seq(): return lax.all_to_all(blocks, 'seq', 0, 0, tiled=True).reshape(rows, model)]
    all_to_all x2 -> x1, waiting for transfers between devices: 25.2 us -> 11.7 us  [over_seq(): return lax.all_to_all(blocks, 'seq', 0, 0, tiled=True).reshape(rows, model)]
    ppermute x24 -> x19, waiting for transfers between devices: 35.7 us -> 23 us  [peer(): return lax.ppermute(x, 'tp', [(i, i ^ d) for i in range(4)])]
    unnamed x40 -> x14, local copies, waits for them, and re-layouts: 9.15 us -> 0.04 us
    ppermute x2 -> x1, waiting for transfers between devices: 8.88 us -> 0.01 us  [across(): return lax.ppermute(x, ('seq', 'tp'), pairs)]
    all_to_all x2 -> x1, starting transfers between devices: 20.1 us -> 12.8 us  [over_seq(): return lax.all_to_all(blocks, 'seq', 0, 0, tiled=True).reshape(rows, model)]
    ppermute x2 -> x1, starting transfers between devices: 4.91 us -> 1.03 us  [across(): return lax.ppermute(x, ('seq', 'tp'), pairs)]
  transfers between devices with their start and end apart: 28 -> 21, of which waited for: 15 -> 10; matrix products, arithmetic and copies ran while one was open for 3% -> 2% of each run, Pallas kernels for 8% -> 9%
where the time goes in v2:
time: 117 us
  waiting for transfers between devices  34.7 us (30%)
  starting transfers between devices  33.9 us (29%)
  Pallas kernels  22.6 us (19%)
  blocking collectives  20.1 us (17%)
  local copies, waits for them, and re-layouts  2.43 us (2%)
  between operations  2.15 us (2%)
    ppermute x19, waiting for transfers between devices, peer(): return lax.ppermute(x, 'tp', [(i, i ^ d) for i in range(4)])  23 us
    all_to_all x1, blocking collectives, over_seq(): return lax.all_to_all(blocks, 'seq', 0, 0, tiled=True).reshape(rows, model)  20.1 us
    ppermute x19, starting transfers between devices, peer(): return lax.ppermute(x, 'tp', [(i, i ^ d) for i in range(4)])  20.1 us
    all_to_all x1, starting transfers between devices, over_seq(): return lax.all_to_all(blocks, 'seq', 0, 0, tiled=True).reshape(rows, model)  12.8 us
    all_to_all x1, waiting for transfers between devices, over_seq(): return lax.all_to_all(blocks, 'seq', 0, 0, tiled=True).reshape(rows, model)  11.7 us
    pallas_call x1, Pallas kernels, spatial_call(): pl.pallas_call(spatial_kernel, out_shape=[jax.ShapeDtypeStruct((frames, s...  8.91 us
    pallas_call x3, Pallas kernels, temporal_call(): pl.pallas_call(temporal_kernel, out_shape=[jax.ShapeDtypeStruct((frames,...  7.42 us
    pallas_call x1, Pallas kernels, near_out_call(): pl.pallas_call(kernel, out_shape=[jax.ShapeDtypeStruct(base.shape, F32)]...  3.04 us
  transfers between devices with their start and end apart: 21, of which 10 were waited for; matrix products, arithmetic and copies ran while one was open for 2% of the time, Pallas kernels for 9%

profile of v2, /device:TPU:1, one launch (start us, length us, event | category | flops | bytes accessed | tf_op | source)
XLA Modules:
  0.0 116.5 jit_solution(891709214833996831)
XLA Ops:
  0.6 8.9 %spatial_attention.1 = (f32[2,64,1408]{2,1,0:T(8,128)S(1)}, bf16[2,64,1408]{2,1,0:T(8,128)(2,1)S(1)}, bf16[2,2,64,1408]{3,2,1,0:T(8,128)(2,1)S(1)}) custom-call(bf16[2,256,1408]{2,1,0:T(8,128)(2,1)} %refs_0_.1, f32[1408]{0:T(1024)} %refs_1_.3, bf16[3,352,1408]{2,1,0:T(8,128)(2,1)} %bitcast.16, bf16[352,1408]{1,0:T(8,128)(2,1)} %refs_3_.2), custom_call_target="tpu_custom_call" | custom-call | tf_op jit(solution)/shard_map/spatial_attention/pallas_call | solution.py:127
  9.6 3.3 %collective-permute-start = (bf16[2,2,64,1408]{3,2,1,0:T(8,128)(2,1)S(1)}, bf16[2,2,64,1408]{3,2,1,0:T(8,128)(2,1)S(1)}, u32[]{:S(2)}, u32[]{:S(2)}) collective-permute-start(bf16[2,2,64,1408]{3,2,1,0:T(8,128)(2,1)S(1)} %get-tuple-element.13), channel_id=1, source_target_pairs={{0,1},{1,0},{2,3},{3,2},{4,5},{5,4},{6,7},{7,6},{8,9},{9,8},{10,11... | collective-permute-start | bytes 2162696 | tf_op jit(solution)/shard_map/ppermute | solution.py:340
  12.9 1.0 collective-permute-start.5
  13.9 0.8 collective-permute-done.recv
  14.9 9.7 %collective-permute-done.1.other = bf16[2,64,1408]{2,1,0:T(8,128)(2,1)S(1)} collective-permute-done((bf16[2,64,1408]{2,1,0:T(8,128)(2,1)S(1)}, bf16[2,64,1408]{2,1,0:T(8,128)(2,1)S(1)}, u32[]{:S(2)}, u32[]{:S(2)}) %collective-permute-start.1) | collective-permute-done | bytes 360480 | tf_op jit(solution)/shard_map/ppermute | solution.py:340
  24.9 0.9 reshape.21
  25.8 12.8 %all-to-all-start = ((bf16[64,2,1408]{2,1,0:T(2,128)(2,1)}), bf16[64,2,1408]{2,1,0:T(2,128)(2,1)}, u32[]{:S(2)}, u32[]{:S(2)}) async-start(bf16[64,2,1408]{2,1,0:T(2,128)(2,1)} %reshape.21), calls=%async_computation | async-start | bytes 720896 | tf_op jit(solution)/shard_map/all_to_all | solution.py:380
  38.6 1.5 %collective-permute-start.4 = (bf16[352,1408]{1,0:T(8,128)(2,1)}, bf16[352,1408]{1,0:T(8,128)(2,1)}, u32[]{:S(2)}, u32[]{:S(2)}) collective-permute-start(bf16[352,1408]{1,0:T(8,128)(2,1)} %refs_3_.3), channel_id=1, source_target_pairs={{0,1},{1,0},{2,3},{3,2},{4,5},{5,4},{6,7},{7,6},{8,9},{9,8},{10,11... | collective-permute-start | bytes 2973704 | tf_op jit(solution)/shard_map/ppermute | solution.py:340
  40.2 11.7 %all-to-all-done = bf16[64,2,1408]{2,1,0:T(2,128)(2,1)} async-done(((bf16[64,2,1408]{2,1,0:T(2,128)(2,1)}), bf16[64,2,1408]{2,1,0:T(2,128)(2,1)}, u32[]{:S(2)}, u32[]{:S(2)}) %all-to-all-start) | async-done | bytes 360480 | tf_op jit(solution)/shard_map/all_to_all | solution.py:380
  51.8 1.1 reshape.22.refs_0_
  53.0 3.5 %collective-permute-start.2 = (bf16[128,1408]{1,0:T(8,128)(2,1)S(1)}, bf16[128,1408]{1,0:T(8,128)(2,1)S(1)}, u32[]{:S(2)}, u32[]{:S(2)}) collective-permute-start(bf16[128,1408]{1,0:T(8,128)(2,1)S(1)} %reshape.22.refs_0_), channel_id=1, source_target_pairs={{0,1},{1,0},{2,3},{3,2},{4,5},{5,4},{6,7},{7,6},{8,9},{9,8},{10,11... | collective-permute-start | bytes 1081352 | tf_op jit(solution)/shard_map/ppermute | solution.py:340
  57.7 3.2 %temporal_attention.3 = (bf16[128,352]{1,0:T(8,128)(2,1)S(1)}, bf16[128,352]{1,0:T(8,128)(2,1)S(1)}) custom-call(s32[1]{0:T(128)} %copy.17.valid_ref, bf16[128,1408]{1,0:T(8,128)(2,1)S(1)} %reshape.22.refs_0_, bf16[128,1408]{1,0:T(8,128)(2,1)S(1)} %collective-permute-done.2.refs_1_, f32[1408]{0:T(1024)S(1)} %copy-done.4, bf16[3,352,1408]{2,1,0:T(8,128)(2,1)S(1)} %bitcast.11), custom_call_target="tpu_custom_call" | custom-call | tf_op jit(solution)/shard_map/temporal_attention/pallas_call | solution.py:193
  61.0 5.2 %collective-permute-done.7.x_ref = bf16[128,1408]{1,0:T(8,128)(2,1)S(1)} collective-permute-done((bf16[128,1408]{1,0:T(8,128)(2,1)S(1)}, bf16[128,1408]{1,0:T(8,128)(2,1)S(1)}, u32[]{:S(2)}, u32[]{:S(2)}) %collective-permute-start.7) | collective-permute-done | bytes 360480 | tf_op jit(solution)/shard_map/ppermute | solution.py:340
  66.2 1.2 %collective-permute-start.9 = (bf16[128,1408]{1,0:T(8,128)(2,1)S(1)}, bf16[128,1408]{1,0:T(8,128)(2,1)S(1)}, u32[]{:S(2)}, u32[]{:S(2)}) collective-permute-start(bf16[128,1408]{1,0:T(8,128)(2,1)S(1)} %after.1.refs_0_), channel_id=1, source_target_pairs={{0,1},{1,0},{2,3},{3,2},{4,5},{5,4},{6,7},{7,6},{8,9},{9,8},{10,11... | collective-permute-start | bytes 1081352 | tf_op jit(solution)/shard_map/ppermute | solution.py:340
  67.4 2.1 %temporal_attention.4 = bf16[128,352]{1,0:T(8,128)(2,1)S(1)} custom-call(s32[1]{0:T(128)} %copy.17.valid_ref, bf16[128,1408]{1,0:T(8,128)(2,1)S(1)} %after.1.refs_0_, f32[1408]{0:T(1024)S(1)} %copy-done.4, bf16[3,352,1408]{2,1,0:T(8,128)(2,1)S(1)} %bitcast.12), custom_call_target="tpu_custom_call" | custom-call | tf_op jit(solution)/shard_map/temporal_attention/pallas_call | solution.py:193
  70.1 2.1 %temporal_attention.5 = bf16[128,352]{1,0:T(8,128)(2,1)S(1)} custom-call(s32[1]{0:T(128)} %copy.17.valid_ref, bf16[128,1408]{1,0:T(8,128)(2,1)S(1)} %collective-permute-done.9.refs_0_, f32[1408]{0:T(1024)S(1)} %copy-done.4, bf16[3,352,1408]{2,1,0:T(8,128)(2,1)S(1)} %bitcast.13), custom_call_target="tpu_custom_call" | custom-call | tf_op jit(solution)/shard_map/temporal_attention/pallas_call | solution.py:193
  72.2 1.7 %collective-permute-start.10 = (bf16[128,352]{1,0:T(8,128)(2,1)S(1)}, bf16[128,352]{1,0:T(8,128)(2,1)S(1)}, u32[]{:S(2)}, u32[]{:S(2)}) collective-permute-start(bf16[128,352]{1,0:T(8,128)(2,1)S(1)} %temporal_attention.5), channel_id=1, source_target_pairs={{0,3},{1,2},{2,1},{3,0},{4,7},{5,6},{6,5},{7,4},{8,11},{9,10},{10,... | collective-permute-start | bytes 270344 | tf_op jit(solution)/shard_map/ppermute | solution.py:340
  73.9 3.0 %temporal_output_near.1 = (f32[128,1408]{1,0:T(8,128)S(1)}, bf16[352,1408]{1,0:T(8,128)(2,1)S(1)}, bf16[352,1408]{1,0:T(8,128)(2,1)S(1)}) custom-call(bf16[128,1408]{1,0:T(8,128)(2,1)S(1)} %reshape.22.refs_0_, bf16[128,352]{1,0:T(8,128)(2,1)S(1)} %get-tuple-element.15.refs_1_.token_ref, bf16[128,352]{1,0:T(8,128)(2,1)S(1)} %collective-permute-done.3.refs_2_, ...), custom_call_target="tpu_custom_call" | custom-call | tf_op jit(solution)/shard_map/temporal_output_near/pallas_call | solution.py:222
  77.1 0.6 collective-permute-done.10.refs_2_
  77.7 0.6 temporal_output_far.1
  78.4 20.1 %all_to_all.10 = bf16[64,2,1408]{2,1,0:T(2,128)(2,1)S(1)} all-to-all(bf16[64,2,1408]{2,1,0:T(2,128)(2,1)S(1)} %reshape.23), channel_id=1, replica_groups=mesh['seq'=64,'tp'=4] {'seq'}, dimensions={0} | all-to-all | bytes 720896 | tf_op jit(solution)/shard_map/all_to_all | solution.py:380
  98.7 0.5 closing_order.1
  99.6 2.9 %collective-permute-start.14 = (f32[2,1408]{1,0:T(2,128)S(1)}, f32[2,1408]{1,0:T(2,128)S(1)}, u32[]{:S(2)}, u32[]{:S(2)}) collective-permute-start(f32[2,1408]{1,0:T(2,128)S(1)} %get-tuple-element.21.s0), channel_id=1, source_target_pairs={{0,1},{1,0},{2,3},{3,2},{4,5},{5,4},{6,7},{7,6},{8,9},{9,8},{10,11... | collective-permute-start | bytes 33800 | tf_op jit(solution)/shard_map/ppermute | solution.py:340
  102.4 1.2 %collective-permute-start.15 = (f32[2,1408]{1,0:T(2,128)S(1)}, f32[2,1408]{1,0:T(2,128)S(1)}, u32[]{:S(2)}, u32[]{:S(2)}) collective-permute-start(f32[2,1408]{1,0:T(2,128)S(1)} %get-tuple-element.21.s0), channel_id=1, source_target_pairs={{0,2},{1,3},{2,0},{3,1},{4,6},{5,7},{6,4},{7,5},{8,10},{9,11},{10,... | collective-permute-start | bytes 33800 | tf_op jit(solution)/shard_map/ppermute | solution.py:340
  104.7 2.1 %collective-permute-done.15.s2 = f32[2,1408]{1,0:T(2,128)S(1)} collective-permute-done((f32[2,1408]{1,0:T(2,128)S(1)}, f32[2,1408]{1,0:T(2,128)S(1)}, u32[]{:S(2)}, u32[]{:S(2)}) %collective-permute-start.15) | collective-permute-done | bytes 11296 | tf_op jit(solution)/shard_map/ppermute | solution.py:340
  106.8 3.3 %collective-permute-done.16.s3 = f32[2,1408]{1,0:T(2,128)S(1)} collective-permute-done((f32[2,1408]{1,0:T(2,128)S(1)}, f32[2,1408]{1,0:T(2,128)S(1)}, u32[]{:S(2)}, u32[]{:S(2)}) %collective-permute-start.16) | collective-permute-done | bytes 11296 | tf_op jit(solution)/shard_map/ppermute | solution.py:340
  110.1 0.6 scoring_head.1
  110.7 0.6 collective-permute-start.17
  111.7 1.4 %collective-permute-start.19 = (f32[2,128]{1,0:T(2,128)S(1)}, f32[2,128]{1,0:T(2,128)S(1)}, u32[]{:S(2)}, u32[]{:S(2)}) collective-permute-start(f32[2,128]{1,0:T(2,128)S(1)} %scoring_head.1), channel_id=1, source_target_pairs={{0,3},{1,2},{2,1},{3,0},{4,7},{5,6},{6,5},{7,4},{8,11},{9,10},{10,... | collective-permute-start | bytes 3080 | tf_op jit(solution)/shard_map/ppermute | solution.py:340
  113.8 0.8 collective-permute-done.19
  114.8 0.5 compare_select_fusion
  115.3 1.2 %assemble.1 = bf16[2,256,1408]{2,1,0:T(8,128)(2,1)} custom-call(bf16[2,64,1408]{2,1,0:T(8,128)(2,1)S(1)} %get-tuple-element.20.refs_0_, bf16[2,64,1408]{2,1,0:T(8,128)(2,1)S(1)} %collective-permute-done.11.refs_1_, bf16[2,64,1408]{2,1,0:T(8,128)(2,1)S(1)} %collective-permute-done.12.refs_2_.token_ref, bf16[2,64,1408]{2,1,0:T(8,128)(2,1)S(1)} %collective-permute-done.13.refs_3_), custom_call_target="tpu_custom_call" | custom-call | tf_op jit(solution)/shard_map/assemble/pallas_call | solution.py:329
  (45 shorter events, 4.1 us)
Async XLA Ops:
  9.6 48.2 %copy-start = (bf16[1408,3,352]{0,2,1:T(8,128)(2,1)S(1)}, bf16[1408,3,352]{0,2,1:T(8,128)(2,1)}, u32[]{:S(2)}) copy-start(bf16[1408,3,352]{0,2,1:T(8,128)(2,1)} %param.19) | copy-start | bytes 8921092
  9.6 48.2 %copy-start.4 = (f32[1408]{0:T(1024)S(1)}, f32[1408]{0:T(1024)}, u32[]{:S(2)}) copy-start(f32[1408]{0:T(1024)} %refs_1_.5) | copy-start | bytes 16900
  9.6 5.1 %collective-permute-start = (bf16[2,2,64,1408]{3,2,1,0:T(8,128)(2,1)S(1)}, bf16[2,2,64,1408]{3,2,1,0:T(8,128)(2,1)S(1)}, u32[]{:S(2)}, u32[]{:S(2)}) collective-permute-start(bf16[2,2,64,1408]{3,2,1,0:T(8,128)(2,1)S(1)} %get-tuple-element.13), channel_id=1, source_target_pairs={{0,1},{1,0},{2,3},{3,2},{4,5},{5,4},{6,7},{7,6},{8,9},{9,8},{10,11... | collective-permute-start | bytes 2162696 | tf_op jit(solution)/shard_map/ppermute | solution.py:340
  12.9 27.1 %collective-permute-start.5 = (bf16[352,1408]{1,0:T(8,128)(2,1)}, bf16[352,1408]{1,0:T(8,128)(2,1)}, u32[]{:S(2)}, u32[]{:S(2)}) collective-permute-start(bf16[352,1408]{1,0:T(8,128)(2,1)} %refs_3_.3), channel_id=1, source_target_pairs={{0,6},{1,7},{2,4},{3,5},{4,2},{5,3},{6,0},{7,1},{8,14},{9,15},{10,... | collective-permute-start | bytes 2973704 | tf_op jit(solution)/shard_map/ppermute | solution.py:351
  14.8 9.8 %collective-permute-start.1 = (bf16[2,64,1408]{2,1,0:T(8,128)(2,1)S(1)}, bf16[2,64,1408]{2,1,0:T(8,128)(2,1)S(1)}, u32[]{:S(2)}, u32[]{:S(2)}) collective-permute-start(bf16[2,64,1408]{2,1,0:T(8,128)(2,1)S(1)} %fusion), channel_id=1, source_target_pairs={{0,2},{1,3},{2,0},{3,1},{4,6},{5,7},{6,4},{7,5},{8,10},{9,11},{10,... | collective-permute-start | bytes 1081352 | tf_op jit(solution)/shard_map/ppermute | solution.py:340
  25.8 26.1 %all-to-all-start = ((bf16[64,2,1408]{2,1,0:T(2,128)(2,1)}), bf16[64,2,1408]{2,1,0:T(2,128)(2,1)}, u32[]{:S(2)}, u32[]{:S(2)}) async-start(bf16[64,2,1408]{2,1,0:T(2,128)(2,1)} %reshape.21), calls=%async_computation | async-start | bytes 720896 | tf_op jit(solution)/shard_map/all_to_all | solution.py:380
  38.6 35.4 %collective-permute-start.4 = (bf16[352,1408]{1,0:T(8,128)(2,1)}, bf16[352,1408]{1,0:T(8,128)(2,1)}, u32[]{:S(2)}, u32[]{:S(2)}) collective-permute-start(bf16[352,1408]{1,0:T(8,128)(2,1)} %refs_3_.3), channel_id=1, source_target_pairs={{0,1},{1,0},{2,3},{3,2},{4,5},{5,4},{6,7},{7,6},{8,9},{9,8},{10,11... | collective-permute-start | bytes 2973704 | tf_op jit(solution)/shard_map/ppermute | solution.py:340
  40.0 33.9 %collective-permute-start.6 = (bf16[352,1408]{1,0:T(8,128)(2,1)}, bf16[352,1408]{1,0:T(8,128)(2,1)}, u32[]{:S(2)}, u32[]{:S(2)}) collective-permute-start(bf16[352,1408]{1,0:T(8,128)(2,1)} %collective-permute-done.5.refs_5_), channel_id=1, source_target_pairs={{0,1},{1,0},{2,3},{3,2},{4,5},{5,4},{6,7},{7,6},{8,9},{9,8},{10,11... | collective-permute-start | bytes 2973704 | tf_op jit(solution)/shard_map/ppermute | solution.py:340
  53.0 4.8 %collective-permute-start.2 = (bf16[128,1408]{1,0:T(8,128)(2,1)S(1)}, bf16[128,1408]{1,0:T(8,128)(2,1)S(1)}, u32[]{:S(2)}, u32[]{:S(2)}) collective-permute-start(bf16[128,1408]{1,0:T(8,128)(2,1)S(1)} %reshape.22.refs_0_), channel_id=1, source_target_pairs={{0,1},{1,0},{2,3},{3,2},{4,5},{5,4},{6,7},{7,6},{8,9},{9,8},{10,11... | collective-permute-start | bytes 1081352 | tf_op jit(solution)/shard_map/ppermute | solution.py:340
  56.4 9.7 %collective-permute-start.7 = (bf16[128,1408]{1,0:T(8,128)(2,1)S(1)}, bf16[128,1408]{1,0:T(8,128)(2,1)S(1)}, u32[]{:S(2)}, u32[]{:S(2)}) collective-permute-start(bf16[128,1408]{1,0:T(8,128)(2,1)S(1)} %reshape.22.refs_0_), channel_id=1, source_target_pairs={{0,2},{1,3},{2,0},{3,1},{4,6},{5,7},{6,4},{7,5},{8,10},{9,11},{10,... | collective-permute-start | bytes 1081352 | tf_op jit(solution)/shard_map/ppermute | solution.py:340
  66.2 3.9 %collective-permute-start.9 = (bf16[128,1408]{1,0:T(8,128)(2,1)S(1)}, bf16[128,1408]{1,0:T(8,128)(2,1)S(1)}, u32[]{:S(2)}, u32[]{:S(2)}) collective-permute-start(bf16[128,1408]{1,0:T(8,128)(2,1)S(1)} %after.1.refs_0_), channel_id=1, source_target_pairs={{0,1},{1,0},{2,3},{3,2},{4,5},{5,4},{6,7},{7,6},{8,9},{9,8},{10,11... | collective-permute-start | bytes 1081352 | tf_op jit(solution)/shard_map/ppermute | solution.py:340
  69.5 4.4 %collective-permute-start.3 = (bf16[128,352]{1,0:T(8,128)(2,1)S(1)}, bf16[128,352]{1,0:T(8,128)(2,1)S(1)}, u32[]{:S(2)}, u32[]{:S(2)}) collective-permute-start(bf16[128,352]{1,0:T(8,128)(2,1)S(1)} %get-tuple-element.16), channel_id=1, source_target_pairs={{0,1},{1,0},{2,3},{3,2},{4,5},{5,4},{6,7},{7,6},{8,9},{9,8},{10,11... | collective-permute-start | bytes 270344 | tf_op jit(solution)/shard_map/ppermute | solution.py:340
  69.6 7.5 %collective-permute-start.8 = (bf16[128,352]{1,0:T(8,128)(2,1)S(1)}, bf16[128,352]{1,0:T(8,128)(2,1)S(1)}, u32[]{:S(2)}, u32[]{:S(2)}) collective-permute-start(bf16[128,352]{1,0:T(8,128)(2,1)S(1)} %temporal_attention.4), channel_id=1, source_target_pairs={{0,2},{1,3},{2,0},{3,1},{4,6},{5,7},{6,4},{7,5},{8,10},{9,11},{10,... | collective-permute-start | bytes 270344 | tf_op jit(solution)/shard_map/ppermute | solution.py:340
  72.2 5.5 %collective-permute-start.10 = (bf16[128,352]{1,0:T(8,128)(2,1)S(1)}, bf16[128,352]{1,0:T(8,128)(2,1)S(1)}, u32[]{:S(2)}, u32[]{:S(2)}) collective-permute-start(bf16[128,352]{1,0:T(8,128)(2,1)S(1)} %temporal_attention.5), channel_id=1, source_target_pairs={{0,3},{1,2},{2,1},{3,0},{4,7},{5,6},{6,5},{7,4},{8,11},{9,10},{10,... | collective-permute-start | bytes 270344 | tf_op jit(solution)/shard_map/ppermute | solution.py:340
  77.0 21.7 %copy-start.5 = (f32[1408]{0:T(1024)S(1)}, f32[1408]{0:T(1024)}, u32[]{:S(2)}) copy-start(f32[1408]{0:T(1024)} %gain_ref.1) | copy-start | bytes 16900
  77.0 27.1 %copy-start.6 = (bf16[352]{0:T(512)(128)(2,1)S(1)}, bf16[352]{0:T(512)(128)(2,1)}, u32[]{:S(2)}) copy-start(bf16[352]{0:T(512)(128)(2,1)} %param.25) | copy-start | bytes 2116
  77.0 33.1 %copy-start.1 = (bf16[1408,352]{0,1:T(8,128)(2,1)S(1)}, bf16[1408,352]{0,1:T(8,128)(2,1)}, u32[]{:S(2)}) copy-start(bf16[1408,352]{0,1:T(8,128)(2,1)} %param.22) | copy-start | bytes 2973700
  77.0 33.1 %copy-start.2 = (bf16[8,1408,16]{1,2,0:T(8,128)(2,1)S(1)}, bf16[8,1408,16]{1,2,0:T(8,128)(2,1)}, u32[]{:S(2)}) copy-start(bf16[8,1408,16]{1,2,0:T(8,128)(2,1)} %param.23) | copy-start | bytes 1081348
  77.0 33.0 %copy-start.3 = (bf16[8,16,352]{2,1,0:T(8,128)(2,1)S(1)}, bf16[8,16,352]{2,1,0:T(8,128)(2,1)}, u32[]{:S(2)}) copy-start(bf16[8,16,352]{2,1,0:T(8,128)(2,1)} %up.1) | copy-start | bytes 270340
  99.2 10.9 %collective-permute-start.12 = (bf16[2,64,1408]{2,1,0:T(8,128)(2,1)S(1)}, bf16[2,64,1408]{2,1,0:T(8,128)(2,1)S(1)}, u32[]{:S(2)}, u32[]{:S(2)}) collective-permute-start(bf16[2,64,1408]{2,1,0:T(8,128)(2,1)S(1)} %get-tuple-element.20.refs_0_), channel_id=1, source_target_pairs={{0,2},{1,3},{2,0},{3,1},{4,6},{5,7},{6,4},{7,5},{8,10},{9,11},{10,... | collective-permute-start | bytes 1081352 | tf_op jit(solution)/shard_map/ppermute | solution.py:340
  99.6 5.2 %collective-permute-start.14 = (f32[2,1408]{1,0:T(2,128)S(1)}, f32[2,1408]{1,0:T(2,128)S(1)}, u32[]{:S(2)}, u32[]{:S(2)}) collective-permute-start(f32[2,1408]{1,0:T(2,128)S(1)} %get-tuple-element.21.s0), channel_id=1, source_target_pairs={{0,1},{1,0},{2,3},{3,2},{4,5},{5,4},{6,7},{7,6},{8,9},{9,8},{10,11... | collective-permute-start | bytes 33800 | tf_op jit(solution)/shard_map/ppermute | solution.py:340
  102.4 4.4 %collective-permute-start.15 = (f32[2,1408]{1,0:T(2,128)S(1)}, f32[2,1408]{1,0:T(2,128)S(1)}, u32[]{:S(2)}, u32[]{:S(2)}) collective-permute-start(f32[2,1408]{1,0:T(2,128)S(1)} %get-tuple-element.21.s0), channel_id=1, source_target_pairs={{0,2},{1,3},{2,0},{3,1},{4,6},{5,7},{6,4},{7,5},{8,10},{9,11},{10,... | collective-permute-start | bytes 33800 | tf_op jit(solution)/shard_map/ppermute | solution.py:340
  103.6 6.4 %collective-permute-start.16 = (f32[2,1408]{1,0:T(2,128)S(1)}, f32[2,1408]{1,0:T(2,128)S(1)}, u32[]{:S(2)}, u32[]{:S(2)}) collective-permute-start(f32[2,1408]{1,0:T(2,128)S(1)} %get-tuple-element.21.s0), channel_id=1, source_target_pairs={{0,3},{1,2},{2,1},{3,0},{4,7},{5,6},{6,5},{7,4},{8,11},{9,10},{10,... | collective-permute-start | bytes 33800 | tf_op jit(solution)/shard_map/ppermute | solution.py:340
  110.7 2.9 %collective-permute-start.17 = (f32[2,128]{1,0:T(2,128)S(1)}, f32[2,128]{1,0:T(2,128)S(1)}, u32[]{:S(2)}, u32[]{:S(2)}) collective-permute-start(f32[2,128]{1,0:T(2,128)S(1)} %scoring_head.1), channel_id=1, source_target_pairs={{0,1},{1,0},{2,3},{3,2},{4,5},{5,4},{6,7},{7,6},{8,9},{9,8},{10,11... | collective-permute-start | bytes 3080 | tf_op jit(solution)/shard_map/ppermute | solution.py:340
  111.4 2.4 %collective-permute-start.18 = (f32[2,128]{1,0:T(2,128)S(1)}, f32[2,128]{1,0:T(2,128)S(1)}, u32[]{:S(2)}, u32[]{:S(2)}) collective-permute-start(f32[2,128]{1,0:T(2,128)S(1)} %scoring_head.1), channel_id=1, source_target_pairs={{0,2},{1,3},{2,0},{3,1},{4,6},{5,7},{6,4},{7,5},{8,10},{9,11},{10,... | collective-permute-start | bytes 3080 | tf_op jit(solution)/shard_map/ppermute | solution.py:340
  111.7 3.0 %collective-permute-start.19 = (f32[2,128]{1,0:T(2,128)S(1)}, f32[2,128]{1,0:T(2,128)S(1)}, u32[]{:S(2)}, u32[]{:S(2)}) collective-permute-start(f32[2,128]{1,0:T(2,128)S(1)} %scoring_head.1), channel_id=1, source_target_pairs={{0,3},{1,2},{2,1},{3,0},{4,7},{5,6},{6,5},{7,4},{8,11},{9,10},{10,... | collective-permute-start | bytes 3080 | tf_op jit(solution)/shard_map/ppermute | solution.py:340
  113.1 2.2 %collective-permute-start.11 = (bf16[2,64,1408]{2,1,0:T(8,128)(2,1)S(1)}, bf16[2,64,1408]{2,1,0:T(8,128)(2,1)S(1)}, u32[]{:S(2)}, u32[]{:S(2)}) collective-permute-start(bf16[2,64,1408]{2,1,0:T(8,128)(2,1)S(1)} %get-tuple-element.20.refs_0_), channel_id=1, source_target_pairs={{0,1},{1,0},{2,3},{3,2},{4,5},{5,4},{6,7},{7,6},{8,9},{9,8},{10,11... | collective-permute-start | bytes 1081352 | tf_op jit(solution)/shard_map/ppermute | solution.py:340
  113.3 2.1 %collective-permute-start.13 = (bf16[2,64,1408]{2,1,0:T(8,128)(2,1)S(1)}, bf16[2,64,1408]{2,1,0:T(8,128)(2,1)S(1)}, u32[]{:S(2)}, u32[]{:S(2)}) collective-permute-start(bf16[2,64,1408]{2,1,0:T(8,128)(2,1)S(1)} %collective-permute-done.12.refs_2_.token_ref), channel_id=1, source_target_pairs={{0,1},{1,0},{2,3},{3,2},{4,5},{5,4},{6,7},{7,6},{8,9},{9,8},{10,11... | collective-permute-start | bytes 1081352 | tf_op jit(solution)/shard_map/ppermute | solution.py:340

commit v3 on v2

--- a/solution.py
+++ b/solution.py
@@ -1,3 +1,5 @@
+import math
+
 import jax
 import jax.numpy as jnp
 from jax import lax
@@ -6,7 +8,7 @@
 from jax.sharding import PartitionSpec as P
 
 HEAD_DIM = 88
-SCALE = HEAD_DIM ** (-0.5)
+SCALE = HEAD_DIM ** (-0.5) * math.log2(math.e)
 LANES = 128
 ADAPTER_SCALE = 2.0
 F32 = jnp.float32
@@ -44,31 +46,38 @@
     arrived(0)
     queries_t = dot_nt(w_ref[0], normed)
     arrived(1)
-    keys = dot_nt(normed, w_ref[1]).astype(BF16)
+    keys = jnp.transpose(dot_nt(w_ref[1], normed)).astype(BF16)
     arrived(2)
     values_t = dot_nt(w_ref[2], normed)
     return queries_t, keys, values_t
 
 
-def attend_t(queries_t, keys, values_t, hidden_keys):
+def attend_t(queries_t, keys, values_t, groups, hidden_keys):
     width = queries_t.shape[0]
-    outs = []
-    for h in range(width // HEAD_DIM):
-        first, last = h * HEAD_DIM, (h + 1) * HEAD_DIM
-        low = first // LANES * LANES
-        high = min(width, -(-last // LANES) * LANES)
-        window = queries_t[low:high]
-        row = lax.broadcasted_iota(jnp.int32, window.shape, 0) + low
-        window = jnp.where((row >= first) & (row < last), window, 0.0).astype(BF16)
-        scores = dot_nn(keys[:, low:high], window) * SCALE
-        if hidden_keys is not None:
-            scores = jnp.where(hidden_keys, -jnp.inf, scores)
-        highest = jnp.max(scores, axis=0, keepdims=True)
-        weights = jnp.exp(scores - highest)
-        total = jnp.sum(weights, axis=0, keepdims=True)
-        mixed = dot_nn(values_t[first:last].astype(BF16), weights.astype(BF16))
-        outs.append(mixed * (1.0 / total))
-    return jnp.transpose(jnp.concatenate(outs, axis=0))
+    heads = [(h * HEAD_DIM, (h + 1) * HEAD_DIM) for h in range(width // HEAD_DIM)]
+    scores = {}
+    for rows in groups:
+        for first, last in heads:
+            low = first // LANES * LANES
+            high = min(width, -(-last // LANES) * LANES)
+            window = queries_t[low:high, rows]
+            row = lax.broadcasted_iota(jnp.int32, window.shape, 0) + low
+            window = jnp.where((row >= first) & (row < last), window * SCALE, 0.0).astype(BF16)
+            score = dot_nn(keys[rows, low:high], window)
+            if hidden_keys is not None:
+                score = jnp.where(hidden_keys, -jnp.inf, score)
+            scores[rows.start, first] = score
+    mixed = []
+    for rows in groups:
+        weights = [scores[rows.start, first] for first, _ in heads]
+        weights = [jnp.exp2(s - jnp.max(s, axis=0, keepdims=True)) for s in weights]
+        totals = [jnp.sum(w, axis=0, keepdims=True) for w in weights]
+        outs = [
+            dot_nn(values_t[first:last, rows].astype(BF16), w.astype(BF16)) * (1.0 / t)
+            for (first, last), w, t in zip(heads, weights, totals)
+        ]
+        mixed.append(jnp.transpose(jnp.concatenate(outs, axis=0)))
+    return mixed
 
 
 def spatial_kernel(*refs):
@@ -81,31 +90,26 @@
     pairs += [(w_hbm.at[i], w_ref.at[i]) for i in range(3)] + [(out_w_hbm, out_w_ref)]
     copies = [pltpu.make_async_copy(s, t, sems.at[i]) for i, (s, t) in enumerate(pairs)]
     first, weights, last = copies[: 1 + frames], copies[1 + frames : 4 + frames], copies[-1]
-    first[0].start()
-    first[1].start()
-    weights[0].start()
+    for copy in [*first, weights[0]]:
+        copy.start()
     first[0].wait()
     normed = []
     for f in range(frames):
         first[1 + f].wait()
-        if f + 1 < frames:
-            first[2 + f].start()
-        else:
+        if f == 0:
             weights[1].start()
+            weights[2].start()
         normed.append(normalize(x_ref[f].astype(F32), gain_ref[...]).astype(BF16))
+    last.start()
     normed = jnp.concatenate(normed, axis=0)
 
     def arrived(i):
         weights[i].wait()
-        if i == 0:
-            weights[2].start()
-        elif i == 1:
-            last.start()
 
     queries_t, keys, values_t = project_qkv(normed, w_ref, arrived)
-    for f in range(frames):
-        rows = slice(f * patches, (f + 1) * patches)
-        mixed[f] = attend_t(queries_t[:, rows], keys[rows], values_t[:, rows], None).astype(BF16)
+    groups = [slice(f * patches, (f + 1) * patches) for f in range(frames)]
+    for f, result in enumerate(attend_t(queries_t, keys, values_t, groups, None)):
+        mixed[f] = result.astype(BF16)
     last.wait()
     me = lax.axis_index("tp")
 
@@ -172,63 +176,68 @@
     )(own, recv, other)
 
 
-def temporal_kernel(valid_ref, *refs):
-    count = len(refs) // 2 - 1
-    inputs, (gain_ref, w_ref), outs = refs[:count], refs[count : count + 2], refs[count + 2 :]
-    frames = inputs[0].shape[0]
-    hidden = lax.broadcasted_iota(jnp.int32, (frames, frames), 0) >= valid_ref[0]
-    x = jnp.concatenate([ref[...].astype(F32) for ref in inputs], axis=0)
-    normed = normalize(x, gain_ref[...]).astype(BF16)
-    queries_t, keys, values_t = project_qkv(normed, w_ref)
-    for d in range(count):
-        rows = slice(d * frames, (d + 1) * frames)
-        outs[d][...] = attend_t(
-            queries_t[:, rows], keys[rows], values_t[:, rows], hidden
-        ).astype(BF16)
-
-
-def temporal_call(valid, quarters, gain, weight_t):
+def temporal_call(valid, quarters, gain, weight_t, sides):
+    count, extra = len(quarters), len(sides)
     frames = quarters[0].shape[0]
     width = weight_t.shape[1]
-    return pl.pallas_call(
-        temporal_kernel,
-        out_shape=[jax.ShapeDtypeStruct((frames, width), BF16)] * len(quarters),
-        in_specs=[SMEM] + [VMEM] * (len(quarters) + 2),
-        out_specs=[VMEM] * len(quarters),
-        compiler_params=pltpu.CompilerParams(vmem_limit_bytes=VMEM_LIMIT),
-        name="temporal_attention",
-    )(valid, *quarters, gain, weight_t)
-
-
-def near_out_call(base, parts, weights, later_weights):
-    count = len(parts)
-
-    def kernel(*refs):
-        base_ref, part_refs, refs = refs[0], refs[1 : 1 + count], refs[1 + count :]
-        weight_refs, later, (out, *later_out) = refs[:count], refs[count : 2 * count], refs[2 * count : -1]
+
+    def kernel(valid_ref, *refs):
+        inputs, (gain_ref, w_ref), refs = refs[:count], refs[count : count + 2], refs[count + 2 :]
+        outs = refs[extra : extra + count]
         copies = [
-            pltpu.make_async_copy(x, y, refs[-1].at[i])
-            for i, (x, y) in enumerate(zip(later, later_out))
+            pltpu.make_async_copy(refs[i], refs[extra + count + i], refs[-1].at[i])
+            for i in range(extra)
         ]
         for copy in copies:
             copy.start()
+        hidden = lax.broadcasted_iota(jnp.int32, (frames, frames), 0) >= valid_ref[0]
+        x = jnp.concatenate([ref[...].astype(F32) for ref in inputs], axis=0)
+        normed = normalize(x, gain_ref[...]).astype(BF16)
+        queries_t, keys, values_t = project_qkv(normed, w_ref)
+        groups = [slice(d * frames, (d + 1) * frames) for d in range(count)]
+        for out, result in zip(outs, attend_t(queries_t, keys, values_t, groups, hidden)):
+            out[...] = result.astype(BF16)
+        for copy in copies:
+            copy.wait()
+
+    out_shape = [jax.ShapeDtypeStruct((frames, width), BF16)] * count
+    out_shape += [jax.ShapeDtypeStruct(x.shape, BF16) for x in sides]
+    return pl.pallas_call(
+        kernel,
+        out_shape=out_shape,
+        in_specs=[SMEM] + [VMEM] * (count + 2) + [ANY] * extra,
+        out_specs=[VMEM] * len(out_shape),
+        scratch_shapes=[pltpu.SemaphoreType.DMA((max(extra, 1),))],
+        compiler_params=pltpu.CompilerParams(vmem_limit_bytes=VMEM_LIMIT),
+        name="temporal_attention",
+    )(valid, *quarters, gain, weight_t, *sides)
+
+
+def near_out_call(base, parts, weights, side):
+    count = len(parts)
+
+    def kernel(*refs):
+        base_ref, side_hbm, out, side_ref, sem = refs[0], refs[-4], *refs[-3:]
+        copy = pltpu.make_async_copy(side_hbm, side_ref, sem)
+        copy.start()
         total = base_ref[...].astype(F32)
-        for part, weight in zip(part_refs, weight_refs):
+        for part, weight in zip(refs[1 : 1 + count], refs[1 + count : 1 + 2 * count]):
             total = total + dot_nn(part[...], weight[...])
         out[...] = total
-        for copy in copies:
-            copy.wait()
-
-    return pl.pallas_call(
-        kernel,
-        out_shape=[jax.ShapeDtypeStruct(base.shape, F32)]
-        + [jax.ShapeDtypeStruct(w.shape, BF16) for w in later_weights],
-        in_specs=[VMEM] * (1 + 2 * count) + [ANY] * count,
-        out_specs=[VMEM] * (1 + count),
-        scratch_shapes=[pltpu.SemaphoreType.DMA((count,))],
+        copy.wait()
+
+    return pl.pallas_call(
+        kernel,
+        out_shape=[
+            jax.ShapeDtypeStruct(base.shape, F32),
+            jax.ShapeDtypeStruct(side.shape, BF16),
+        ],
+        in_specs=[VMEM] * (1 + 2 * count) + [ANY],
+        out_specs=[VMEM] * 2,
+        scratch_shapes=[pltpu.SemaphoreType.DMA],
         compiler_params=pltpu.CompilerParams(vmem_limit_bytes=VMEM_LIMIT),
         name="temporal_output_near",
-    )(base, *parts, *weights, *later_weights)
+    )(base, *parts, *weights, side)
 
 
 def far_out_call(base, parts, weights):
@@ -386,27 +395,26 @@
     pair_term = (far.astype(F32) + recv[1].astype(F32)).astype(BF16)
     stream = stream_call(own, recv, peer(pair_term, 2))
     other_weight = across(temporal_output_weight)
-    temporal_weights = [
-        temporal_output_weight,
-        peer(temporal_output_weight, 1),
-        other_weight,
-        peer(other_weight, 1),
-    ]
     moved = over_seq(stream)
+    temporal_qkv = turned(temporal_query_key_value)
+
+    def temporal(quarters, *side):
+        return temporal_call(
+            valid_frame_count, quarters, temporal_norm_gain, temporal_qkv, side
+        )
+
     core, chip = peer(moved, 1), peer(moved, 2)
-    temporal_qkv = turned(temporal_query_key_value)
-
-    def temporal(quarters):
-        return temporal_call(valid_frame_count, quarters, temporal_norm_gain, temporal_qkv)
-
-    near = temporal([moved, core])
-    chip = after(chip, near[0])
-    last = peer(chip, 1)
-    mixed = exchange_four([*near, *temporal([chip]), *temporal([last])])
-    updated, *far_weights = near_out_call(
-        moved, mixed[:2], temporal_weights[:2], temporal_weights[2:]
+    mixed_own, weight_own, weight_chip = temporal(
+        [moved], temporal_output_weight, other_weight
     )
-    updated = far_out_call(updated, mixed[2:], far_weights)
+    chip = after(chip, mixed_own)
+    mixed_core, mixed_chip = temporal([core, chip])
+    (mixed_last,) = temporal([peer(chip, 1)])
+    mixed = exchange_four([mixed_own, mixed_core, mixed_chip, mixed_last])
+    updated, weight_last = near_out_call(
+        moved, mixed[:2], [weight_own, peer(temporal_output_weight, 1)], peer(other_weight, 1)
+    )
+    updated = far_out_call(updated, mixed[2:], [weight_chip, weight_last])
     returned = over_seq(updated)
     own, sums = order_call(returned, closing_norm_gain, frames_here)
     sums = exchange_four([sums] * 4)

time: 117 us -> 112 us (0.957)
  Pallas kernels: 22.6 us -> 17.4 us
  waiting for transfers between devices: 34.7 us -> 30.2 us
  starting transfers between devices: 33.9 us -> 37.2 us
  blocking collectives: 20.1 us -> 22.1 us
    ppermute x19, waiting for transfers between devices: 23 us -> 18.5 us  [peer(): return lax.ppermute(x, 'tp', [(i, i ^ d) for i in range(4)])]
    ppermute x19, starting transfers between devices: 20.1 us -> 23.4 us  [peer(): return lax.ppermute(x, 'tp', [(i, i ^ d) for i in range(4)])]
    pallas_call x4, Pallas kernels: 10.5 us -> 7.56 us  [the longest x3 5.11 us: temporal_call(): pl.pallas_call(kernel, out_shape=out_shape, in_specs=[SMEM] + [VMEM] * (c...]
    pallas_call x1, Pallas kernels: 8.91 us -> 6.62 us  [spatial_call(): pl.pallas_call(spatial_kernel, out_shape=[jax.ShapeDtypeStruct((frames, s...]
    all_to_all x1, blocking collectives: 20.1 us -> 22.1 us  [over_seq(): return lax.all_to_all(blocks, 'seq', 0, 0, tiled=True).reshape(rows, model)]
  transfers between devices with their start and end apart: 21 -> 21, of which waited for: 10 -> 8; matrix products, arithmetic and copies ran while one was open for 2% -> 2% of each run, Pallas kernels for 9% -> 7%
where the time goes in v3:
time: 112 us
  starting transfers between devices  37.2 us (33%)
  waiting for transfers between devices  30.2 us (27%)
  blocking collectives  22.1 us (20%)
  Pallas kernels  17.4 us (16%)
  local copies, waits for them, and re-layouts  2.43 us (2%)
  between operations  2.17 us (2%)
    ppermute x19, starting transfers between devices, peer(): return lax.ppermute(x, 'tp', [(i, i ^ d) for i in range(4)])  23.4 us
    all_to_all x1, blocking collectives, over_seq(): return lax.all_to_all(blocks, 'seq', 0, 0, tiled=True).reshape(rows, model)  22.1 us
    ppermute x19, waiting for transfers between devices, peer(): return lax.ppermute(x, 'tp', [(i, i ^ d) for i in range(4)])  18.5 us
    all_to_all x1, starting transfers between devices, over_seq(): return lax.all_to_all(blocks, 'seq', 0, 0, tiled=True).reshape(rows, model)  12.8 us
    all_to_all x1, waiting for transfers between devices, over_seq(): return lax.all_to_all(blocks, 'seq', 0, 0, tiled=True).reshape(rows, model)  11.7 us
    pallas_call x1, Pallas kernels, spatial_call(): pl.pallas_call(spatial_kernel, out_shape=[jax.ShapeDtypeStruct((frames, s...  6.62 us
    pallas_call x3, Pallas kernels, temporal_call(): pl.pallas_call(kernel, out_shape=out_shape, in_specs=[SMEM] + [VMEM] * (c...  5.11 us
    pallas_call x1, Pallas kernels, near_out_call(): pl.pallas_call(kernel, out_shape=[jax.ShapeDtypeStruct(base.shape, F32),...  2.44 us
  transfers between devices with their start and end apart: 21, of which 8 were waited for; matrix products, arithmetic and copies ran while one was open for 2% of the time, Pallas kernels for 7%

profile of v3, /device:TPU:1, one launch (start us, length us, event | category | flops | bytes accessed | tf_op | source)
XLA Modules:
  0.0 112.1 jit_solution(2487080029814375181)
XLA Ops:
  0.6 6.6 %spatial_attention.1 = (f32[2,64,1408]{2,1,0:T(8,128)S(1)}, bf16[2,64,1408]{2,1,0:T(8,128)(2,1)S(1)}, bf16[2,2,64,1408]{3,2,1,0:T(8,128)(2,1)S(1)}) custom-call(bf16[2,256,1408]{2,1,0:T(8,128)(2,1)} %refs_0_.1, f32[1408]{0:T(1024)} %refs_1_.3, bf16[3,352,1408]{2,1,0:T(8,128)(2,1)} %bitcast.16, bf16[352,1408]{1,0:T(8,128)(2,1)} %refs_3_.2), custom_call_target="tpu_custom_call" | custom-call | tf_op jit(solution)/shard_map/spatial_attention/pallas_call | solution.py:131
  7.3 3.3 %collective-permute-start = (bf16[2,2,64,1408]{3,2,1,0:T(8,128)(2,1)S(1)}, bf16[2,2,64,1408]{3,2,1,0:T(8,128)(2,1)S(1)}, u32[]{:S(2)}, u32[]{:S(2)}) collective-permute-start(bf16[2,2,64,1408]{3,2,1,0:T(8,128)(2,1)S(1)} %get-tuple-element.15), channel_id=1, source_target_pairs={{0,1},{1,0},{2,3},{3,2},{4,5},{5,4},{6,7},{7,6},{8,9},{9,8},{10,11... | collective-permute-start | bytes 2162696 | tf_op jit(solution)/shard_map/ppermute | solution.py:349
  10.6 1.0 collective-permute-start.2
  11.6 0.8 collective-permute-done.recv
  12.6 9.7 %collective-permute-done.1.other = bf16[2,64,1408]{2,1,0:T(8,128)(2,1)S(1)} collective-permute-done((bf16[2,64,1408]{2,1,0:T(8,128)(2,1)S(1)}, bf16[2,64,1408]{2,1,0:T(8,128)(2,1)S(1)}, u32[]{:S(2)}, u32[]{:S(2)}) %collective-permute-start.1) | collective-permute-done | bytes 360480 | tf_op jit(solution)/shard_map/ppermute | solution.py:349
  22.6 0.9 reshape.21
  23.5 12.8 %all-to-all-start = ((bf16[64,2,1408]{2,1,0:T(2,128)(2,1)}), bf16[64,2,1408]{2,1,0:T(2,128)(2,1)}, u32[]{:S(2)}, u32[]{:S(2)}) async-start(bf16[64,2,1408]{2,1,0:T(2,128)(2,1)} %reshape.21), calls=%async_computation | async-start | bytes 720896 | tf_op jit(solution)/shard_map/all_to_all | solution.py:389
  36.3 1.5 %collective-permute-start.6 = (bf16[352,1408]{1,0:T(8,128)(2,1)}, bf16[352,1408]{1,0:T(8,128)(2,1)}, u32[]{:S(2)}, u32[]{:S(2)}) collective-permute-start(bf16[352,1408]{1,0:T(8,128)(2,1)} %refs_3_.3), channel_id=1, source_target_pairs={{0,1},{1,0},{2,3},{3,2},{4,5},{5,4},{6,7},{7,6},{8,9},{9,8},{10,11... | collective-permute-start | bytes 2973704 | tf_op jit(solution)/shard_map/ppermute | solution.py:349
  37.9 11.7 %all-to-all-done = bf16[64,2,1408]{2,1,0:T(2,128)(2,1)} async-done(((bf16[64,2,1408]{2,1,0:T(2,128)(2,1)}), bf16[64,2,1408]{2,1,0:T(2,128)(2,1)}, u32[]{:S(2)}, u32[]{:S(2)}) %all-to-all-start) | async-done | bytes 360480 | tf_op jit(solution)/shard_map/all_to_all | solution.py:389
  49.6 1.1 reshape.22.refs_0_
  50.7 0.5 collective-permute-start.4
  51.8 3.7 %collective-permute-start.3 = (bf16[128,1408]{1,0:T(8,128)(2,1)S(1)}, bf16[128,1408]{1,0:T(8,128)(2,1)S(1)}, u32[]{:S(2)}, u32[]{:S(2)}) collective-permute-start(bf16[128,1408]{1,0:T(8,128)(2,1)S(1)} %reshape.22.refs_0_), channel_id=1, source_target_pairs={{0,1},{1,0},{2,3},{3,2},{4,5},{5,4},{6,7},{7,6},{8,9},{9,8},{10,11... | collective-permute-start | bytes 1081352 | tf_op jit(solution)/shard_map/ppermute | solution.py:349
  55.6 1.6 %temporal_attention.3 = (bf16[128,352]{1,0:T(8,128)(2,1)S(1)}, bf16[352,1408]{1,0:T(8,128)(2,1)S(1)}, bf16[352,1408]{1,0:T(8,128)(2,1)S(1)}) custom-call(s32[1]{0:T(128)} %copy.17.valid_ref, bf16[128,1408]{1,0:T(8,128)(2,1)S(1)} %reshape.22.refs_0_, f32[1408]{0:T(1024)S(1)} %copy-done.4, bf16[3,352,1408]{2,1,0:T(8,128)(2,1)S(1)} %bitcast.11, ...), custom_call_target="tpu_custom_call" | custom-call | tf_op jit(solution)/shard_map/temporal_attention/pallas_call | solution.py:205
  57.2 4.7 %collective-permute-start.9 = (bf16[128,1408]{1,0:T(8,128)(2,1)S(1)}, bf16[128,1408]{1,0:T(8,128)(2,1)S(1)}, u32[]{:S(2)}, u32[]{:S(2)}) collective-permute-start(bf16[128,1408]{1,0:T(8,128)(2,1)S(1)} %after.1.refs_1_), channel_id=1, source_target_pairs={{0,1},{1,0},{2,3},{3,2},{4,5},{5,4},{6,7},{7,6},{8,9},{9,8},{10,11... | collective-permute-start | bytes 1081352 | tf_op jit(solution)/shard_map/ppermute | solution.py:349
  61.9 1.9 %temporal_attention.4 = (bf16[128,352]{1,0:T(8,128)(2,1)S(1)}, bf16[128,352]{1,0:T(8,128)(2,1)S(1)}) custom-call(s32[1]{0:T(128)} %copy.17.valid_ref, bf16[128,1408]{1,0:T(8,128)(2,1)S(1)} %collective-permute-done.3.refs_0_, bf16[128,1408]{1,0:T(8,128)(2,1)S(1)} %after.1.refs_1_, f32[1408]{0:T(1024)S(1)} %copy-done.4, bf16[3,352,1408]{2,1,0:T(8,128)(2,1)S(1)} %bitcast.12), custom_call_target="tpu_custom_call" | custom-call | tf_op jit(solution)/shard_map/temporal_attention/pallas_call | solution.py:205
  63.9 0.5 collective-permute-start.8
  64.4 1.6 %temporal_attention.5 = bf16[128,352]{1,0:T(8,128)(2,1)S(1)} custom-call(s32[1]{0:T(128)} %copy.17.valid_ref, bf16[128,1408]{1,0:T(8,128)(2,1)S(1)} %collective-permute-done.9.refs_0_, f32[1408]{0:T(1024)S(1)} %copy-done.4, bf16[3,352,1408]{2,1,0:T(8,128)(2,1)S(1)} %bitcast.13), custom_call_target="tpu_custom_call" | custom-call | tf_op jit(solution)/shard_map/temporal_attention/pallas_call | solution.py:205
  66.0 1.7 %collective-permute-start.10 = (bf16[128,352]{1,0:T(8,128)(2,1)S(1)}, bf16[128,352]{1,0:T(8,128)(2,1)S(1)}, u32[]{:S(2)}, u32[]{:S(2)}) collective-permute-start(bf16[128,352]{1,0:T(8,128)(2,1)S(1)} %temporal_attention.5), channel_id=1, source_target_pairs={{0,3},{1,2},{2,1},{3,0},{4,7},{5,6},{6,5},{7,4},{8,11},{9,10},{10,... | collective-permute-start | bytes 270344 | tf_op jit(solution)/shard_map/ppermute | solution.py:349
  67.8 2.4 %temporal_output_near.1 = (f32[128,1408]{1,0:T(8,128)S(1)}, bf16[352,1408]{1,0:T(8,128)(2,1)S(1)}) custom-call(bf16[128,1408]{1,0:T(8,128)(2,1)S(1)} %reshape.22.refs_0_, bf16[128,352]{1,0:T(8,128)(2,1)S(1)} %get-tuple-element.17.token_ref.refs_1_, bf16[128,352]{1,0:T(8,128)(2,1)S(1)} %collective-permute-done.5.refs_2_, ...), custom_call_target="tpu_custom_call" | custom-call | tf_op jit(solution)/shard_map/temporal_output_near/pallas_call | solution.py:229
  70.3 1.2 %collective-permute-done.10.refs_2_ = bf16[128,352]{1,0:T(8,128)(2,1)S(1)} collective-permute-done((bf16[128,352]{1,0:T(8,128)(2,1)S(1)}, bf16[128,352]{1,0:T(8,128)(2,1)S(1)}, u32[]{:S(2)}, u32[]{:S(2)}) %collective-permute-start.10) | collective-permute-done | bytes 90144 | tf_op jit(solution)/shard_map/ppermute | solution.py:349
  71.5 0.6 temporal_output_far.1
  72.2 22.1 %all_to_all.10 = bf16[64,2,1408]{2,1,0:T(2,128)(2,1)S(1)} all-to-all(bf16[64,2,1408]{2,1,0:T(2,128)(2,1)S(1)} %reshape.23), channel_id=1, replica_groups=mesh['seq'=64,'tp'=4] {'seq'}, dimensions={0} | all-to-all | bytes 720896 | tf_op jit(solution)/shard_map/all_to_all | solution.py:389
  94.5 0.5 closing_order.1
  95.1 2.8 %collective-permute-start.14 = (f32[2,1408]{1,0:T(2,128)S(1)}, f32[2,1408]{1,0:T(2,128)S(1)}, u32[]{:S(2)}, u32[]{:S(2)}) collective-permute-start(f32[2,1408]{1,0:T(2,128)S(1)} %get-tuple-element.25.s0), channel_id=1, source_target_pairs={{0,1},{1,0},{2,3},{3,2},{4,5},{5,4},{6,7},{7,6},{8,9},{9,8},{10,11... | collective-permute-start | bytes 33800 | tf_op jit(solution)/shard_map/ppermute | solution.py:349
  97.9 1.5 %collective-permute-start.15 = (f32[2,1408]{1,0:T(2,128)S(1)}, f32[2,1408]{1,0:T(2,128)S(1)}, u32[]{:S(2)}, u32[]{:S(2)}) collective-permute-start(f32[2,1408]{1,0:T(2,128)S(1)} %get-tuple-element.25.s0), channel_id=1, source_target_pairs={{0,2},{1,3},{2,0},{3,1},{4,6},{5,7},{6,4},{7,5},{8,10},{9,11},{10,... | collective-permute-start | bytes 33800 | tf_op jit(solution)/shard_map/ppermute | solution.py:349
  100.2 2.4 %collective-permute-done.15.s2 = f32[2,1408]{1,0:T(2,128)S(1)} collective-permute-done((f32[2,1408]{1,0:T(2,128)S(1)}, f32[2,1408]{1,0:T(2,128)S(1)}, u32[]{:S(2)}, u32[]{:S(2)}) %collective-permute-start.15) | collective-permute-done | bytes 11296 | tf_op jit(solution)/shard_map/ppermute | solution.py:349
  102.7 3.2 %collective-permute-done.16.s3 = f32[2,1408]{1,0:T(2,128)S(1)} collective-permute-done((f32[2,1408]{1,0:T(2,128)S(1)}, f32[2,1408]{1,0:T(2,128)S(1)}, u32[]{:S(2)}, u32[]{:S(2)}) %collective-permute-start.16) | collective-permute-done | bytes 11296 | tf_op jit(solution)/shard_map/ppermute | solution.py:349
  105.9 0.6 scoring_head.1
  107.0 1.7 %collective-permute-start.19 = (f32[2,128]{1,0:T(2,128)S(1)}, f32[2,128]{1,0:T(2,128)S(1)}, u32[]{:S(2)}, u32[]{:S(2)}) collective-permute-start(f32[2,128]{1,0:T(2,128)S(1)} %scoring_head.1), channel_id=1, source_target_pairs={{0,3},{1,2},{2,1},{3,0},{4,7},{5,6},{6,5},{7,4},{8,11},{9,10},{10,... | collective-permute-start | bytes 3080 | tf_op jit(solution)/shard_map/ppermute | solution.py:349
  109.4 0.8 collective-permute-done.19
  110.4 0.5 compare_select_fusion
  110.9 1.2 %assemble.1 = bf16[2,256,1408]{2,1,0:T(8,128)(2,1)} custom-call(bf16[2,64,1408]{2,1,0:T(8,128)(2,1)S(1)} %get-tuple-element.24.refs_0_, bf16[2,64,1408]{2,1,0:T(8,128)(2,1)S(1)} %collective-permute-done.11.refs_1_, bf16[2,64,1408]{2,1,0:T(8,128)(2,1)S(1)} %collective-permute-done.12.refs_2_.token_ref, bf16[2,64,1408]{2,1,0:T(8,128)(2,1)S(1)} %collective-permute-done.13.refs_3_), custom_call_target="tpu_custom_call" | custom-call | tf_op jit(solution)/shard_map/assemble/pallas_call | solution.py:338
  (45 shorter events, 2.5 us)
Async XLA Ops:
  7.3 48.3 %copy-start = (bf16[1408,3,352]{0,2,1:T(8,128)(2,1)S(1)}, bf16[1408,3,352]{0,2,1:T(8,128)(2,1)}, u32[]{:S(2)}) copy-start(bf16[1408,3,352]{0,2,1:T(8,128)(2,1)} %param.19) | copy-start | bytes 8921092
  7.3 48.3 %copy-start.4 = (f32[1408]{0:T(1024)S(1)}, f32[1408]{0:T(1024)}, u32[]{:S(2)}) copy-start(f32[1408]{0:T(1024)} %refs_1_.5) | copy-start | bytes 16900
  7.3 5.2 %collective-permute-start = (bf16[2,2,64,1408]{3,2,1,0:T(8,128)(2,1)S(1)}, bf16[2,2,64,1408]{3,2,1,0:T(8,128)(2,1)S(1)}, u32[]{:S(2)}, u32[]{:S(2)}) collective-permute-start(bf16[2,2,64,1408]{3,2,1,0:T(8,128)(2,1)S(1)} %get-tuple-element.15), channel_id=1, source_target_pairs={{0,1},{1,0},{2,3},{3,2},{4,5},{5,4},{6,7},{7,6},{8,9},{9,8},{10,11... | collective-permute-start | bytes 2162696 | tf_op jit(solution)/shard_map/ppermute | solution.py:349
  10.6 27.1 %collective-permute-start.2 = (bf16[352,1408]{1,0:T(8,128)(2,1)}, bf16[352,1408]{1,0:T(8,128)(2,1)}, u32[]{:S(2)}, u32[]{:S(2)}) collective-permute-start(bf16[352,1408]{1,0:T(8,128)(2,1)} %refs_3_.3), channel_id=1, source_target_pairs={{0,6},{1,7},{2,4},{3,5},{4,2},{5,3},{6,0},{7,1},{8,14},{9,15},{10,... | collective-permute-start | bytes 2973704 | tf_op jit(solution)/shard_map/ppermute | solution.py:360
  12.5 9.8 %collective-permute-start.1 = (bf16[2,64,1408]{2,1,0:T(8,128)(2,1)S(1)}, bf16[2,64,1408]{2,1,0:T(8,128)(2,1)S(1)}, u32[]{:S(2)}, u32[]{:S(2)}) collective-permute-start(bf16[2,64,1408]{2,1,0:T(8,128)(2,1)S(1)} %fusion), channel_id=1, source_target_pairs={{0,2},{1,3},{2,0},{3,1},{4,6},{5,7},{6,4},{7,5},{8,10},{9,11},{10,... | collective-permute-start | bytes 1081352 | tf_op jit(solution)/shard_map/ppermute | solution.py:349
  23.5 26.1 %all-to-all-start = ((bf16[64,2,1408]{2,1,0:T(2,128)(2,1)}), bf16[64,2,1408]{2,1,0:T(2,128)(2,1)}, u32[]{:S(2)}, u32[]{:S(2)}) async-start(bf16[64,2,1408]{2,1,0:T(2,128)(2,1)} %reshape.21), calls=%async_computation | async-start | bytes 720896 | tf_op jit(solution)/shard_map/all_to_all | solution.py:389
  36.3 31.5 %collective-permute-start.6 = (bf16[352,1408]{1,0:T(8,128)(2,1)}, bf16[352,1408]{1,0:T(8,128)(2,1)}, u32[]{:S(2)}, u32[]{:S(2)}) collective-permute-start(bf16[352,1408]{1,0:T(8,128)(2,1)} %refs_3_.3), channel_id=1, source_target_pairs={{0,1},{1,0},{2,3},{3,2},{4,5},{5,4},{6,7},{7,6},{8,9},{9,8},{10,11... | collective-permute-start | bytes 2973704 | tf_op jit(solution)/shard_map/ppermute | solution.py:349
  37.7 30.0 %collective-permute-start.7 = (bf16[352,1408]{1,0:T(8,128)(2,1)}, bf16[352,1408]{1,0:T(8,128)(2,1)}, u32[]{:S(2)}, u32[]{:S(2)}) collective-permute-start(bf16[352,1408]{1,0:T(8,128)(2,1)} %collective-permute-done.2.refs_4_), channel_id=1, source_target_pairs={{0,1},{1,0},{2,3},{3,2},{4,5},{5,4},{6,7},{7,6},{8,9},{9,8},{10,11... | collective-permute-start | bytes 2973704 | tf_op jit(solution)/shard_map/ppermute | solution.py:349
  50.7 6.5 %collective-permute-start.4 = (bf16[128,1408]{1,0:T(8,128)(2,1)S(1)}, bf16[128,1408]{1,0:T(8,128)(2,1)S(1)}, u32[]{:S(2)}, u32[]{:S(2)}) collective-permute-start(bf16[128,1408]{1,0:T(8,128)(2,1)S(1)} %reshape.22.refs_0_), channel_id=1, source_target_pairs={{0,2},{1,3},{2,0},{3,1},{4,6},{5,7},{6,4},{7,5},{8,10},{9,11},{10,... | collective-permute-start | bytes 1081352 | tf_op jit(solution)/shard_map/ppermute | solution.py:349
  51.8 10.1 %collective-permute-start.3 = (bf16[128,1408]{1,0:T(8,128)(2,1)S(1)}, bf16[128,1408]{1,0:T(8,128)(2,1)S(1)}, u32[]{:S(2)}, u32[]{:S(2)}) collective-permute-start(bf16[128,1408]{1,0:T(8,128)(2,1)S(1)} %reshape.22.refs_0_), channel_id=1, source_target_pairs={{0,1},{1,0},{2,3},{3,2},{4,5},{5,4},{6,7},{7,6},{8,9},{9,8},{10,11... | collective-permute-start | bytes 1081352 | tf_op jit(solution)/shard_map/ppermute | solution.py:349
  57.2 7.2 %collective-permute-start.9 = (bf16[128,1408]{1,0:T(8,128)(2,1)S(1)}, bf16[128,1408]{1,0:T(8,128)(2,1)S(1)}, u32[]{:S(2)}, u32[]{:S(2)}) collective-permute-start(bf16[128,1408]{1,0:T(8,128)(2,1)S(1)} %after.1.refs_1_), channel_id=1, source_target_pairs={{0,1},{1,0},{2,3},{3,2},{4,5},{5,4},{6,7},{7,6},{8,9},{9,8},{10,11... | collective-permute-start | bytes 1081352 | tf_op jit(solution)/shard_map/ppermute | solution.py:349
  63.8 3.9 %collective-permute-start.5 = (bf16[128,352]{1,0:T(8,128)(2,1)S(1)}, bf16[128,352]{1,0:T(8,128)(2,1)S(1)}, u32[]{:S(2)}, u32[]{:S(2)}) collective-permute-start(bf16[128,352]{1,0:T(8,128)(2,1)S(1)} %get-tuple-element.18), channel_id=1, source_target_pairs={{0,1},{1,0},{2,3},{3,2},{4,5},{5,4},{6,7},{7,6},{8,9},{9,8},{10,11... | collective-permute-start | bytes 270344 | tf_op jit(solution)/shard_map/ppermute | solution.py:349
  63.9 6.3 %collective-permute-start.8 = (bf16[128,352]{1,0:T(8,128)(2,1)S(1)}, bf16[128,352]{1,0:T(8,128)(2,1)S(1)}, u32[]{:S(2)}, u32[]{:S(2)}) collective-permute-start(bf16[128,352]{1,0:T(8,128)(2,1)S(1)} %get-tuple-element.21), channel_id=1, source_target_pairs={{0,2},{1,3},{2,0},{3,1},{4,6},{5,7},{6,4},{7,5},{8,10},{9,11},{10,... | collective-permute-start | bytes 270344 | tf_op jit(solution)/shard_map/ppermute | solution.py:349
  66.0 5.5 %collective-permute-start.10 = (bf16[128,352]{1,0:T(8,128)(2,1)S(1)}, bf16[128,352]{1,0:T(8,128)(2,1)S(1)}, u32[]{:S(2)}, u32[]{:S(2)}) collective-permute-start(bf16[128,352]{1,0:T(8,128)(2,1)S(1)} %temporal_attention.5), channel_id=1, source_target_pairs={{0,3},{1,2},{2,1},{3,0},{4,7},{5,6},{6,5},{7,4},{8,11},{9,10},{10,... | collective-permute-start | bytes 270344 | tf_op jit(solution)/shard_map/ppermute | solution.py:349
  70.2 24.3 %copy-start.5 = (f32[1408]{0:T(1024)S(1)}, f32[1408]{0:T(1024)}, u32[]{:S(2)}) copy-start(f32[1408]{0:T(1024)} %gain_ref.1) | copy-start | bytes 16900
  70.2 29.3 %copy-start.6 = (bf16[352]{0:T(512)(128)(2,1)S(1)}, bf16[352]{0:T(512)(128)(2,1)}, u32[]{:S(2)}) copy-start(bf16[352]{0:T(512)(128)(2,1)} %param.25) | copy-start | bytes 2116
  70.2 35.7 %copy-start.1 = (bf16[1408,352]{0,1:T(8,128)(2,1)S(1)}, bf16[1408,352]{0,1:T(8,128)(2,1)}, u32[]{:S(2)}) copy-start(bf16[1408,352]{0,1:T(8,128)(2,1)} %param.22) | copy-start | bytes 2973700
  70.2 35.7 %copy-start.2 = (bf16[8,1408,16]{1,2,0:T(8,128)(2,1)S(1)}, bf16[8,1408,16]{1,2,0:T(8,128)(2,1)}, u32[]{:S(2)}) copy-start(bf16[8,1408,16]{1,2,0:T(8,128)(2,1)} %param.23) | copy-start | bytes 1081348
  70.3 35.7 %copy-start.3 = (bf16[8,16,352]{2,1,0:T(8,128)(2,1)S(1)}, bf16[8,16,352]{2,1,0:T(8,128)(2,1)}, u32[]{:S(2)}) copy-start(bf16[8,16,352]{2,1,0:T(8,128)(2,1)} %up.1) | copy-start | bytes 270340
  95.0 10.9 %collective-permute-start.12 = (bf16[2,64,1408]{2,1,0:T(8,128)(2,1)S(1)}, bf16[2,64,1408]{2,1,0:T(8,128)(2,1)S(1)}, u32[]{:S(2)}, u32[]{:S(2)}) collective-permute-start(bf16[2,64,1408]{2,1,0:T(8,128)(2,1)S(1)} %get-tuple-element.24.refs_0_), channel_id=1, source_target_pairs={{0,2},{1,3},{2,0},{3,1},{4,6},{5,7},{6,4},{7,5},{8,10},{9,11},{10,... | collective-permute-start | bytes 1081352 | tf_op jit(solution)/shard_map/ppermute | solution.py:349
  95.1 5.1 %collective-permute-start.14 = (f32[2,1408]{1,0:T(2,128)S(1)}, f32[2,1408]{1,0:T(2,128)S(1)}, u32[]{:S(2)}, u32[]{:S(2)}) collective-permute-start(f32[2,1408]{1,0:T(2,128)S(1)} %get-tuple-element.25.s0), channel_id=1, source_target_pairs={{0,1},{1,0},{2,3},{3,2},{4,5},{5,4},{6,7},{7,6},{8,9},{9,8},{10,11... | collective-permute-start | bytes 33800 | tf_op jit(solution)/shard_map/ppermute | solution.py:349
  97.9 4.7 %collective-permute-start.15 = (f32[2,1408]{1,0:T(2,128)S(1)}, f32[2,1408]{1,0:T(2,128)S(1)}, u32[]{:S(2)}, u32[]{:S(2)}) collective-permute-start(f32[2,1408]{1,0:T(2,128)S(1)} %get-tuple-element.25.s0), channel_id=1, source_target_pairs={{0,2},{1,3},{2,0},{3,1},{4,6},{5,7},{6,4},{7,5},{8,10},{9,11},{10,... | collective-permute-start | bytes 33800 | tf_op jit(solution)/shard_map/ppermute | solution.py:349
  99.4 6.5 %collective-permute-start.16 = (f32[2,1408]{1,0:T(2,128)S(1)}, f32[2,1408]{1,0:T(2,128)S(1)}, u32[]{:S(2)}, u32[]{:S(2)}) collective-permute-start(f32[2,1408]{1,0:T(2,128)S(1)} %get-tuple-element.25.s0), channel_id=1, source_target_pairs={{0,3},{1,2},{2,1},{3,0},{4,7},{5,6},{6,5},{7,4},{8,11},{9,10},{10,... | collective-permute-start | bytes 33800 | tf_op jit(solution)/shard_map/ppermute | solution.py:349
  106.6 2.7 %collective-permute-start.17 = (f32[2,128]{1,0:T(2,128)S(1)}, f32[2,128]{1,0:T(2,128)S(1)}, u32[]{:S(2)}, u32[]{:S(2)}) collective-permute-start(f32[2,128]{1,0:T(2,128)S(1)} %scoring_head.1), channel_id=1, source_target_pairs={{0,1},{1,0},{2,3},{3,2},{4,5},{5,4},{6,7},{7,6},{8,9},{9,8},{10,11... | collective-permute-start | bytes 3080 | tf_op jit(solution)/shard_map/ppermute | solution.py:349
  107.0 2.4 %collective-permute-start.18 = (f32[2,128]{1,0:T(2,128)S(1)}, f32[2,128]{1,0:T(2,128)S(1)}, u32[]{:S(2)}, u32[]{:S(2)}) collective-permute-start(f32[2,128]{1,0:T(2,128)S(1)} %scoring_head.1), channel_id=1, source_target_pairs={{0,2},{1,3},{2,0},{3,1},{4,6},{5,7},{6,4},{7,5},{8,10},{9,11},{10,... | collective-permute-start | bytes 3080 | tf_op jit(solution)/shard_map/ppermute | solution.py:349
  107.0 3.2 %collective-permute-start.19 = (f32[2,128]{1,0:T(2,128)S(1)}, f32[2,128]{1,0:T(2,128)S(1)}, u32[]{:S(2)}, u32[]{:S(2)}) collective-permute-start(f32[2,128]{1,0:T(2,128)S(1)} %scoring_head.1), channel_id=1, source_target_pairs={{0,3},{1,2},{2,1},{3,0},{4,7},{5,6},{6,5},{7,4},{8,11},{9,10},{10,... | collective-permute-start | bytes 3080 | tf_op jit(solution)/shard_map/ppermute | solution.py:349
  108.7 2.2 %collective-permute-start.11 = (bf16[2,64,1408]{2,1,0:T(8,128)(2,1)S(1)}, bf16[2,64,1408]{2,1,0:T(8,128)(2,1)S(1)}, u32[]{:S(2)}, u32[]{:S(2)}) collective-permute-start(bf16[2,64,1408]{2,1,0:T(8,128)(2,1)S(1)} %get-tuple-element.24.refs_0_), channel_id=1, source_target_pairs={{0,1},{1,0},{2,3},{3,2},{4,5},{5,4},{6,7},{7,6},{8,9},{9,8},{10,11... | collective-permute-start | bytes 1081352 | tf_op jit(solution)/shard_map/ppermute | solution.py:349
  108.9 2.0 %collective-permute-start.13 = (bf16[2,64,1408]{2,1,0:T(8,128)(2,1)S(1)}, bf16[2,64,1408]{2,1,0:T(8,128)(2,1)S(1)}, u32[]{:S(2)}, u32[]{:S(2)}) collective-permute-start(bf16[2,64,1408]{2,1,0:T(8,128)(2,1)S(1)} %collective-permute-done.12.refs_2_.token_ref), channel_id=1, source_target_pairs={{0,1},{1,0},{2,3},{3,2},{4,5},{5,4},{6,7},{7,6},{8,9},{9,8},{10,11... | collective-permute-start | bytes 1081352 | tf_op jit(solution)/shard_map/ppermute | solution.py:349

commit v4 on v3

--- a/solution.py
+++ b/solution.py
@@ -81,15 +81,14 @@
 
 
 def spatial_kernel(*refs):
-    x_hbm, gain_hbm, w_hbm, out_w_hbm, own, far, send = refs[:7]
-    gain_ref, w_ref, out_w_ref, x_ref, mixed, sems = refs[7:]
+    x_hbm, gain_hbm, w_hbm, keep, send, base, gain_ref, w_ref, x_ref, mixed, sems = refs
     frames, patches, _ = x_ref.shape
-    share = own.shape[1]
+    share = base.shape[1]
     pairs = [(gain_hbm, gain_ref)]
     pairs += [(x_hbm.at[f], x_ref.at[f]) for f in range(frames)]
-    pairs += [(w_hbm.at[i], w_ref.at[i]) for i in range(3)] + [(out_w_hbm, out_w_ref)]
+    pairs += [(w_hbm.at[i], w_ref.at[i]) for i in range(3)]
     copies = [pltpu.make_async_copy(s, t, sems.at[i]) for i, (s, t) in enumerate(pairs)]
-    first, weights, last = copies[: 1 + frames], copies[1 + frames : 4 + frames], copies[-1]
+    first, weights = copies[: 1 + frames], copies[1 + frames :]
     for copy in [*first, weights[0]]:
         copy.start()
     first[0].wait()
@@ -100,7 +99,6 @@
             weights[1].start()
             weights[2].start()
         normed.append(normalize(x_ref[f].astype(F32), gain_ref[...]).astype(BF16))
-    last.start()
     normed = jnp.concatenate(normed, axis=0)
 
     def arrived(i):
@@ -110,44 +108,69 @@
     groups = [slice(f * patches, (f + 1) * patches) for f in range(frames)]
     for f, result in enumerate(attend_t(queries_t, keys, values_t, groups, None)):
         mixed[f] = result.astype(BF16)
-    last.wait()
     me = lax.axis_index("tp")
 
     def rows_of(d):
         return pl.ds(pl.multiple_of(jnp.bitwise_xor(me, d) * share, share), share)
 
     for f in range(frames):
-        for d, out in ((1, send.at[0]), (3, send.at[1]), (2, far), (0, own)):
-            term = dot_nn(mixed[f, rows_of(d)], out_w_ref[...])
-            if d == 0:
-                term = x_ref[f, rows_of(0)].astype(F32) + term
-            out[f] = term.astype(out.dtype)
-
-
-def spatial_call(video, gain, weight_t, out_weight):
+        keep[0, f] = mixed[f, rows_of(0)]
+        keep[1, f] = mixed[f, rows_of(2)]
+        send[0, f] = mixed[f, rows_of(1)]
+        send[1, f] = mixed[f, rows_of(3)]
+        base[f] = x_ref[f, rows_of(0)]
+
+
+def spatial_call(video, gain, weight_t):
     frames, patches, model = video.shape
-    width = out_weight.shape[0]
+    width = weight_t.shape[1]
     share = patches // 4
     return pl.pallas_call(
         spatial_kernel,
         out_shape=[
-            jax.ShapeDtypeStruct((frames, share, model), F32),
+            jax.ShapeDtypeStruct((2, frames, share, width), BF16),
+            jax.ShapeDtypeStruct((2, frames, share, width), BF16),
             jax.ShapeDtypeStruct((frames, share, model), BF16),
-            jax.ShapeDtypeStruct((2, frames, share, model), BF16),
         ],
-        in_specs=[ANY] * 4,
+        in_specs=[ANY] * 3,
         out_specs=[VMEM] * 3,
         scratch_shapes=[
             pltpu.VMEM(gain.shape, F32),
             pltpu.VMEM(weight_t.shape, BF16),
-            pltpu.VMEM(out_weight.shape, BF16),
             pltpu.VMEM(video.shape, BF16),
             pltpu.VMEM((frames, patches, width), BF16),
-            pltpu.SemaphoreType.DMA((5 + frames,)),
+            pltpu.SemaphoreType.DMA((4 + frames,)),
         ],
         compiler_params=pltpu.CompilerParams(vmem_limit_bytes=VMEM_LIMIT),
         name="spatial_attention",
-    )(*(in_hbm(x) for x in (video, gain, weight_t, out_weight)))
+    )(*(in_hbm(x) for x in (video, gain, weight_t)))
+
+
+def spatial_out_kernel(keep, recv, w_own, w_core, base, own, far):
+    frames, share, model = own.shape
+
+    def term(place):
+        rows = frames * share
+        total = dot_nn(keep[place].reshape(rows, -1), w_own[...])
+        total = total + dot_nn(recv[place].reshape(rows, -1), w_core[...])
+        return total.reshape(frames, share, model)
+
+    far[...] = term(1).astype(BF16)
+    own[...] = base[...].astype(F32) + term(0)
+
+
+def spatial_out_call(keep, recv, w_own, w_core, base):
+    return pl.pallas_call(
+        spatial_out_kernel,
+        out_shape=[
+            jax.ShapeDtypeStruct(base.shape, F32),
+            jax.ShapeDtypeStruct(base.shape, BF16),
+        ],
+        in_specs=[VMEM] * 5,
+        out_specs=[VMEM] * 2,
+        compiler_params=pltpu.CompilerParams(vmem_limit_bytes=VMEM_LIMIT),
+        name="spatial_output",
+    )(keep, recv, w_own, w_core, base)
 
 
 def one_hot_rows(rows, source):
@@ -156,24 +179,25 @@
     return jnp.where(source(i) == j, 1.0, 0.0).astype(BF16)
 
 
-def stream_kernel(own, recv, other, out):
+def stream_kernel(own, other, out):
     frames, share, model = own.shape
-    stream = own[...] + recv[0].astype(F32) + other[...].astype(F32)
+    stream = own[...] + other[...].astype(F32)
     stream = stream.astype(BF16).reshape(frames * share, model)
     order = one_hot_rows(frames * share, lambda i: (i % frames) * share + i // frames)
     out[...] = dot_nn(order, stream).astype(BF16)
 
 
-def stream_call(own, recv, other):
+def stream_call(own, other):
     frames, share, model = own.shape
     return pl.pallas_call(
         stream_kernel,
         out_shape=jax.ShapeDtypeStruct((frames * share, model), BF16),
-        in_specs=[VMEM] * 3,
+        in_specs=[VMEM] * 2,
         out_specs=VMEM,
         compiler_params=pltpu.CompilerParams(vmem_limit_bytes=VMEM_LIMIT),
+        cost_estimate=pl.CostEstimate(flops=2 * 10**9, transcendentals=0, bytes_accessed=0),
         name="stream",
-    )(own, recv, other)
+    )(own, other)
 
 
 def temporal_call(valid, quarters, gain, weight_t, sides):
@@ -388,12 +412,13 @@
         blocks = x.reshape(seq, rows // seq, model)
         return lax.all_to_all(blocks, "seq", 0, 0, tiled=True).reshape(rows, model)
 
-    own, far, send = spatial_call(
-        video, spatial_norm_gain, turned(spatial_query_key_value), spatial_output_weight
-    )
-    recv = peer(send, 1)
-    pair_term = (far.astype(F32) + recv[1].astype(F32)).astype(BF16)
-    stream = stream_call(own, recv, peer(pair_term, 2))
+    keep, send, base = spatial_call(
+        video, spatial_norm_gain, turned(spatial_query_key_value)
+    )
+    own, far = spatial_out_call(
+        keep, peer(send, 1), spatial_output_weight, peer(spatial_output_weight, 1), base
+    )
+    stream = stream_call(own, peer(far, 2))
     other_weight = across(temporal_output_weight)
     moved = over_seq(stream)
     temporal_qkv = turned(temporal_query_key_value)

time: 112 us -> 112 us (level)
    pallas_call x1 -> x2, Pallas kernels: 6.62 us -> 6.17 us  [the longest x1 5.19 us: spatial_call(): pl.pallas_call(spatial_kernel, out_shape=[jax.ShapeDtypeStruct((2, frames...]
    ppermute x19 -> x20, starting transfers between devices: 23.4 us -> 23.5 us  [peer(): return lax.ppermute(x, 'tp', [(i, i ^ d) for i in range(4)])]
    ppermute x19 -> x20, waiting for transfers between devices: 18.5 us -> 18.3 us  [peer(): return lax.ppermute(x, 'tp', [(i, i ^ d) for i in range(4)])]
  transfers between devices with their start and end apart: 21 -> 22, of which waited for: 8 -> 9; matrix products, arithmetic and copies ran while one was open for 2% -> 2% of each run, Pallas kernels for 7% -> 12%
where the time goes in v4:
time: 112 us
  starting transfers between devices  37.8 us (34%)
  waiting for transfers between devices  29.8 us (27%)
  blocking collectives  21.9 us (20%)
  Pallas kernels  16.9 us (15%)
  local copies, waits for them, and re-layouts  2.43 us (2%)
  between operations  2.16 us (2%)
    ppermute x20, starting transfers between devices, peer(): return lax.ppermute(x, 'tp', [(i, i ^ d) for i in range(4)])  23.5 us
    all_to_all x1, blocking collectives, over_seq(): return lax.all_to_all(blocks, 'seq', 0, 0, tiled=True).reshape(rows, model)  21.9 us
    ppermute x20, waiting for transfers between devices, peer(): return lax.ppermute(x, 'tp', [(i, i ^ d) for i in range(4)])  18.3 us
    all_to_all x1, starting transfers between devices, over_seq(): return lax.all_to_all(blocks, 'seq', 0, 0, tiled=True).reshape(rows, model)  12.8 us
    all_to_all x1, waiting for transfers between devices, over_seq(): return lax.all_to_all(blocks, 'seq', 0, 0, tiled=True).reshape(rows, model)  11.5 us
    pallas_call x1, Pallas kernels, spatial_call(): pl.pallas_call(spatial_kernel, out_shape=[jax.ShapeDtypeStruct((2, frames...  5.19 us
    pallas_call x3, Pallas kernels, temporal_call(): pl.pallas_call(kernel, out_shape=out_shape, in_specs=[SMEM] + [VMEM] * (c...  5.11 us
    pallas_call x1, Pallas kernels, near_out_call(): pl.pallas_call(kernel, out_shape=[jax.ShapeDtypeStruct(base.shape, F32),...  2.44 us
  transfers between devices with their start and end apart: 22, of which 9 were waited for; matrix products, arithmetic and copies ran while one was open for 2% of the time, Pallas kernels for 12%

profile of v4, /device:TPU:1, one launch (start us, length us, event | category | flops | bytes accessed | tf_op | source)
XLA Modules:
  0.0 111.5 jit_solution(9329828832389662060)
XLA Ops:
  0.6 3.3 %collective-permute-start.1 = (bf16[352,1408]{1,0:T(8,128)(2,1)}, bf16[352,1408]{1,0:T(8,128)(2,1)S(1)}, u32[]{:S(2)}, u32[]{:S(2)}) collective-permute-start(bf16[352,1408]{1,0:T(8,128)(2,1)} %w_own.1), channel_id=1, source_target_pairs={{0,1},{1,0},{2,3},{3,2},{4,5},{5,4},{6,7},{7,6},{8,9},{9,8},{10,11... | collective-permute-start | bytes 2973704 | tf_op jit(solution)/shard_map/ppermute | solution.py:373
  4.0 5.2 %spatial_attention.1 = (bf16[2,2,64,352]{3,2,1,0:T(8,128)(2,1)S(1)}, bf16[2,2,64,352]{3,2,1,0:T(8,128)(2,1)S(1)}, bf16[2,64,1408]{2,1,0:T(8,128)(2,1)S(1)}) custom-call(bf16[2,256,1408]{2,1,0:T(8,128)(2,1)} %refs_0_.1, f32[1408]{0:T(1024)} %refs_1_.3, bf16[3,352,1408]{2,1,0:T(8,128)(2,1)} %bitcast.11), custom_call_target="tpu_custom_call" | custom-call | tf_op jit(solution)/shard_map/spatial_attention/pallas_call | solution.py:128
  9.3 1.4 %collective-permute-done.recv = bf16[2,2,64,352]{3,2,1,0:T(8,128)(2,1)S(1)} collective-permute-done((bf16[2,2,64,352]{3,2,1,0:T(8,128)(2,1)S(1)}, bf16[2,2,64,352]{3,2,1,0:T(8,128)(2,1)S(1)}, u32[]{:S(2)}, u32[]{:S(2)}) %collective-permute-start) | collective-permute-done | bytes 180256 | tf_op jit(solution)/shard_map/ppermute | solution.py:373
  10.7 1.0 spatial_output.1
  11.8 1.5 %collective-permute-start.3 = (bf16[352,1408]{1,0:T(8,128)(2,1)}, bf16[352,1408]{1,0:T(8,128)(2,1)}, u32[]{:S(2)}, u32[]{:S(2)}) collective-permute-start(bf16[352,1408]{1,0:T(8,128)(2,1)} %refs_3_.1), channel_id=1, source_target_pairs={{0,6},{1,7},{2,4},{3,5},{4,2},{5,3},{6,0},{7,1},{8,14},{9,15},{10,... | collective-permute-start | bytes 2973704 | tf_op jit(solution)/shard_map/ppermute | solution.py:384
  13.2 8.5 %collective-permute-done.2.other = bf16[2,64,1408]{2,1,0:T(8,128)(2,1)S(1)} collective-permute-done((bf16[2,64,1408]{2,1,0:T(8,128)(2,1)S(1)}, bf16[2,64,1408]{2,1,0:T(8,128)(2,1)S(1)}, u32[]{:S(2)}, u32[]{:S(2)}) %collective-permute-start.2) | collective-permute-done | bytes 360480 | tf_op jit(solution)/shard_map/ppermute | solution.py:373
  22.0 0.9 reshape.19
  22.9 12.8 %all-to-all-start = ((bf16[64,2,1408]{2,1,0:T(2,128)(2,1)}), bf16[64,2,1408]{2,1,0:T(2,128)(2,1)}, u32[]{:S(2)}, u32[]{:S(2)}) async-start(bf16[64,2,1408]{2,1,0:T(2,128)(2,1)} %reshape.19), calls=%async_computation | async-start | bytes 720896 | tf_op jit(solution)/shard_map/all_to_all | solution.py:413
  35.7 1.2 %collective-permute-start.7 = (bf16[352,1408]{1,0:T(8,128)(2,1)}, bf16[352,1408]{1,0:T(8,128)(2,1)}, u32[]{:S(2)}, u32[]{:S(2)}) collective-permute-start(bf16[352,1408]{1,0:T(8,128)(2,1)} %refs_3_.1), channel_id=1, source_target_pairs={{0,1},{1,0},{2,3},{3,2},{4,5},{5,4},{6,7},{7,6},{8,9},{9,8},{10,11... | collective-permute-start | bytes 2973704 | tf_op jit(solution)/shard_map/ppermute | solution.py:373
  36.9 0.9 collective-permute-start.8
  37.7 11.5 %all-to-all-done = bf16[64,2,1408]{2,1,0:T(2,128)(2,1)} async-done(((bf16[64,2,1408]{2,1,0:T(2,128)(2,1)}), bf16[64,2,1408]{2,1,0:T(2,128)(2,1)}, u32[]{:S(2)}, u32[]{:S(2)}) %all-to-all-start) | async-done | bytes 360480 | tf_op jit(solution)/shard_map/all_to_all | solution.py:413
  49.2 1.1 %reshape.20.refs_0_ = bf16[128,1408]{1,0:T(8,128)(2,1)S(1)} reshape(bf16[64,2,1408]{2,1,0:T(2,128)(2,1)} %all-to-all-done) | data formatting | bytes 720896 | tf_op jit(solution)/shard_map/reshape | solution.py:413
  51.5 3.5 %collective-permute-start.4 = (bf16[128,1408]{1,0:T(8,128)(2,1)S(1)}, bf16[128,1408]{1,0:T(8,128)(2,1)S(1)}, u32[]{:S(2)}, u32[]{:S(2)}) collective-permute-start(bf16[128,1408]{1,0:T(8,128)(2,1)S(1)} %reshape.20.refs_0_), channel_id=1, source_target_pairs={{0,1},{1,0},{2,3},{3,2},{4,5},{5,4},{6,7},{7,6},{8,9},{9,8},{10,11... | collective-permute-start | bytes 1081352 | tf_op jit(solution)/shard_map/ppermute | solution.py:373
  55.0 1.6 %temporal_attention.3 = (bf16[128,352]{1,0:T(8,128)(2,1)S(1)}, bf16[352,1408]{1,0:T(8,128)(2,1)S(1)}, bf16[352,1408]{1,0:T(8,128)(2,1)S(1)}) custom-call(s32[1]{0:T(128)} %copy.17.valid_ref, bf16[128,1408]{1,0:T(8,128)(2,1)S(1)} %reshape.20.refs_0_, f32[1408]{0:T(1024)S(1)} %copy-done.5, bf16[3,352,1408]{2,1,0:T(8,128)(2,1)S(1)} %bitcast.6, ...), custom_call_target="tpu_custom_call" | custom-call | tf_op jit(solution)/shard_map/temporal_attention/pallas_call | solution.py:229
  56.6 0.6 collective-permute-done.5.x_ref
  57.2 4.3 %collective-permute-start.10 = (bf16[128,1408]{1,0:T(8,128)(2,1)S(1)}, bf16[128,1408]{1,0:T(8,128)(2,1)S(1)}, u32[]{:S(2)}, u32[]{:S(2)}) collective-permute-start(bf16[128,1408]{1,0:T(8,128)(2,1)S(1)} %after.1.refs_1_), channel_id=1, source_target_pairs={{0,1},{1,0},{2,3},{3,2},{4,5},{5,4},{6,7},{7,6},{8,9},{9,8},{10,11... | collective-permute-start | bytes 1081352 | tf_op jit(solution)/shard_map/ppermute | solution.py:373
  61.6 1.9 %temporal_attention.4 = (bf16[128,352]{1,0:T(8,128)(2,1)S(1)}, bf16[128,352]{1,0:T(8,128)(2,1)S(1)}) custom-call(s32[1]{0:T(128)} %copy.17.valid_ref, bf16[128,1408]{1,0:T(8,128)(2,1)S(1)} %collective-permute-done.4.refs_0_, bf16[128,1408]{1,0:T(8,128)(2,1)S(1)} %after.1.refs_1_, f32[1408]{0:T(1024)S(1)} %copy-done.5, bf16[3,352,1408]{2,1,0:T(8,128)(2,1)S(1)} %bitcast.7), custom_call_target="tpu_custom_call" | custom-call | tf_op jit(solution)/shard_map/temporal_attention/pallas_call | solution.py:229
  64.1 1.6 %temporal_attention.5 = bf16[128,352]{1,0:T(8,128)(2,1)S(1)} custom-call(s32[1]{0:T(128)} %copy.17.valid_ref, bf16[128,1408]{1,0:T(8,128)(2,1)S(1)} %collective-permute-done.10.refs_0_, f32[1408]{0:T(1024)S(1)} %copy-done.5, bf16[3,352,1408]{2,1,0:T(8,128)(2,1)S(1)} %bitcast.8), custom_call_target="tpu_custom_call" | custom-call | tf_op jit(solution)/shard_map/temporal_attention/pallas_call | solution.py:229
  65.7 1.7 %collective-permute-start.11 = (bf16[128,352]{1,0:T(8,128)(2,1)S(1)}, bf16[128,352]{1,0:T(8,128)(2,1)S(1)}, u32[]{:S(2)}, u32[]{:S(2)}) collective-permute-start(bf16[128,352]{1,0:T(8,128)(2,1)S(1)} %temporal_attention.5), channel_id=1, source_target_pairs={{0,3},{1,2},{2,1},{3,0},{4,7},{5,6},{6,5},{7,4},{8,11},{9,10},{10,... | collective-permute-start | bytes 270344 | tf_op jit(solution)/shard_map/ppermute | solution.py:373
  67.4 2.4 %temporal_output_near.1 = (f32[128,1408]{1,0:T(8,128)S(1)}, bf16[352,1408]{1,0:T(8,128)(2,1)S(1)}) custom-call(bf16[128,1408]{1,0:T(8,128)(2,1)S(1)} %reshape.20.refs_0_, bf16[128,352]{1,0:T(8,128)(2,1)S(1)} %get-tuple-element.21.token_ref.refs_1_, bf16[128,352]{1,0:T(8,128)(2,1)S(1)} %collective-permute-done.6.refs_2_, ...), custom_call_target="tpu_custom_call" | custom-call | tf_op jit(solution)/shard_map/temporal_output_near/pallas_call | solution.py:253
  70.0 1.2 %collective-permute-done.11.refs_2_ = bf16[128,352]{1,0:T(8,128)(2,1)S(1)} collective-permute-done((bf16[128,352]{1,0:T(8,128)(2,1)S(1)}, bf16[128,352]{1,0:T(8,128)(2,1)S(1)}, u32[]{:S(2)}, u32[]{:S(2)}) %collective-permute-start.11) | collective-permute-done | bytes 90144 | tf_op jit(solution)/shard_map/ppermute | solution.py:373
  71.2 0.6 temporal_output_far.1
  71.9 21.9 %all_to_all.10 = bf16[64,2,1408]{2,1,0:T(2,128)(2,1)S(1)} all-to-all(bf16[64,2,1408]{2,1,0:T(2,128)(2,1)S(1)} %reshape.21), channel_id=1, replica_groups=mesh['seq'=64,'tp'=4] {'seq'}, dimensions={0} | all-to-all | bytes 720896 | tf_op jit(solution)/shard_map/all_to_all | solution.py:413
  93.9 0.5 closing_order.1
  94.5 2.9 %collective-permute-start.15 = (f32[2,1408]{1,0:T(2,128)S(1)}, f32[2,1408]{1,0:T(2,128)S(1)}, u32[]{:S(2)}, u32[]{:S(2)}) collective-permute-start(f32[2,1408]{1,0:T(2,128)S(1)} %get-tuple-element.29.s0), channel_id=1, source_target_pairs={{0,1},{1,0},{2,3},{3,2},{4,5},{5,4},{6,7},{7,6},{8,9},{9,8},{10,11... | collective-permute-start | bytes 33800 | tf_op jit(solution)/shard_map/ppermute | solution.py:373
  97.4 1.5 %collective-permute-start.16 = (f32[2,1408]{1,0:T(2,128)S(1)}, f32[2,1408]{1,0:T(2,128)S(1)}, u32[]{:S(2)}, u32[]{:S(2)}) collective-permute-start(f32[2,1408]{1,0:T(2,128)S(1)} %get-tuple-element.29.s0), channel_id=1, source_target_pairs={{0,2},{1,3},{2,0},{3,1},{4,6},{5,7},{6,4},{7,5},{8,10},{9,11},{10,... | collective-permute-start | bytes 33800 | tf_op jit(solution)/shard_map/ppermute | solution.py:373
  99.7 2.4 %collective-permute-done.16.s2 = f32[2,1408]{1,0:T(2,128)S(1)} collective-permute-done((f32[2,1408]{1,0:T(2,128)S(1)}, f32[2,1408]{1,0:T(2,128)S(1)}, u32[]{:S(2)}, u32[]{:S(2)}) %collective-permute-start.16) | collective-permute-done | bytes 11296 | tf_op jit(solution)/shard_map/ppermute | solution.py:373
  102.0 3.3 %collective-permute-done.17.s3 = f32[2,1408]{1,0:T(2,128)S(1)} collective-permute-done((f32[2,1408]{1,0:T(2,128)S(1)}, f32[2,1408]{1,0:T(2,128)S(1)}, u32[]{:S(2)}, u32[]{:S(2)}) %collective-permute-start.17) | collective-permute-done | bytes 11296 | tf_op jit(solution)/shard_map/ppermute | solution.py:373
  105.3 0.6 scoring_head.1
  106.4 1.7 %collective-permute-start.20 = (f32[2,128]{1,0:T(2,128)S(1)}, f32[2,128]{1,0:T(2,128)S(1)}, u32[]{:S(2)}, u32[]{:S(2)}) collective-permute-start(f32[2,128]{1,0:T(2,128)S(1)} %scoring_head.1), channel_id=1, source_target_pairs={{0,3},{1,2},{2,1},{3,0},{4,7},{5,6},{6,5},{7,4},{8,11},{9,10},{10,... | collective-permute-start | bytes 3080 | tf_op jit(solution)/shard_map/ppermute | solution.py:373
  108.8 0.8 collective-permute-done.20
  110.3 1.2 %assemble.1 = bf16[2,256,1408]{2,1,0:T(8,128)(2,1)} custom-call(bf16[2,64,1408]{2,1,0:T(8,128)(2,1)S(1)} %get-tuple-element.28.refs_0_, bf16[2,64,1408]{2,1,0:T(8,128)(2,1)S(1)} %collective-permute-done.12.refs_1_, bf16[2,64,1408]{2,1,0:T(8,128)(2,1)S(1)} %collective-permute-done.13.refs_2_.token_ref, bf16[2,64,1408]{2,1,0:T(8,128)(2,1)S(1)} %collective-permute-done.14.refs_3_), custom_call_target="tpu_custom_call" | custom-call | tf_op jit(solution)/shard_map/assemble/pallas_call | solution.py:362
  (49 shorter events, 4.0 us)
Async XLA Ops:
  0.6 10.1 %copy-start.1 = (bf16[352,1408]{1,0:T(8,128)(2,1)S(1)}, bf16[352,1408]{1,0:T(8,128)(2,1)}, u32[]{:S(2)}) copy-start(bf16[352,1408]{1,0:T(8,128)(2,1)} %w_own.1) | copy-start | bytes 2973700
  0.6 10.1 %collective-permute-start.1 = (bf16[352,1408]{1,0:T(8,128)(2,1)}, bf16[352,1408]{1,0:T(8,128)(2,1)S(1)}, u32[]{:S(2)}, u32[]{:S(2)}) collective-permute-start(bf16[352,1408]{1,0:T(8,128)(2,1)} %w_own.1), channel_id=1, source_target_pairs={{0,1},{1,0},{2,3},{3,2},{4,5},{5,4},{6,7},{7,6},{8,9},{9,8},{10,11... | collective-permute-start | bytes 2973704 | tf_op jit(solution)/shard_map/ppermute | solution.py:373
  9.2 1.5 %collective-permute-start = (bf16[2,2,64,352]{3,2,1,0:T(8,128)(2,1)S(1)}, bf16[2,2,64,352]{3,2,1,0:T(8,128)(2,1)S(1)}, u32[]{:S(2)}, u32[]{:S(2)}) collective-permute-start(bf16[2,2,64,352]{3,2,1,0:T(8,128)(2,1)S(1)} %get-tuple-element.17), channel_id=1, source_target_pairs={{0,1},{1,0},{2,3},{3,2},{4,5},{5,4},{6,7},{7,6},{8,9},{9,8},{10,11... | collective-permute-start | bytes 540680 | tf_op jit(solution)/shard_map/ppermute | solution.py:373
  11.7 10.1 %collective-permute-start.2 = (bf16[2,64,1408]{2,1,0:T(8,128)(2,1)S(1)}, bf16[2,64,1408]{2,1,0:T(8,128)(2,1)S(1)}, u32[]{:S(2)}, u32[]{:S(2)}) collective-permute-start(bf16[2,64,1408]{2,1,0:T(8,128)(2,1)S(1)} %get-tuple-element.20), channel_id=1, source_target_pairs={{0,2},{1,3},{2,0},{3,1},{4,6},{5,7},{6,4},{7,5},{8,10},{9,11},{10,... | collective-permute-start | bytes 1081352 | tf_op jit(solution)/shard_map/ppermute | solution.py:373
  11.8 25.1 %collective-permute-start.3 = (bf16[352,1408]{1,0:T(8,128)(2,1)}, bf16[352,1408]{1,0:T(8,128)(2,1)}, u32[]{:S(2)}, u32[]{:S(2)}) collective-permute-start(bf16[352,1408]{1,0:T(8,128)(2,1)} %refs_3_.1), channel_id=1, source_target_pairs={{0,6},{1,7},{2,4},{3,5},{4,2},{5,3},{6,0},{7,1},{8,14},{9,15},{10,... | collective-permute-start | bytes 2973704 | tf_op jit(solution)/shard_map/ppermute | solution.py:384
  21.8 33.3 %copy-start = (bf16[1408,3,352]{0,2,1:T(8,128)(2,1)S(1)}, bf16[1408,3,352]{0,2,1:T(8,128)(2,1)}, u32[]{:S(2)}) copy-start(bf16[1408,3,352]{0,2,1:T(8,128)(2,1)} %param.19) | copy-start | bytes 8921092
  21.8 33.3 %copy-start.5 = (f32[1408]{0:T(1024)S(1)}, f32[1408]{0:T(1024)}, u32[]{:S(2)}) copy-start(f32[1408]{0:T(1024)} %refs_1_.5) | copy-start | bytes 16900
  22.9 26.4 %all-to-all-start = ((bf16[64,2,1408]{2,1,0:T(2,128)(2,1)}), bf16[64,2,1408]{2,1,0:T(2,128)(2,1)}, u32[]{:S(2)}, u32[]{:S(2)}) async-start(bf16[64,2,1408]{2,1,0:T(2,128)(2,1)} %reshape.19), calls=%async_computation | async-start | bytes 720896 | tf_op jit(solution)/shard_map/all_to_all | solution.py:413
  35.7 31.8 %collective-permute-start.7 = (bf16[352,1408]{1,0:T(8,128)(2,1)}, bf16[352,1408]{1,0:T(8,128)(2,1)}, u32[]{:S(2)}, u32[]{:S(2)}) collective-permute-start(bf16[352,1408]{1,0:T(8,128)(2,1)} %refs_3_.1), channel_id=1, source_target_pairs={{0,1},{1,0},{2,3},{3,2},{4,5},{5,4},{6,7},{7,6},{8,9},{9,8},{10,11... | collective-permute-start | bytes 2973704 | tf_op jit(solution)/shard_map/ppermute | solution.py:373
  36.9 30.5 %collective-permute-start.8 = (bf16[352,1408]{1,0:T(8,128)(2,1)}, bf16[352,1408]{1,0:T(8,128)(2,1)}, u32[]{:S(2)}, u32[]{:S(2)}) collective-permute-start(bf16[352,1408]{1,0:T(8,128)(2,1)} %collective-permute-done.3.refs_4_), channel_id=1, source_target_pairs={{0,1},{1,0},{2,3},{3,2},{4,5},{5,4},{6,7},{7,6},{8,9},{9,8},{10,11... | collective-permute-start | bytes 2973704 | tf_op jit(solution)/shard_map/ppermute | solution.py:373
  50.4 6.8 %collective-permute-start.5 = (bf16[128,1408]{1,0:T(8,128)(2,1)S(1)}, bf16[128,1408]{1,0:T(8,128)(2,1)S(1)}, u32[]{:S(2)}, u32[]{:S(2)}) collective-permute-start(bf16[128,1408]{1,0:T(8,128)(2,1)S(1)} %reshape.20.refs_0_), channel_id=1, source_target_pairs={{0,2},{1,3},{2,0},{3,1},{4,6},{5,7},{6,4},{7,5},{8,10},{9,11},{10,... | collective-permute-start | bytes 1081352 | tf_op jit(solution)/shard_map/ppermute | solution.py:373
  51.5 10.1 %collective-permute-start.4 = (bf16[128,1408]{1,0:T(8,128)(2,1)S(1)}, bf16[128,1408]{1,0:T(8,128)(2,1)S(1)}, u32[]{:S(2)}, u32[]{:S(2)}) collective-permute-start(bf16[128,1408]{1,0:T(8,128)(2,1)S(1)} %reshape.20.refs_0_), channel_id=1, source_target_pairs={{0,1},{1,0},{2,3},{3,2},{4,5},{5,4},{6,7},{7,6},{8,9},{9,8},{10,11... | collective-permute-start | bytes 1081352 | tf_op jit(solution)/shard_map/ppermute | solution.py:373
  57.2 6.8 %collective-permute-start.10 = (bf16[128,1408]{1,0:T(8,128)(2,1)S(1)}, bf16[128,1408]{1,0:T(8,128)(2,1)S(1)}, u32[]{:S(2)}, u32[]{:S(2)}) collective-permute-start(bf16[128,1408]{1,0:T(8,128)(2,1)S(1)} %after.1.refs_1_), channel_id=1, source_target_pairs={{0,1},{1,0},{2,3},{3,2},{4,5},{5,4},{6,7},{7,6},{8,9},{9,8},{10,11... | collective-permute-start | bytes 1081352 | tf_op jit(solution)/shard_map/ppermute | solution.py:373
  63.5 3.9 %collective-permute-start.6 = (bf16[128,352]{1,0:T(8,128)(2,1)S(1)}, bf16[128,352]{1,0:T(8,128)(2,1)S(1)}, u32[]{:S(2)}, u32[]{:S(2)}) collective-permute-start(bf16[128,352]{1,0:T(8,128)(2,1)S(1)} %get-tuple-element.22), channel_id=1, source_target_pairs={{0,1},{1,0},{2,3},{3,2},{4,5},{5,4},{6,7},{7,6},{8,9},{9,8},{10,11... | collective-permute-start | bytes 270344 | tf_op jit(solution)/shard_map/ppermute | solution.py:373
  63.6 6.3 %collective-permute-start.9 = (bf16[128,352]{1,0:T(8,128)(2,1)S(1)}, bf16[128,352]{1,0:T(8,128)(2,1)S(1)}, u32[]{:S(2)}, u32[]{:S(2)}) collective-permute-start(bf16[128,352]{1,0:T(8,128)(2,1)S(1)} %get-tuple-element.25), channel_id=1, source_target_pairs={{0,2},{1,3},{2,0},{3,1},{4,6},{5,7},{6,4},{7,5},{8,10},{9,11},{10,... | collective-permute-start | bytes 270344 | tf_op jit(solution)/shard_map/ppermute | solution.py:373
  65.7 5.5 %collective-permute-start.11 = (bf16[128,352]{1,0:T(8,128)(2,1)S(1)}, bf16[128,352]{1,0:T(8,128)(2,1)S(1)}, u32[]{:S(2)}, u32[]{:S(2)}) collective-permute-start(bf16[128,352]{1,0:T(8,128)(2,1)S(1)} %temporal_attention.5), channel_id=1, source_target_pairs={{0,3},{1,2},{2,1},{3,0},{4,7},{5,6},{6,5},{7,4},{8,11},{9,10},{10,... | collective-permute-start | bytes 270344 | tf_op jit(solution)/shard_map/ppermute | solution.py:373
  69.9 24.0 %copy-start.6 = (f32[1408]{0:T(1024)S(1)}, f32[1408]{0:T(1024)}, u32[]{:S(2)}) copy-start(f32[1408]{0:T(1024)} %gain_ref.1) | copy-start | bytes 16900
  69.9 29.1 %copy-start.7 = (bf16[352]{0:T(512)(128)(2,1)S(1)}, bf16[352]{0:T(512)(128)(2,1)}, u32[]{:S(2)}) copy-start(bf16[352]{0:T(512)(128)(2,1)} %param.25) | copy-start | bytes 2116
  69.9 35.4 %copy-start.2 = (bf16[1408,352]{0,1:T(8,128)(2,1)S(1)}, bf16[1408,352]{0,1:T(8,128)(2,1)}, u32[]{:S(2)}) copy-start(bf16[1408,352]{0,1:T(8,128)(2,1)} %param.22) | copy-start | bytes 2973700
  69.9 35.4 %copy-start.3 = (bf16[8,1408,16]{1,2,0:T(8,128)(2,1)S(1)}, bf16[8,1408,16]{1,2,0:T(8,128)(2,1)}, u32[]{:S(2)}) copy-start(bf16[8,1408,16]{1,2,0:T(8,128)(2,1)} %param.23) | copy-start | bytes 1081348
  69.9 35.4 %copy-start.4 = (bf16[8,16,352]{2,1,0:T(8,128)(2,1)S(1)}, bf16[8,16,352]{2,1,0:T(8,128)(2,1)}, u32[]{:S(2)}) copy-start(bf16[8,16,352]{2,1,0:T(8,128)(2,1)} %up.1) | copy-start | bytes 270340
  94.4 10.9 %collective-permute-start.13 = (bf16[2,64,1408]{2,1,0:T(8,128)(2,1)S(1)}, bf16[2,64,1408]{2,1,0:T(8,128)(2,1)S(1)}, u32[]{:S(2)}, u32[]{:S(2)}) collective-permute-start(bf16[2,64,1408]{2,1,0:T(8,128)(2,1)S(1)} %get-tuple-element.28.refs_0_), channel_id=1, source_target_pairs={{0,2},{1,3},{2,0},{3,1},{4,6},{5,7},{6,4},{7,5},{8,10},{9,11},{10,... | collective-permute-start | bytes 1081352 | tf_op jit(solution)/shard_map/ppermute | solution.py:373
  94.5 5.2 %collective-permute-start.15 = (f32[2,1408]{1,0:T(2,128)S(1)}, f32[2,1408]{1,0:T(2,128)S(1)}, u32[]{:S(2)}, u32[]{:S(2)}) collective-permute-start(f32[2,1408]{1,0:T(2,128)S(1)} %get-tuple-element.29.s0), channel_id=1, source_target_pairs={{0,1},{1,0},{2,3},{3,2},{4,5},{5,4},{6,7},{7,6},{8,9},{9,8},{10,11... | collective-permute-start | bytes 33800 | tf_op jit(solution)/shard_map/ppermute | solution.py:373
  97.4 4.7 %collective-permute-start.16 = (f32[2,1408]{1,0:T(2,128)S(1)}, f32[2,1408]{1,0:T(2,128)S(1)}, u32[]{:S(2)}, u32[]{:S(2)}) collective-permute-start(f32[2,1408]{1,0:T(2,128)S(1)} %get-tuple-element.29.s0), channel_id=1, source_target_pairs={{0,2},{1,3},{2,0},{3,1},{4,6},{5,7},{6,4},{7,5},{8,10},{9,11},{10,... | collective-permute-start | bytes 33800 | tf_op jit(solution)/shard_map/ppermute | solution.py:373
  98.8 6.4 %collective-permute-start.17 = (f32[2,1408]{1,0:T(2,128)S(1)}, f32[2,1408]{1,0:T(2,128)S(1)}, u32[]{:S(2)}, u32[]{:S(2)}) collective-permute-start(f32[2,1408]{1,0:T(2,128)S(1)} %get-tuple-element.29.s0), channel_id=1, source_target_pairs={{0,3},{1,2},{2,1},{3,0},{4,7},{5,6},{6,5},{7,4},{8,11},{9,10},{10,... | collective-permute-start | bytes 33800 | tf_op jit(solution)/shard_map/ppermute | solution.py:373
  105.9 2.7 %collective-permute-start.18 = (f32[2,128]{1,0:T(2,128)S(1)}, f32[2,128]{1,0:T(2,128)S(1)}, u32[]{:S(2)}, u32[]{:S(2)}) collective-permute-start(f32[2,128]{1,0:T(2,128)S(1)} %scoring_head.1), channel_id=1, source_target_pairs={{0,1},{1,0},{2,3},{3,2},{4,5},{5,4},{6,7},{7,6},{8,9},{9,8},{10,11... | collective-permute-start | bytes 3080 | tf_op jit(solution)/shard_map/ppermute | solution.py:373
  106.4 2.4 %collective-permute-start.19 = (f32[2,128]{1,0:T(2,128)S(1)}, f32[2,128]{1,0:T(2,128)S(1)}, u32[]{:S(2)}, u32[]{:S(2)}) collective-permute-start(f32[2,128]{1,0:T(2,128)S(1)} %scoring_head.1), channel_id=1, source_target_pairs={{0,2},{1,3},{2,0},{3,1},{4,6},{5,7},{6,4},{7,5},{8,10},{9,11},{10,... | collective-permute-start | bytes 3080 | tf_op jit(solution)/shard_map/ppermute | solution.py:373
  106.4 3.2 %collective-permute-start.20 = (f32[2,128]{1,0:T(2,128)S(1)}, f32[2,128]{1,0:T(2,128)S(1)}, u32[]{:S(2)}, u32[]{:S(2)}) collective-permute-start(f32[2,128]{1,0:T(2,128)S(1)} %scoring_head.1), channel_id=1, source_target_pairs={{0,3},{1,2},{2,1},{3,0},{4,7},{5,6},{6,5},{7,4},{8,11},{9,10},{10,... | collective-permute-start | bytes 3080 | tf_op jit(solution)/shard_map/ppermute | solution.py:373
  108.1 2.2 %collective-permute-start.12 = (bf16[2,64,1408]{2,1,0:T(8,128)(2,1)S(1)}, bf16[2,64,1408]{2,1,0:T(8,128)(2,1)S(1)}, u32[]{:S(2)}, u32[]{:S(2)}) collective-permute-start(bf16[2,64,1408]{2,1,0:T(8,128)(2,1)S(1)} %get-tuple-element.28.refs_0_), channel_id=1, source_target_pairs={{0,1},{1,0},{2,3},{3,2},{4,5},{5,4},{6,7},{7,6},{8,9},{9,8},{10,11... | collective-permute-start | bytes 1081352 | tf_op jit(solution)/shard_map/ppermute | solution.py:373
  108.2 2.0 %collective-permute-start.14 = (bf16[2,64,1408]{2,1,0:T(8,128)(2,1)S(1)}, bf16[2,64,1408]{2,1,0:T(8,128)(2,1)S(1)}, u32[]{:S(2)}, u32[]{:S(2)}) collective-permute-start(bf16[2,64,1408]{2,1,0:T(8,128)(2,1)S(1)} %collective-permute-done.13.refs_2_.token_ref), channel_id=1, source_target_pairs={{0,1},{1,0},{2,3},{3,2},{4,5},{5,4},{6,7},{7,6},{8,9},{9,8},{10,11... | collective-permute-start | bytes 1081352 | tf_op jit(solution)/shard_map/ppermute | solution.py:373

commit v5 on v4

--- a/solution.py
+++ b/solution.py
@@ -182,16 +182,15 @@
 def stream_kernel(own, other, out):
     frames, share, model = own.shape
     stream = own[...] + other[...].astype(F32)
-    stream = stream.astype(BF16).reshape(frames * share, model)
-    order = one_hot_rows(frames * share, lambda i: (i % frames) * share + i // frames)
-    out[...] = dot_nn(order, stream).astype(BF16)
+    for f in range(frames):
+        out[:, f, :] = stream[f].astype(BF16)
 
 
 def stream_call(own, other):
     frames, share, model = own.shape
     return pl.pallas_call(
         stream_kernel,
-        out_shape=jax.ShapeDtypeStruct((frames * share, model), BF16),
+        out_shape=jax.ShapeDtypeStruct((share, frames, model), BF16),
         in_specs=[VMEM] * 2,
         out_specs=VMEM,
         compiler_params=pltpu.CompilerParams(vmem_limit_bytes=VMEM_LIMIT),
@@ -408,7 +407,7 @@
         return jnp.transpose(weight, (1, 2, 0))
 
     def over_seq(x):
-        rows = x.shape[0]
+        rows = x.size // model
         blocks = x.reshape(seq, rows // seq, model)
         return lax.all_to_all(blocks, "seq", 0, 0, tiled=True).reshape(rows, model)
 

time: 112 us -> 112 us (level)
  no operation moved by 1% of the time
where the time goes in v5:
time: 112 us; the launch traced here: 111 us
  starting transfers between devices  37.9 us (34%)
  waiting for transfers between devices  29.8 us (27%)
  blocking collectives  21.8 us (19%)
  Pallas kernels  17.7 us (16%)
  between operations  2.15 us (2%)
  local copies, waits for them, and re-layouts  1.56 us (1%)
    ppermute x20, starting transfers between devices, peer(): return lax.ppermute(x, 'tp', [(i, i ^ d) for i in range(4)])  23.6 us
    all_to_all x1, blocking collectives, over_seq(): return lax.all_to_all(blocks, 'seq', 0, 0, tiled=True).reshape(rows, model)  21.8 us
    ppermute x20, waiting for transfers between devices, peer(): return lax.ppermute(x, 'tp', [(i, i ^ d) for i in range(4)])  18.3 us
    all_to_all x1, starting transfers between devices, over_seq(): return lax.all_to_all(blocks, 'seq', 0, 0, tiled=True).reshape(rows, model)  12.8 us
    all_to_all x1, waiting for transfers between devices, over_seq(): return lax.all_to_all(blocks, 'seq', 0, 0, tiled=True).reshape(rows, model)  11.4 us
    pallas_call x1, Pallas kernels, spatial_call(): pl.pallas_call(spatial_kernel, out_shape=[jax.ShapeDtypeStruct((2, frames...  5.19 us
    pallas_call x3, Pallas kernels, temporal_call(): pl.pallas_call(kernel, out_shape=out_shape, in_specs=[SMEM] + [VMEM] * (c...  5.11 us
    pallas_call x1, Pallas kernels, near_out_call(): pl.pallas_call(kernel, out_shape=[jax.ShapeDtypeStruct(base.shape, F32),...  2.44 us
  transfers between devices with their start and end apart: 22, of which 9 were waited for; matrix products, arithmetic and copies ran while one was open for 2% of the time, Pallas kernels for 12%

profile of v5, /device:TPU:1, one launch (start us, length us, event | category | flops | bytes accessed | tf_op | source)
XLA Modules:
  0.0 111.4 jit_solution(1051395265329458111)
XLA Ops:
  0.6 3.3 %collective-permute-start.1 = (bf16[352,1408]{1,0:T(8,128)(2,1)}, bf16[352,1408]{1,0:T(8,128)(2,1)S(1)}, u32[]{:S(2)}, u32[]{:S(2)}) collective-permute-start(bf16[352,1408]{1,0:T(8,128)(2,1)} %w_own.1), channel_id=1, source_target_pairs={{0,1},{1,0},{2,3},{3,2},{4,5},{5,4},{6,7},{7,6},{8,9},{9,8},{10,11... | collective-permute-start | bytes 2973704 | tf_op jit(solution)/shard_map/ppermute | solution.py:372
  4.0 5.2 %spatial_attention.1 = (bf16[2,2,64,352]{3,2,1,0:T(8,128)(2,1)S(1)}, bf16[2,2,64,352]{3,2,1,0:T(8,128)(2,1)S(1)}, bf16[2,64,1408]{2,1,0:T(8,128)(2,1)S(1)}) custom-call(bf16[2,256,1408]{2,1,0:T(8,128)(2,1)} %refs_0_.1, f32[1408]{0:T(1024)} %refs_1_.3, bf16[3,352,1408]{2,1,0:T(8,128)(2,1)} %bitcast.11), custom_call_target="tpu_custom_call" | custom-call | tf_op jit(solution)/shard_map/spatial_attention/pallas_call | solution.py:128
  9.3 1.4 %collective-permute-done.recv = bf16[2,2,64,352]{3,2,1,0:T(8,128)(2,1)S(1)} collective-permute-done((bf16[2,2,64,352]{3,2,1,0:T(8,128)(2,1)S(1)}, bf16[2,2,64,352]{3,2,1,0:T(8,128)(2,1)S(1)}, u32[]{:S(2)}, u32[]{:S(2)}) %collective-permute-start) | collective-permute-done | bytes 180256 | tf_op jit(solution)/shard_map/ppermute | solution.py:372
  10.7 1.0 spatial_output.1
  11.8 1.5 %collective-permute-start.3 = (bf16[352,1408]{1,0:T(8,128)(2,1)}, bf16[352,1408]{1,0:T(8,128)(2,1)}, u32[]{:S(2)}, u32[]{:S(2)}) collective-permute-start(bf16[352,1408]{1,0:T(8,128)(2,1)} %refs_3_.1), channel_id=1, source_target_pairs={{0,6},{1,7},{2,4},{3,5},{4,2},{5,3},{6,0},{7,1},{8,14},{9,15},{10,... | collective-permute-start | bytes 2973704 | tf_op jit(solution)/shard_map/ppermute | solution.py:383
  13.2 8.5 %collective-permute-done.2.other = bf16[2,64,1408]{2,1,0:T(8,128)(2,1)S(1)} collective-permute-done((bf16[2,64,1408]{2,1,0:T(8,128)(2,1)S(1)}, bf16[2,64,1408]{2,1,0:T(8,128)(2,1)S(1)}, u32[]{:S(2)}, u32[]{:S(2)}) %collective-permute-start.2) | collective-permute-done | bytes 360480 | tf_op jit(solution)/shard_map/ppermute | solution.py:372
  21.7 1.0 stream.1
  22.8 12.8 %all-to-all-start = ((bf16[64,2,1408]{2,1,0:T(2,128)(2,1)}), bf16[64,2,1408]{2,1,0:T(2,128)(2,1)}, u32[]{:S(2)}, u32[]{:S(2)}) async-start(bf16[64,2,1408]{2,1,0:T(2,128)(2,1)} %stream.1), calls=%async_computation | async-start | bytes 720896 | tf_op jit(solution)/shard_map/all_to_all | solution.py:412
  35.6 1.2 %collective-permute-start.7 = (bf16[352,1408]{1,0:T(8,128)(2,1)}, bf16[352,1408]{1,0:T(8,128)(2,1)}, u32[]{:S(2)}, u32[]{:S(2)}) collective-permute-start(bf16[352,1408]{1,0:T(8,128)(2,1)} %refs_3_.1), channel_id=1, source_target_pairs={{0,1},{1,0},{2,3},{3,2},{4,5},{5,4},{6,7},{7,6},{8,9},{9,8},{10,11... | collective-permute-start | bytes 2973704 | tf_op jit(solution)/shard_map/ppermute | solution.py:372
  36.8 0.9 collective-permute-start.8
  37.7 11.4 %all-to-all-done = bf16[64,2,1408]{2,1,0:T(2,128)(2,1)} async-done(((bf16[64,2,1408]{2,1,0:T(2,128)(2,1)}), bf16[64,2,1408]{2,1,0:T(2,128)(2,1)}, u32[]{:S(2)}, u32[]{:S(2)}) %all-to-all-start) | async-done | bytes 360480 | tf_op jit(solution)/shard_map/all_to_all | solution.py:412
  49.1 1.1 %reshape.16.refs_0_ = bf16[128,1408]{1,0:T(8,128)(2,1)S(1)} reshape(bf16[64,2,1408]{2,1,0:T(2,128)(2,1)} %all-to-all-done) | data formatting | bytes 720896 | tf_op jit(solution)/shard_map/reshape | solution.py:412
  51.4 3.5 %collective-permute-start.4 = (bf16[128,1408]{1,0:T(8,128)(2,1)S(1)}, bf16[128,1408]{1,0:T(8,128)(2,1)S(1)}, u32[]{:S(2)}, u32[]{:S(2)}) collective-permute-start(bf16[128,1408]{1,0:T(8,128)(2,1)S(1)} %reshape.16.refs_0_), channel_id=1, source_target_pairs={{0,1},{1,0},{2,3},{3,2},{4,5},{5,4},{6,7},{7,6},{8,9},{9,8},{10,11... | collective-permute-start | bytes 1081352 | tf_op jit(solution)/shard_map/ppermute | solution.py:372
  54.9 1.6 %temporal_attention.3 = (bf16[128,352]{1,0:T(8,128)(2,1)S(1)}, bf16[352,1408]{1,0:T(8,128)(2,1)S(1)}, bf16[352,1408]{1,0:T(8,128)(2,1)S(1)}) custom-call(s32[1]{0:T(128)} %copy.17.valid_ref, bf16[128,1408]{1,0:T(8,128)(2,1)S(1)} %reshape.16.refs_0_, f32[1408]{0:T(1024)S(1)} %copy-done.5, bf16[3,352,1408]{2,1,0:T(8,128)(2,1)S(1)} %bitcast.6, ...), custom_call_target="tpu_custom_call" | custom-call | tf_op jit(solution)/shard_map/temporal_attention/pallas_call | solution.py:228
  56.5 0.6 collective-permute-done.5.x_ref
  57.2 4.3 %collective-permute-start.10 = (bf16[128,1408]{1,0:T(8,128)(2,1)S(1)}, bf16[128,1408]{1,0:T(8,128)(2,1)S(1)}, u32[]{:S(2)}, u32[]{:S(2)}) collective-permute-start(bf16[128,1408]{1,0:T(8,128)(2,1)S(1)} %after.1.refs_1_), channel_id=1, source_target_pairs={{0,1},{1,0},{2,3},{3,2},{4,5},{5,4},{6,7},{7,6},{8,9},{9,8},{10,11... | collective-permute-start | bytes 1081352 | tf_op jit(solution)/shard_map/ppermute | solution.py:372
  61.5 1.9 %temporal_attention.4 = (bf16[128,352]{1,0:T(8,128)(2,1)S(1)}, bf16[128,352]{1,0:T(8,128)(2,1)S(1)}) custom-call(s32[1]{0:T(128)} %copy.17.valid_ref, bf16[128,1408]{1,0:T(8,128)(2,1)S(1)} %collective-permute-done.4.refs_0_, bf16[128,1408]{1,0:T(8,128)(2,1)S(1)} %after.1.refs_1_, f32[1408]{0:T(1024)S(1)} %copy-done.5, bf16[3,352,1408]{2,1,0:T(8,128)(2,1)S(1)} %bitcast.7), custom_call_target="tpu_custom_call" | custom-call | tf_op jit(solution)/shard_map/temporal_attention/pallas_call | solution.py:228
  64.0 1.6 %temporal_attention.5 = bf16[128,352]{1,0:T(8,128)(2,1)S(1)} custom-call(s32[1]{0:T(128)} %copy.17.valid_ref, bf16[128,1408]{1,0:T(8,128)(2,1)S(1)} %collective-permute-done.10.refs_0_, f32[1408]{0:T(1024)S(1)} %copy-done.5, bf16[3,352,1408]{2,1,0:T(8,128)(2,1)S(1)} %bitcast.8), custom_call_target="tpu_custom_call" | custom-call | tf_op jit(solution)/shard_map/temporal_attention/pallas_call | solution.py:228
  65.6 1.7 %collective-permute-start.11 = (bf16[128,352]{1,0:T(8,128)(2,1)S(1)}, bf16[128,352]{1,0:T(8,128)(2,1)S(1)}, u32[]{:S(2)}, u32[]{:S(2)}) collective-permute-start(bf16[128,352]{1,0:T(8,128)(2,1)S(1)} %temporal_attention.5), channel_id=1, source_target_pairs={{0,3},{1,2},{2,1},{3,0},{4,7},{5,6},{6,5},{7,4},{8,11},{9,10},{10,... | collective-permute-start | bytes 270344 | tf_op jit(solution)/shard_map/ppermute | solution.py:372
  67.3 2.4 %temporal_output_near.1 = (f32[128,1408]{1,0:T(8,128)S(1)}, bf16[352,1408]{1,0:T(8,128)(2,1)S(1)}) custom-call(bf16[128,1408]{1,0:T(8,128)(2,1)S(1)} %reshape.16.refs_0_, bf16[128,352]{1,0:T(8,128)(2,1)S(1)} %get-tuple-element.21.token_ref.refs_1_, bf16[128,352]{1,0:T(8,128)(2,1)S(1)} %collective-permute-done.6.refs_2_, ...), custom_call_target="tpu_custom_call" | custom-call | tf_op jit(solution)/shard_map/temporal_output_near/pallas_call | solution.py:252
  69.9 1.2 %collective-permute-done.11.refs_2_ = bf16[128,352]{1,0:T(8,128)(2,1)S(1)} collective-permute-done((bf16[128,352]{1,0:T(8,128)(2,1)S(1)}, bf16[128,352]{1,0:T(8,128)(2,1)S(1)}, u32[]{:S(2)}, u32[]{:S(2)}) %collective-permute-start.11) | collective-permute-done | bytes 90144 | tf_op jit(solution)/shard_map/ppermute | solution.py:372
  71.1 0.6 temporal_output_far.1
  71.8 21.8 %all_to_all.10 = bf16[64,2,1408]{2,1,0:T(2,128)(2,1)S(1)} all-to-all(bf16[64,2,1408]{2,1,0:T(2,128)(2,1)S(1)} %reshape.17), channel_id=1, replica_groups=mesh['seq'=64,'tp'=4] {'seq'}, dimensions={0} | all-to-all | bytes 720896 | tf_op jit(solution)/shard_map/all_to_all | solution.py:412
  93.8 0.5 closing_order.1
  94.4 2.9 %collective-permute-start.15 = (f32[2,1408]{1,0:T(2,128)S(1)}, f32[2,1408]{1,0:T(2,128)S(1)}, u32[]{:S(2)}, u32[]{:S(2)}) collective-permute-start(f32[2,1408]{1,0:T(2,128)S(1)} %get-tuple-element.29.s0), channel_id=1, source_target_pairs={{0,1},{1,0},{2,3},{3,2},{4,5},{5,4},{6,7},{7,6},{8,9},{9,8},{10,11... | collective-permute-start | bytes 33800 | tf_op jit(solution)/shard_map/ppermute | solution.py:372
  97.3 1.5 %collective-permute-start.16 = (f32[2,1408]{1,0:T(2,128)S(1)}, f32[2,1408]{1,0:T(2,128)S(1)}, u32[]{:S(2)}, u32[]{:S(2)}) collective-permute-start(f32[2,1408]{1,0:T(2,128)S(1)} %get-tuple-element.29.s0), channel_id=1, source_target_pairs={{0,2},{1,3},{2,0},{3,1},{4,6},{5,7},{6,4},{7,5},{8,10},{9,11},{10,... | collective-permute-start | bytes 33800 | tf_op jit(solution)/shard_map/ppermute | solution.py:372
  99.6 2.4 %collective-permute-done.16.s2 = f32[2,1408]{1,0:T(2,128)S(1)} collective-permute-done((f32[2,1408]{1,0:T(2,128)S(1)}, f32[2,1408]{1,0:T(2,128)S(1)}, u32[]{:S(2)}, u32[]{:S(2)}) %collective-permute-start.16) | collective-permute-done | bytes 11296 | tf_op jit(solution)/shard_map/ppermute | solution.py:372
  101.9 3.3 %collective-permute-done.17.s3 = f32[2,1408]{1,0:T(2,128)S(1)} collective-permute-done((f32[2,1408]{1,0:T(2,128)S(1)}, f32[2,1408]{1,0:T(2,128)S(1)}, u32[]{:S(2)}, u32[]{:S(2)}) %collective-permute-start.17) | collective-permute-done | bytes 11296 | tf_op jit(solution)/shard_map/ppermute | solution.py:372
  105.2 0.6 scoring_head.1
  106.3 1.7 %collective-permute-start.20 = (f32[2,128]{1,0:T(2,128)S(1)}, f32[2,128]{1,0:T(2,128)S(1)}, u32[]{:S(2)}, u32[]{:S(2)}) collective-permute-start(f32[2,128]{1,0:T(2,128)S(1)} %scoring_head.1), channel_id=1, source_target_pairs={{0,3},{1,2},{2,1},{3,0},{4,7},{5,6},{6,5},{7,4},{8,11},{9,10},{10,... | collective-permute-start | bytes 3080 | tf_op jit(solution)/shard_map/ppermute | solution.py:372
  108.7 0.8 collective-permute-done.20
  110.2 1.2 %assemble.1 = bf16[2,256,1408]{2,1,0:T(8,128)(2,1)} custom-call(bf16[2,64,1408]{2,1,0:T(8,128)(2,1)S(1)} %get-tuple-element.28.refs_0_, bf16[2,64,1408]{2,1,0:T(8,128)(2,1)S(1)} %collective-permute-done.12.refs_1_, bf16[2,64,1408]{2,1,0:T(8,128)(2,1)S(1)} %collective-permute-done.13.refs_2_.token_ref, bf16[2,64,1408]{2,1,0:T(8,128)(2,1)S(1)} %collective-permute-done.14.refs_3_), custom_call_target="tpu_custom_call" | custom-call | tf_op jit(solution)/shard_map/assemble/pallas_call | solution.py:361
  (48 shorter events, 3.8 us)
Async XLA Ops:
  0.6 10.1 %copy-start.1 = (bf16[352,1408]{1,0:T(8,128)(2,1)S(1)}, bf16[352,1408]{1,0:T(8,128)(2,1)}, u32[]{:S(2)}) copy-start(bf16[352,1408]{1,0:T(8,128)(2,1)} %w_own.1) | copy-start | bytes 2973700
  0.6 10.1 %collective-permute-start.1 = (bf16[352,1408]{1,0:T(8,128)(2,1)}, bf16[352,1408]{1,0:T(8,128)(2,1)S(1)}, u32[]{:S(2)}, u32[]{:S(2)}) collective-permute-start(bf16[352,1408]{1,0:T(8,128)(2,1)} %w_own.1), channel_id=1, source_target_pairs={{0,1},{1,0},{2,3},{3,2},{4,5},{5,4},{6,7},{7,6},{8,9},{9,8},{10,11... | collective-permute-start | bytes 2973704 | tf_op jit(solution)/shard_map/ppermute | solution.py:372
  9.2 1.5 %collective-permute-start = (bf16[2,2,64,352]{3,2,1,0:T(8,128)(2,1)S(1)}, bf16[2,2,64,352]{3,2,1,0:T(8,128)(2,1)S(1)}, u32[]{:S(2)}, u32[]{:S(2)}) collective-permute-start(bf16[2,2,64,352]{3,2,1,0:T(8,128)(2,1)S(1)} %get-tuple-element.17), channel_id=1, source_target_pairs={{0,1},{1,0},{2,3},{3,2},{4,5},{5,4},{6,7},{7,6},{8,9},{9,8},{10,11... | collective-permute-start | bytes 540680 | tf_op jit(solution)/shard_map/ppermute | solution.py:372
  11.7 10.1 %collective-permute-start.2 = (bf16[2,64,1408]{2,1,0:T(8,128)(2,1)S(1)}, bf16[2,64,1408]{2,1,0:T(8,128)(2,1)S(1)}, u32[]{:S(2)}, u32[]{:S(2)}) collective-permute-start(bf16[2,64,1408]{2,1,0:T(8,128)(2,1)S(1)} %get-tuple-element.20), channel_id=1, source_target_pairs={{0,2},{1,3},{2,0},{3,1},{4,6},{5,7},{6,4},{7,5},{8,10},{9,11},{10,... | collective-permute-start | bytes 1081352 | tf_op jit(solution)/shard_map/ppermute | solution.py:372
  11.8 25.0 %collective-permute-start.3 = (bf16[352,1408]{1,0:T(8,128)(2,1)}, bf16[352,1408]{1,0:T(8,128)(2,1)}, u32[]{:S(2)}, u32[]{:S(2)}) collective-permute-start(bf16[352,1408]{1,0:T(8,128)(2,1)} %refs_3_.1), channel_id=1, source_target_pairs={{0,6},{1,7},{2,4},{3,5},{4,2},{5,3},{6,0},{7,1},{8,14},{9,15},{10,... | collective-permute-start | bytes 2973704 | tf_op jit(solution)/shard_map/ppermute | solution.py:383
  21.7 33.2 %copy-start = (bf16[1408,3,352]{0,2,1:T(8,128)(2,1)S(1)}, bf16[1408,3,352]{0,2,1:T(8,128)(2,1)}, u32[]{:S(2)}) copy-start(bf16[1408,3,352]{0,2,1:T(8,128)(2,1)} %param.19) | copy-start | bytes 8921092
  21.7 33.2 %copy-start.5 = (f32[1408]{0:T(1024)S(1)}, f32[1408]{0:T(1024)}, u32[]{:S(2)}) copy-start(f32[1408]{0:T(1024)} %refs_1_.5) | copy-start | bytes 16900
  22.8 26.4 %all-to-all-start = ((bf16[64,2,1408]{2,1,0:T(2,128)(2,1)}), bf16[64,2,1408]{2,1,0:T(2,128)(2,1)}, u32[]{:S(2)}, u32[]{:S(2)}) async-start(bf16[64,2,1408]{2,1,0:T(2,128)(2,1)} %stream.1), calls=%async_computation | async-start | bytes 720896 | tf_op jit(solution)/shard_map/all_to_all | solution.py:412
  35.6 31.8 %collective-permute-start.7 = (bf16[352,1408]{1,0:T(8,128)(2,1)}, bf16[352,1408]{1,0:T(8,128)(2,1)}, u32[]{:S(2)}, u32[]{:S(2)}) collective-permute-start(bf16[352,1408]{1,0:T(8,128)(2,1)} %refs_3_.1), channel_id=1, source_target_pairs={{0,1},{1,0},{2,3},{3,2},{4,5},{5,4},{6,7},{7,6},{8,9},{9,8},{10,11... | collective-permute-start | bytes 2973704 | tf_op jit(solution)/shard_map/ppermute | solution.py:372
  36.8 30.5 %collective-permute-start.8 = (bf16[352,1408]{1,0:T(8,128)(2,1)}, bf16[352,1408]{1,0:T(8,128)(2,1)}, u32[]{:S(2)}, u32[]{:S(2)}) collective-permute-start(bf16[352,1408]{1,0:T(8,128)(2,1)} %collective-permute-done.3.refs_4_), channel_id=1, source_target_pairs={{0,1},{1,0},{2,3},{3,2},{4,5},{5,4},{6,7},{7,6},{8,9},{9,8},{10,11... | collective-permute-start | bytes 2973704 | tf_op jit(solution)/shard_map/ppermute | solution.py:372
  50.3 6.8 %collective-permute-start.5 = (bf16[128,1408]{1,0:T(8,128)(2,1)S(1)}, bf16[128,1408]{1,0:T(8,128)(2,1)S(1)}, u32[]{:S(2)}, u32[]{:S(2)}) collective-permute-start(bf16[128,1408]{1,0:T(8,128)(2,1)S(1)} %reshape.16.refs_0_), channel_id=1, source_target_pairs={{0,2},{1,3},{2,0},{3,1},{4,6},{5,7},{6,4},{7,5},{8,10},{9,11},{10,... | collective-permute-start | bytes 1081352 | tf_op jit(solution)/shard_map/ppermute | solution.py:372
  51.4 10.1 %collective-permute-start.4 = (bf16[128,1408]{1,0:T(8,128)(2,1)S(1)}, bf16[128,1408]{1,0:T(8,128)(2,1)S(1)}, u32[]{:S(2)}, u32[]{:S(2)}) collective-permute-start(bf16[128,1408]{1,0:T(8,128)(2,1)S(1)} %reshape.16.refs_0_), channel_id=1, source_target_pairs={{0,1},{1,0},{2,3},{3,2},{4,5},{5,4},{6,7},{7,6},{8,9},{9,8},{10,11... | collective-permute-start | bytes 1081352 | tf_op jit(solution)/shard_map/ppermute | solution.py:372
  57.2 6.9 %collective-permute-start.10 = (bf16[128,1408]{1,0:T(8,128)(2,1)S(1)}, bf16[128,1408]{1,0:T(8,128)(2,1)S(1)}, u32[]{:S(2)}, u32[]{:S(2)}) collective-permute-start(bf16[128,1408]{1,0:T(8,128)(2,1)S(1)} %after.1.refs_1_), channel_id=1, source_target_pairs={{0,1},{1,0},{2,3},{3,2},{4,5},{5,4},{6,7},{7,6},{8,9},{9,8},{10,11... | collective-permute-start | bytes 1081352 | tf_op jit(solution)/shard_map/ppermute | solution.py:372
  63.4 3.9 %collective-permute-start.6 = (bf16[128,352]{1,0:T(8,128)(2,1)S(1)}, bf16[128,352]{1,0:T(8,128)(2,1)S(1)}, u32[]{:S(2)}, u32[]{:S(2)}) collective-permute-start(bf16[128,352]{1,0:T(8,128)(2,1)S(1)} %get-tuple-element.22), channel_id=1, source_target_pairs={{0,1},{1,0},{2,3},{3,2},{4,5},{5,4},{6,7},{7,6},{8,9},{9,8},{10,11... | collective-permute-start | bytes 270344 | tf_op jit(solution)/shard_map/ppermute | solution.py:372
  63.5 6.3 %collective-permute-start.9 = (bf16[128,352]{1,0:T(8,128)(2,1)S(1)}, bf16[128,352]{1,0:T(8,128)(2,1)S(1)}, u32[]{:S(2)}, u32[]{:S(2)}) collective-permute-start(bf16[128,352]{1,0:T(8,128)(2,1)S(1)} %get-tuple-element.25), channel_id=1, source_target_pairs={{0,2},{1,3},{2,0},{3,1},{4,6},{5,7},{6,4},{7,5},{8,10},{9,11},{10,... | collective-permute-start | bytes 270344 | tf_op jit(solution)/shard_map/ppermute | solution.py:372
  65.6 5.5 %collective-permute-start.11 = (bf16[128,352]{1,0:T(8,128)(2,1)S(1)}, bf16[128,352]{1,0:T(8,128)(2,1)S(1)}, u32[]{:S(2)}, u32[]{:S(2)}) collective-permute-start(bf16[128,352]{1,0:T(8,128)(2,1)S(1)} %temporal_attention.5), channel_id=1, source_target_pairs={{0,3},{1,2},{2,1},{3,0},{4,7},{5,6},{6,5},{7,4},{8,11},{9,10},{10,... | collective-permute-start | bytes 270344 | tf_op jit(solution)/shard_map/ppermute | solution.py:372
  69.8 24.0 %copy-start.6 = (f32[1408]{0:T(1024)S(1)}, f32[1408]{0:T(1024)}, u32[]{:S(2)}) copy-start(f32[1408]{0:T(1024)} %gain_ref.1) | copy-start | bytes 16900
  69.8 29.1 %copy-start.7 = (bf16[352]{0:T(512)(128)(2,1)S(1)}, bf16[352]{0:T(512)(128)(2,1)}, u32[]{:S(2)}) copy-start(bf16[352]{0:T(512)(128)(2,1)} %param.25) | copy-start | bytes 2116
  69.8 35.4 %copy-start.2 = (bf16[1408,352]{0,1:T(8,128)(2,1)S(1)}, bf16[1408,352]{0,1:T(8,128)(2,1)}, u32[]{:S(2)}) copy-start(bf16[1408,352]{0,1:T(8,128)(2,1)} %param.22) | copy-start | bytes 2973700
  69.8 35.4 %copy-start.3 = (bf16[8,1408,16]{1,2,0:T(8,128)(2,1)S(1)}, bf16[8,1408,16]{1,2,0:T(8,128)(2,1)}, u32[]{:S(2)}) copy-start(bf16[8,1408,16]{1,2,0:T(8,128)(2,1)} %param.23) | copy-start | bytes 1081348
  69.8 35.4 %copy-start.4 = (bf16[8,16,352]{2,1,0:T(8,128)(2,1)S(1)}, bf16[8,16,352]{2,1,0:T(8,128)(2,1)}, u32[]{:S(2)}) copy-start(bf16[8,16,352]{2,1,0:T(8,128)(2,1)} %up.1) | copy-start | bytes 270340
  94.3 10.9 %collective-permute-start.13 = (bf16[2,64,1408]{2,1,0:T(8,128)(2,1)S(1)}, bf16[2,64,1408]{2,1,0:T(8,128)(2,1)S(1)}, u32[]{:S(2)}, u32[]{:S(2)}) collective-permute-start(bf16[2,64,1408]{2,1,0:T(8,128)(2,1)S(1)} %get-tuple-element.28.refs_0_), channel_id=1, source_target_pairs={{0,2},{1,3},{2,0},{3,1},{4,6},{5,7},{6,4},{7,5},{8,10},{9,11},{10,... | collective-permute-start | bytes 1081352 | tf_op jit(solution)/shard_map/ppermute | solution.py:372
  94.4 5.2 %collective-permute-start.15 = (f32[2,1408]{1,0:T(2,128)S(1)}, f32[2,1408]{1,0:T(2,128)S(1)}, u32[]{:S(2)}, u32[]{:S(2)}) collective-permute-start(f32[2,1408]{1,0:T(2,128)S(1)} %get-tuple-element.29.s0), channel_id=1, source_target_pairs={{0,1},{1,0},{2,3},{3,2},{4,5},{5,4},{6,7},{7,6},{8,9},{9,8},{10,11... | collective-permute-start | bytes 33800 | tf_op jit(solution)/shard_map/ppermute | solution.py:372
  97.3 4.7 %collective-permute-start.16 = (f32[2,1408]{1,0:T(2,128)S(1)}, f32[2,1408]{1,0:T(2,128)S(1)}, u32[]{:S(2)}, u32[]{:S(2)}) collective-permute-start(f32[2,1408]{1,0:T(2,128)S(1)} %get-tuple-element.29.s0), channel_id=1, source_target_pairs={{0,2},{1,3},{2,0},{3,1},{4,6},{5,7},{6,4},{7,5},{8,10},{9,11},{10,... | collective-permute-start | bytes 33800 | tf_op jit(solution)/shard_map/ppermute | solution.py:372
  98.7 6.4 %collective-permute-start.17 = (f32[2,1408]{1,0:T(2,128)S(1)}, f32[2,1408]{1,0:T(2,128)S(1)}, u32[]{:S(2)}, u32[]{:S(2)}) collective-permute-start(f32[2,1408]{1,0:T(2,128)S(1)} %get-tuple-element.29.s0), channel_id=1, source_target_pairs={{0,3},{1,2},{2,1},{3,0},{4,7},{5,6},{6,5},{7,4},{8,11},{9,10},{10,... | collective-permute-start | bytes 33800 | tf_op jit(solution)/shard_map/ppermute | solution.py:372
  105.8 2.7 %collective-permute-start.18 = (f32[2,128]{1,0:T(2,128)S(1)}, f32[2,128]{1,0:T(2,128)S(1)}, u32[]{:S(2)}, u32[]{:S(2)}) collective-permute-start(f32[2,128]{1,0:T(2,128)S(1)} %scoring_head.1), channel_id=1, source_target_pairs={{0,1},{1,0},{2,3},{3,2},{4,5},{5,4},{6,7},{7,6},{8,9},{9,8},{10,11... | collective-permute-start | bytes 3080 | tf_op jit(solution)/shard_map/ppermute | solution.py:372
  106.3 2.4 %collective-permute-start.19 = (f32[2,128]{1,0:T(2,128)S(1)}, f32[2,128]{1,0:T(2,128)S(1)}, u32[]{:S(2)}, u32[]{:S(2)}) collective-permute-start(f32[2,128]{1,0:T(2,128)S(1)} %scoring_head.1), channel_id=1, source_target_pairs={{0,2},{1,3},{2,0},{3,1},{4,6},{5,7},{6,4},{7,5},{8,10},{9,11},{10,... | collective-permute-start | bytes 3080 | tf_op jit(solution)/shard_map/ppermute | solution.py:372
  106.3 3.2 %collective-permute-start.20 = (f32[2,128]{1,0:T(2,128)S(1)}, f32[2,128]{1,0:T(2,128)S(1)}, u32[]{:S(2)}, u32[]{:S(2)}) collective-permute-start(f32[2,128]{1,0:T(2,128)S(1)} %scoring_head.1), channel_id=1, source_target_pairs={{0,3},{1,2},{2,1},{3,0},{4,7},{5,6},{6,5},{7,4},{8,11},{9,10},{10,... | collective-permute-start | bytes 3080 | tf_op jit(solution)/shard_map/ppermute | solution.py:372
  108.0 2.2 %collective-permute-start.12 = (bf16[2,64,1408]{2,1,0:T(8,128)(2,1)S(1)}, bf16[2,64,1408]{2,1,0:T(8,128)(2,1)S(1)}, u32[]{:S(2)}, u32[]{:S(2)}) collective-permute-start(bf16[2,64,1408]{2,1,0:T(8,128)(2,1)S(1)} %get-tuple-element.28.refs_0_), channel_id=1, source_target_pairs={{0,1},{1,0},{2,3},{3,2},{4,5},{5,4},{6,7},{7,6},{8,9},{9,8},{10,11... | collective-permute-start | bytes 1081352 | tf_op jit(solution)/shard_map/ppermute | solution.py:372
  108.2 2.0 %collective-permute-start.14 = (bf16[2,64,1408]{2,1,0:T(8,128)(2,1)S(1)}, bf16[2,64,1408]{2,1,0:T(8,128)(2,1)S(1)}, u32[]{:S(2)}, u32[]{:S(2)}) collective-permute-start(bf16[2,64,1408]{2,1,0:T(8,128)(2,1)S(1)} %collective-permute-done.13.refs_2_.token_ref), channel_id=1, source_target_pairs={{0,1},{1,0},{2,3},{3,2},{4,5},{5,4},{6,7},{7,6},{8,9},{9,8},{10,11... | collective-permute-start | bytes 1081352 | tf_op jit(solution)/shard_map/ppermute | solution.py:372
